TPU v7x, 256 devices: a whole 4x4x8 slice. The times are simulated.
256 devices in a mesh: vocab: 4 (over y), hidden: 64 (over x, z, core).
Axes of the slice: x: 4, y: 4, z: 8, core: 2. Of those that a mesh axis runs over, the one named last changes fastest.
Arguments:
- gradient: bfloat16 [1024, 14336], P('vocab', 'hidden'), may hold values from -6 to 6
- moment_first: float32 [4096, 14336], P('vocab', 'hidden'), may hold values from -6 to 6
- moment_second: float32 [4096, 14336], P('vocab', 'hidden'), may hold values from 0.05 to 2
- basis: bfloat16 [14336, 14336], P('hidden'), may hold values from -0.125 to 0.125
- block_ids: int32 [4, 2], replicated, may hold values from -1 to 7, as said below
Outputs:
- update: float32 [1024, 14336], P('vocab', 'hidden')
- new_first: float32 [4096, 14336], P('vocab', 'hidden')
- new_second: float32 [4096, 14336], P('vocab', 'hidden')
Inputs may be any that keep to these rules, and one draw needn't show every extreme that they name: `block_ids`: live slots in all number 4; one or two owners have 2 live slots, the same number of owners have none, and every other owner has one; an owner's live slots are its first ones, and its live entries are distinct resident blocks of that owner.
All inputs are finite; a program needn't handle non-finite values.
Results may differ from a plain program's by a relative error of at most 0.0029.
Values may be sent and summed in bfloat16 or wider, within the bound.
No kernel may reach another device: no remote copies, remote signals or barrier semaphores. Data moves between devices by JAX's collectives and lax.ppermute only.
A program may use at most 64 MiB of HBM per device.

v0:
```python
import jax
import jax.numpy as jnp
from jax import lax
from jax.sharding import PartitionSpec as P

BLK = 128


beta_first = 0.9
beta_second = 0.95
epsilon = 1e-08


def rotate(row_block, basis):
    summed = lax.psum_scatter(
        lax.dot_general(
            basis, row_block, (((0,), (1,)), ((), ())), preferred_element_type=jnp.float32
        ),
        "hidden",
        scatter_dimension=0,
        tiled=True,
    )
    return summed.T


def rotate_back(direction, basis):
    return lax.dot_general(
        lax.all_gather(direction, "hidden", axis=1, tiled=True),
        basis,
        (((1,), (1,)), ((), ())),
        preferred_element_type=jnp.float32,
    )


def adam_moments(rotated, old_first, old_second):
    first = beta_first * old_first + (1.0 - beta_first) * rotated
    second = beta_second * old_second + (1.0 - beta_second) * rotated * rotated
    direction = (first / (jnp.sqrt(second) + epsilon)).astype(jnp.bfloat16)
    return (first, second, direction)


def shards(gradient, moment_first, moment_second, basis, block_ids):
    slab_width = gradient.shape[1]
    capacity = block_ids.shape[1]
    table_blocks = moment_first.shape[0] // BLK
    worker = lax.axis_index("vocab")
    own_ids = lax.dynamic_index_in_dim(block_ids, worker, 0, keepdims=False)
    write_blocks = jnp.where(own_ids >= 0, own_ids, table_blocks)
    read_blocks = jnp.minimum(write_blocks, table_blocks - 1)
    first_table = moment_first.reshape(table_blocks, BLK, slab_width)
    second_table = moment_second.reshape(table_blocks, BLK, slab_width)
    old_first = first_table[read_blocks]
    old_second = second_table[read_blocks]
    active = (own_ids >= 0)[:, None, None]
    rotated = rotate(gradient, basis).reshape(capacity, BLK, slab_width)
    first, second, direction = adam_moments(rotated, old_first, old_second)
    direction = jnp.where(active, direction, jnp.zeros_like(direction))
    update = rotate_back(direction.reshape(capacity * BLK, slab_width), basis)
    update = update.reshape(capacity, BLK, slab_width)
    new_first = (
        first_table.at[write_blocks].set(first, mode="drop").reshape(table_blocks * BLK, slab_width)
    )
    new_second = (
        second_table.at[write_blocks]
        .set(second, mode="drop")
        .reshape(table_blocks * BLK, slab_width)
    )
    return (update.reshape(capacity * BLK, slab_width), new_first, new_second)


def solution(mesh):
    placed = (
        P("vocab", "hidden"),
        P("vocab", "hidden"),
        P("vocab", "hidden"),
        P("hidden", None),
        P(),
    )
    return jax.shard_map(
        shards,
        mesh=mesh,
        in_specs=placed,
        out_specs=(P("vocab", "hidden"), P("vocab", "hidden"), P("vocab", "hidden")),
        check_vma=False,
    )
```

profile of v0, /device:TPU:1, one launch (start us, length us, event | category | flops | bytes accessed | tf_op | source)
XLA Modules:
  0.0 285.3 jit_solution(18356243462042357964)
XLA Ops:
  7.2 0.0 copy-start
  7.2 0.0 reduce-scatter.2.cloned.1.call-start
  7.2 10.3 %fusion.9 = f32[14336,256]{1,0:T(8,128)} fusion(bf16[224,14336]{1,0:T(8,128)(2,1)} %param.8, bf16[256,224]{0,1:T(8,128)(2,1)} %param.5), kind=kOutput, calls=%fused_computation.32 | convolution fusion | flops 1644167168 | bytes 21217280 | tf_op jit(solution)/shard_map/dot_general | solution.py:16
  17.5 0.0 copy-start.1
  17.5 0.0 reduce-scatter.2.cloned.1.call-update
  17.5 0.0 all-gather.2.cloned.1.call-start
  17.6 0.6 copy-done.1
  18.2 0.2 dynamic-slice_reduce_fusion
  18.4 0.0 copy-done
  18.4 0.1 copy_bitcast_fusion.3
  18.5 0.6 gather_fusion
  19.0 1.2 copy_bitcast_fusion.2
  20.3 0.6 gather_fusion.1
  20.9 0.2 compare_reduce_fusion
  21.0 0.1 broadcast_bitcast_fusion
  21.1 162.0 %reduce-scatter.2.cloned.1.call-done = f32[224,256]{1,0:T(8,128)} async-done(((f32[14336,256]{1,0:T(8,128)}), f32[224,256]{1,0:T(8,128)}) %reduce-scatter.2.cloned.1.call-update) | async-done | bytes 229392 | tf_op jit(solution)/shard_map/reduce_scatter | solution.py:15
  183.1 1.7 fusion.4
  184.8 1.7 broadcast_select_fusion
  186.5 0.0 all-gather.2.cloned.1.call-update
  186.6 1.5 scatter_fusion
  188.1 0.6 scatter_fusion.1
  188.7 1.5 copy_bitcast_fusion
  190.2 80.8 %all-gather.2.cloned.1.call-done = bf16[256,14336]{0,1:T(8,128)(2,1)} async-done(((bf16[256,224]{0,1:T(8,128)(2,1)}), bf16[256,14336]{0,1:T(8,128)(2,1)}) %all-gather.2.cloned.1.call-update) | async-done | bytes 7340048 | tf_op jit(solution)/shard_map/all_gather | solution.py:28
  271.0 7.4 %fusion.10 = f32[256,224]{0,1:T(8,128)} fusion(bf16[224,14336]{1,0:T(8,128)(2,1)} %param.8, bf16[256,14336]{0,1:T(8,128)(2,1)} %all-gather.2.cloned.1.call-done), kind=kOutput, calls=%fused_computation.33 | convolution fusion | flops 1644167168 | bytes 13991936 | tf_op jit(solution)/shard_map/dot_general | solution.py:27
  (2 shorter events, 0.0 us)
Async XLA Ops:
  7.2 11.2 %copy-start = (f32[1024,224]{0,1:T(8,128)S(1)}, f32[1024,224]{0,1:T(8,128)}, u32[]{:S(2)}) copy-start(f32[1024,224]{0,1:T(8,128)} %param.6) | copy-start | bytes 2752516
  7.2 175.9 %reduce-scatter.2.cloned.1.call-start = ((), (), s32[]{:S(2)}) async-start(), calls=%async_computation.1 | async-start | bytes 14909440 | tf_op jit(solution)/shard_map/reduce_scatter | solution.py:15
  17.5 0.7 copy-start.1
  17.5 253.4 %all-gather.2.cloned.1.call-start = ((), (), s32[]{:S(2)}) async-start(), calls=%async_computation.2 | async-start | bytes 7454720 | tf_op jit(solution)/shard_map/all_gather | solution.py:28
Sparse Core Ops, SparseCore 0:
  17.6 165.4 reduce-scatter.1
  186.7 84.2 all-gather.1
where the time goes:
time: 285 us
  waiting for transfers between devices  243 us (85%)
  matrix products  17.7 us (6%)
  between operations  14.1 us (5%)
  local copies, waits for them, and re-layouts  6.94 us (2%)
  other arithmetic  3.62 us (1%)
    reduce_scatter x1, waiting for transfers between devices, rotate(): lax.psum_scatter(lax.dot_general(basis, row_block, (((0,), (1,)), ((), ()...  162 us
    all_gather x1, waiting for transfers between devices, rotate_back(): lax.all_gather(direction, 'hidden', axis=1, tiled=True)  80.8 us
    dot_general x1, matrix products, rotate(): lax.dot_general(basis, row_block, (((0,), (1,)), ((), ())), preferred_ele...  10.3 us
    dot_general x1, matrix products, rotate_back(): lax.dot_general(lax.all_gather(direction, 'hidden', axis=1, tiled=True),...  7.44 us
  transfers between devices with their start and end apart: 2, of which 2 were waited for; matrix products, arithmetic and copies ran while one was open for 2% of the time, Pallas kernels for 0%

commit v1 on v0

v1 whole, which is shorter than its diff:
```python
import functools

import jax
import jax.numpy as jnp
from jax import lax
from jax.experimental import pallas as pl
from jax.experimental.pallas import tpu as pltpu
from jax.sharding import Mesh
from jax.sharding import PartitionSpec as P

BLK = 128
OWNERS = 4
XS, ZH, ZL, CORES = 4, 4, 2, 2
SCALE = 4.0

beta_first = 0.9
beta_second = 0.95
epsilon = 1e-08

f32, bf16, f16 = jnp.float32, jnp.bfloat16, jnp.float16


def rotate_kernel(core_ref, basis_ref, rows_ref, keep_ref, send_ref):
    width = rows_ref.shape[1]
    part = lax.dot_general(
        basis_ref[...], rows_ref[...], (((0,), (1,)), ((), ())), preferred_element_type=f32
    )
    part = part.reshape(ZL, CORES, width, BLK) * SCALE
    mine = core_ref[0] == 0
    keep_ref[0, :, 0] = jnp.where(mine, part[:, 0], part[:, 1])
    send_ref[0, :, 0] = jnp.where(mine, part[:, 1], part[:, 0])


def rotate_partials(core, basis, rows):
    width = rows.shape[1]
    cols = ZL * CORES * width
    shape = (XS, ZL, ZH, width, BLK)
    out = pl.BlockSpec((1, ZL, 1, width, BLK), lambda i: (i // ZH, 0, i % ZH, 0, 0))
    return pl.pallas_call(
        rotate_kernel,
        grid=(XS * ZH,),
        in_specs=[
            pl.BlockSpec(memory_space=pltpu.SMEM),
            pl.BlockSpec((width, cols), lambda i: (0, i)),
            pl.BlockSpec((BLK, width), lambda i: (0, 0)),
        ],
        out_specs=[out, out],
        out_shape=[jax.ShapeDtypeStruct(shape, f32)] * 2,
    )(core, basis, rows)


def back_kernel(core_ref, basis_ref, own_ref, other_ref, out_ref):
    width = basis_ref.shape[0]
    own = own_ref[0, :, 0]
    other = other_ref[0, :, 0]
    mine = core_ref[0] == 0
    even = jnp.where(mine, own, other)
    odd = jnp.where(mine, other, own)
    cols = jnp.stack([even, odd], axis=1).reshape(ZL * CORES * width, BLK)
    part = jnp.dot(basis_ref[...], cols, preferred_element_type=f32)

    @pl.when(pl.program_id(0) == 0)
    def _():
        out_ref[...] = part

    @pl.when(pl.program_id(0) > 0)
    def _():
        out_ref[...] += part


def rotate_back(core, basis, own, other):
    width = own.shape[3]
    cols = ZL * CORES * width
    block = pl.BlockSpec((1, ZL, 1, width, BLK), lambda i: (i // ZH, 0, i % ZH, 0, 0))
    return pl.pallas_call(
        back_kernel,
        grid=(XS * ZH,),
        in_specs=[
            pl.BlockSpec(memory_space=pltpu.SMEM),
            pl.BlockSpec((width, cols), lambda i: (0, i)),
            block,
            block,
        ],
        out_specs=pl.BlockSpec((width, BLK), lambda i: (0, 0)),
        out_shape=jax.ShapeDtypeStruct((width, BLK), f32),
    )(core, basis, own, other)


def adam_moments(rotated, old_first, old_second):
    first = beta_first * old_first + (1.0 - beta_first) * rotated
    second = beta_second * old_second + (1.0 - beta_second) * rotated * rotated
    direction = (first / (jnp.sqrt(second) + epsilon)).astype(bf16)
    return (first, second, direction)


def from_owner(x, distance):
    got = [
        lax.ppermute(x, "y", [(i, (i + k) % OWNERS) for i in range(OWNERS)])
        for k in range(1, OWNERS)
    ]
    out = got[0]
    for k in range(2, OWNERS):
        out = jnp.where(distance == k, got[k - 1], out)
    return out


def all_to_all(x, axes):
    return lax.all_to_all(x, axes, 0, 0, tiled=True)


def swap_cores(x):
    return lax.ppermute(x, "c", [(0, 1), (1, 0)])


def shards(gradient, moment_first, moment_second, basis, block_ids):
    width = gradient.shape[1]
    table_blocks = moment_first.shape[0] // BLK
    me = lax.axis_index("y")
    core = lax.axis_index("c").astype(jnp.int32).reshape(1)

    counts = jnp.sum((block_ids >= 0).astype(jnp.int32), axis=1)
    full, empty = counts == 2, counts == 0
    full_rank = jnp.cumsum(full.astype(jnp.int32))
    empty_rank = jnp.cumsum(empty.astype(jnp.int32))
    owners = jnp.arange(OWNERS, dtype=jnp.int32)
    count = counts[me]
    source = jnp.sum(jnp.where(full & (full_rank == empty_rank[me]), owners, 0))
    helper = jnp.sum(jnp.where(empty & (empty_rank == full_rank[me]), owners, 0))
    back_to_source = (me - source) % OWNERS
    back_to_helper = (me - helper) % OWNERS
    helping = count == 0
    doubled = count == 2

    ids = jnp.clip(block_ids[me], 0, table_blocks - 1)
    first_table = moment_first.reshape(table_blocks, BLK, width)
    second_table = moment_second.reshape(table_blocks, BLK, width)
    old_first = first_table[ids]
    old_second = second_table[ids]

    rows = jnp.where(helping, from_owner(gradient[BLK:], back_to_source), gradient[:BLK])
    lent_first = from_owner(old_first[1], back_to_source)
    lent_second = from_owner(old_second[1], back_to_source)
    work_first = jnp.where(helping, lent_first, old_first[0])
    work_second = jnp.where(helping, lent_second, old_second[0])

    keep, send = rotate_partials(core, basis, rows)
    part = (keep + swap_cores(send.astype(f16)).astype(f32)).astype(f16)
    part = all_to_all(part.reshape(XS * ZL, ZH * width, BLK), ("x", "zl"))
    part = jnp.sum(part.astype(f32), axis=0).astype(f16)
    part = all_to_all(part.reshape(ZH, width, BLK), "zh")
    rotated = (jnp.sum(part.astype(f32), axis=0) * (1.0 / SCALE)).T

    first, second, direction = adam_moments(rotated, work_first, work_second)
    gathered = jnp.broadcast_to(direction.T[None], (ZH, width, BLK))
    gathered = all_to_all(gathered, "zh")
    gathered = jnp.broadcast_to(gathered[None], (XS * ZL, ZH, width, BLK))
    gathered = all_to_all(gathered, ("x", "zl")).reshape(XS, ZL, ZH, width, BLK)

    other_rotated = from_owner(rotated, back_to_helper)
    first_1, second_1, _ = adam_moments(other_rotated, old_first[1], old_second[1])
    block = jnp.arange(table_blocks)
    zero_at = jnp.where(count >= 1, ids[0], -1)
    one_at = jnp.where(doubled, ids[1], -1)

    def written(table, zero, one):
        out = jnp.where((block == zero_at)[:, None, None], zero[None], table)
        out = jnp.where((block == one_at)[:, None, None], one[None], out)
        return out.reshape(table_blocks * BLK, width)

    new_first = written(first_table, first, first_1)
    new_second = written(second_table, second, second_1)

    update = rotate_back(core, basis, gathered, swap_cores(gathered)).T
    lent = from_owner(update.astype(f16), back_to_helper).astype(f32)
    update = jnp.concatenate(
        [jnp.where(count >= 1, update, 0.0), jnp.where(doubled, lent, 0.0)], axis=0
    )
    return (update, new_first, new_second)


def solution(mesh):
    split = Mesh(
        mesh.devices.reshape(OWNERS, XS, ZH, ZL, CORES), ("y", "x", "zh", "zl", "c")
    )
    hidden = ("x", "zh", "zl", "c")
    placed = (P("y", hidden), P("y", hidden), P("y", hidden), P(hidden, None), P())
    return jax.shard_map(
        shards,
        mesh=split,
        in_specs=placed,
        out_specs=(P("y", hidden),) * 3,
        check_vma=False,
    )
```

time: 285 us -> 164 us (0.58)
  waiting for transfers between devices: 243 us -> 35.2 us
  starting transfers between devices: 0.08 us -> 39.9 us
  blocking collectives: 0 us -> 34.1 us
  Pallas kernels: 0 us -> 25.9 us
  matrix products: 17.7 us -> 0 us
  other arithmetic: 3.62 us -> 14 us
  between operations: 14.1 us -> 5.38 us
    reduce_scatter x1 -> x0, waiting for transfers between devices: 162 us -> none  [rotate(): lax.psum_scatter(lax.dot_general(basis, row_block, (((0,), (1,)), ((), ()...]
    all_gather x1 -> x0, waiting for transfers between devices: 80.8 us -> none  [rotate_back(): lax.all_gather(direction, 'hidden', axis=1, tiled=True)]
    all_to_all x0 -> x2, blocking collectives: none -> 34.1 us  [all_to_all(): return lax.all_to_all(x, axes, 0, 0, tiled=True)]
    ppermute x0 -> x17, starting transfers between devices: none -> 27.1 us  [the longest x15 19.2 us: from_owner(): lax.ppermute(x, 'y', [(i, (i + k) % OWNERS) for i in range(OWNERS)])]
    pallas_call x0 -> x2, Pallas kernels: none -> 25.9 us  [the longest x1 13.7 us: rotate_partials(): pl.pallas_call(rotate_kernel, grid=(XS * ZH,), in_specs=[pl.BlockSpec(mem...]
    all_to_all x0 -> x2, waiting for transfers between devices: none -> 23.7 us  [all_to_all(): return lax.all_to_all(x, axes, 0, 0, tiled=True)]
    dot_general x2 -> x0, matrix products: 17.7 us -> none  [the longest x1 10.3 us: rotate(): lax.dot_general(basis, row_block, (((0,), (1,)), ((), ())), preferred_ele...]
    all_to_all x0 -> x2, starting transfers between devices: none -> 12.8 us  [all_to_all(): return lax.all_to_all(x, axes, 0, 0, tiled=True)]
  transfers between devices with their start and end apart: 2 -> 19, of which waited for: 2 -> 9; matrix products, arithmetic and copies ran while one was open for 2% -> 7% of each run, Pallas kernels for 0% -> 0%
where the time goes in v1:
time: 164 us; the launch traced here: 163 us
  starting transfers between devices  39.9 us (24%)
  waiting for transfers between devices  35.2 us (21%)
  blocking collectives  34.1 us (21%)
  Pallas kernels  25.9 us (16%)
  other arithmetic  14 us (9%)
  local copies, waits for them, and re-layouts  8.35 us (5%)
  between operations  5.38 us (3%)
    all_to_all x2, blocking collectives, all_to_all(): return lax.all_to_all(x, axes, 0, 0, tiled=True)  34.1 us
    all_to_all x2, waiting for transfers between devices, all_to_all(): return lax.all_to_all(x, axes, 0, 0, tiled=True)  23.7 us
    ppermute x15, starting transfers between devices, from_owner(): lax.ppermute(x, 'y', [(i, (i + k) % OWNERS) for i in range(OWNERS)])  19.2 us
    pallas_call x1, Pallas kernels, rotate_partials(): pl.pallas_call(rotate_kernel, grid=(XS * ZH,), in_specs=[pl.BlockSpec(mem...  13.7 us
    all_to_all x2, starting transfers between devices, all_to_all(): return lax.all_to_all(x, axes, 0, 0, tiled=True)  12.8 us
    pallas_call x1, Pallas kernels, rotate_back(): pl.pallas_call(back_kernel, grid=(XS * ZH,), in_specs=[pl.BlockSpec(memor...  12.2 us
    ppermute x2, starting transfers between devices, swap_cores(): return lax.ppermute(x, 'c', [(0, 1), (1, 0)])  7.9 us
    ppermute x15, waiting for transfers between devices, from_owner(): lax.ppermute(x, 'y', [(i, (i + k) % OWNERS) for i in range(OWNERS)])  7.8 us
  transfers between devices with their start and end apart: 19, of which 9 were waited for; matrix products, arithmetic and copies ran while one was open for 7% of the time, Pallas kernels for 0%

profile of v1, /device:TPU:1, one launch (start us, length us, event | category | flops | bytes accessed | tf_op | source)
XLA Modules:
  0.0 162.9 jit_solution(7844883509216087324)
XLA Ops:
  0.6 0.8 slice.30
  1.5 3.6 %collective-permute-start.3 = (bf16[128,224]{0,1:T(8,128)(2,1)S(1)}, bf16[128,224]{0,1:T(8,128)(2,1)S(1)}, u32[]{:S(2)}, u32[]{:S(2)}) collective-permute-start(bf16[128,224]{0,1:T(8,128)(2,1)S(1)} %slice.30), channel_id=1, source_target_pairs={{0,192},{64,0},{128,64},{192,128},{1,193},{65,1},{129,65},{193,129... | collective-permute-start | bytes 172040 | tf_op jit(solution)/shard_map/ppermute | solution.py:98
  5.0 0.3 collective-permute-start.4
  5.4 0.7 collective-permute-start.5
  6.1 0.7 fusion.12
  6.8 0.2 reduce-window.9
  6.9 0.2 reduce-window.6
  7.1 0.6 constant_dynamic-slice_fusion
  7.7 1.9 %fusion.17 = (s32[]{:T(128)}, s32[]{:T(128)}) fusion(s32[4,1]{0,1:T(1,128)S(1)} %reduce-window.9, s32[4]{0:T(128)S(1)} %fusion.12, s32[]{:T(128)} %bitcast.21, s32[4,1]{0,1:T(1,128)S(1)} %reduce-window.6, s32[]{:T(128)} %bitcast.5), kind=kLoop, calls=%fused_computation.55 | loop fusion | flops 38 | bytes 64 | tf_op jit(solution)/shard_map/reduce_sum | solution.py:128
  10.3 0.6 dynamic_slice.12
  11.6 0.0 collective-permute-done.4
  11.6 0.8 slice_select_fusion
  12.4 0.7 copy.14.rows_ref
  13.2 13.7 %shard_map.76 = (f32[4,2,4,224,128]{4,3,2,1,0:T(8,128)}, f32[4,2,4,224,128]{4,3,2,1,0:T(8,128)}) custom-call(s32[1]{0:T(128)} %bitcast.1.core_ref, bf16[224,14336]{1,0:T(8,128)(2,1)} %basis_ref.3, bf16[128,224]{1,0:T(8,128)(2,1)} %copy.14.rows_ref), custom_call_target="tpu_custom_call" | custom-call | tf_op jit(solution)/shard_map/pallas_call | solution.py:39
  26.9 2.4 %convert_element_type.68 = f16[4,2,4,224,128]{4,3,2,1,0:T(8,128)(2,1)S(1)} convert(f32[4,2,4,224,128]{4,3,2,1,0:T(8,128)} %get-tuple-element.6) | non-fusion elementwise | flops 917504 | bytes 5505024 | tf_op jit(solution)/shard_map/convert_element_type | solution.py:147
  29.3 1.6 collective-permute-start.6
  30.9 3.4 %collective-permute-done.6 = f16[4,2,4,224,128]{4,3,2,1,0:T(8,128)(2,1)S(1)} collective-permute-done((f16[4,2,4,224,128]{4,3,2,1,0:T(8,128)(2,1)S(1)}, f16[4,2,4,224,128]{4,3,2,1,0:T(8,128)(2,1)S(1)}, u32[]{:S(2)}, u32[]{:S(2)}) %collective-permute-start.6) | collective-permute-done | bytes 1835040 | tf_op jit(solution)/shard_map/ppermute | solution.py:112
  34.3 1.8 %add_convert_fusion = f16[4,2,4,224,128]{4,3,2,1,0:T(8,128)(2,1)} fusion(f32[4,2,4,224,128]{4,3,2,1,0:T(8,128)S(1)} %copy-done.1, f16[4,2,4,224,128]{4,3,2,1,0:T(8,128)(2,1)S(1)} %collective-permute-done.6), kind=kLoop, calls=%fused_computation.3 | loop fusion | flops 2752512 | bytes 7340032 | tf_op jit(solution)/shard_map/convert_element_type | solution.py:147
  36.1 5.5 %all-to-all-start = ((f16[8,896,128]{2,1,0:T(8,128)(2,1)}), f16[8,896,128]{2,1,0:T(8,128)(2,1)S(1)}, u32[]{:S(2)}, u32[]{:S(2)}) async-start(f16[8,896,128]{2,1,0:T(8,128)(2,1)} %bitcast.10), calls=%async_computation | async-start | bytes 3670016 | tf_op jit(solution)/shard_map/all_to_all | solution.py:108
  41.6 0.7 fusion.20
  42.4 0.0 copy-start.5
  42.4 1.0 copy_bitcast_fusion
  43.4 1.7 %gather_fusion.1 = f32[2,128,224]{1,2,0:T(8,128)S(1)} fusion(f32[8,128,224]{1,2,0:T(8,128)} %copy_bitcast_fusion, s32[1024]{0:T(1024)S(1)} %pad_clamp_fusion), kind=kCustom, calls=%fused_computation.1 | custom fusion | bytes 458760 | tf_op jit(solution)/shard_map/gather | solution.py:138
  45.2 20.1 %all-to-all-done = f16[8,896,128]{2,1,0:T(8,128)(2,1)S(1)} async-done(((f16[8,896,128]{2,1,0:T(8,128)(2,1)}), f16[8,896,128]{2,1,0:T(8,128)(2,1)S(1)}, u32[]{:S(2)}, u32[]{:S(2)}) %all-to-all-start) | async-done | bytes 1835040 | tf_op jit(solution)/shard_map/all_to_all | solution.py:108
  65.2 0.3 convert_reduce_fusion
  65.5 0.0 copy-start.3
  65.5 0.7 convert_element_type.72
  66.2 7.3 %all-to-all-start.1 = ((f16[4,224,128]{2,1,0:T(8,128)(2,1)}), f16[4,224,128]{2,1,0:T(8,128)(2,1)S(1)}, u32[]{:S(2)}, u32[]{:S(2)}) async-start(f16[4,224,128]{2,1,0:T(8,128)(2,1)} %bitcast.11), calls=%async_computation.1 | async-start | bytes 458752 | tf_op jit(solution)/shard_map/all_to_all | solution.py:108
  73.5 2.1 %collective-permute-start.7 = (f32[128,224]{0,1:T(8,128)S(1)}, f32[128,224]{0,1:T(8,128)S(1)}, u32[]{:S(2)}, u32[]{:S(2)}) collective-permute-start(f32[128,224]{0,1:T(8,128)S(1)} %slice_bitcast_fusion.1), channel_id=1, source_target_pairs={{0,192},{64,0},{128,64},{192,128},{1,193},{65,1},{129,65},{193,129... | collective-permute-start | bytes 344072 | tf_op jit(solution)/shard_map/ppermute | solution.py:98
  75.6 1.4 collective-permute-start.8
  77.0 0.1 copy_bitcast_fusion.1
  77.1 0.7 gather_fusion
  77.8 3.6 %all-to-all-done.1 = f16[4,224,128]{2,1,0:T(8,128)(2,1)S(1)} async-done(((f16[4,224,128]{2,1,0:T(8,128)(2,1)}), f16[4,224,128]{2,1,0:T(8,128)(2,1)S(1)}, u32[]{:S(2)}, u32[]{:S(2)}) %all-to-all-start.1) | async-done | bytes 229408 | tf_op jit(solution)/shard_map/all_to_all | solution.py:108
  81.4 2.1 %collective-permute-start.14 = (f32[128,224]{0,1:T(8,128)S(1)}, f32[128,224]{0,1:T(8,128)S(1)}, u32[]{:S(2)}, u32[]{:S(2)}) collective-permute-start(f32[128,224]{0,1:T(8,128)S(1)} %multiply_bitcast_fusion), channel_id=1, source_target_pairs={{0,192},{64,0},{128,64},{192,128},{1,193},{65,1},{129,65},{193,129... | collective-permute-start | bytes 344072 | tf_op jit(solution)/shard_map/ppermute | solution.py:98
  83.5 1.4 collective-permute-start.15
  85.6 1.3 collective-permute-start.9
  86.9 2.7 %collective-permute-start = (f32[128,224]{0,1:T(8,128)S(1)}, f32[128,224]{0,1:T(8,128)S(1)}, u32[]{:S(2)}, u32[]{:S(2)}) collective-permute-start(f32[128,224]{0,1:T(8,128)S(1)} %slice_bitcast_fusion.3), channel_id=1, source_target_pairs={{0,192},{64,0},{128,64},{192,128},{1,193},{65,1},{129,65},{193,129... | collective-permute-start | bytes 344072 | tf_op jit(solution)/shard_map/ppermute | solution.py:98
  89.6 0.6 collective-permute-start.1
  90.1 0.2 collective-permute-start.2
  90.4 0.7 collective-permute-done.9
  91.1 1.6 %collective-permute-done = f32[128,224]{0,1:T(8,128)S(1)} collective-permute-done((f32[128,224]{0,1:T(8,128)S(1)}, f32[128,224]{0,1:T(8,128)S(1)}, u32[]{:S(2)}, u32[]{:S(2)}) %collective-permute-start) | collective-permute-done | bytes 114720 | tf_op jit(solution)/shard_map/ppermute | solution.py:98
  92.7 2.9 %collective-permute-done.1 = f32[128,224]{0,1:T(8,128)S(1)} collective-permute-done((f32[128,224]{0,1:T(8,128)S(1)}, f32[128,224]{0,1:T(8,128)S(1)}, u32[]{:S(2)}, u32[]{:S(2)}) %collective-permute-start.1) | collective-permute-done | bytes 114720 | tf_op jit(solution)/shard_map/ppermute | solution.py:98
  95.6 2.0 %collective-permute-done.2 = f32[128,224]{0,1:T(8,128)S(1)} collective-permute-done((f32[128,224]{0,1:T(8,128)S(1)}, f32[128,224]{0,1:T(8,128)S(1)}, u32[]{:S(2)}, u32[]{:S(2)}) %collective-permute-start.2) | collective-permute-done | bytes 114720 | tf_op jit(solution)/shard_map/ppermute | solution.py:98
  97.6 0.1 fusion.9
  97.8 11.2 %all_to_all.20 = bf16[4,224,128]{2,1,0:T(8,128)(2,1)S(1)} all-to-all(bf16[4,224,128]{2,1,0:T(8,128)(2,1)S(1)} %broadcast_in_dim.90), channel_id=1, replica_groups=mesh['y'=4,'x'=4,'zh'=4,'zl'=2,'c'=2] {'zh'}, dimensions={0} | all-to-all | bytes 458752 | tf_op jit(solution)/shard_map/all_to_all | solution.py:108
  109.0 0.3 broadcast_in_dim.91
  109.3 22.9 %all_to_all.21 = bf16[8,4,224,128]{3,2,1,0:T(8,128)(2,1)S(1)} all-to-all(bf16[8,4,224,128]{3,2,1,0:T(8,128)(2,1)S(1)} %broadcast_in_dim.91), channel_id=1, replica_groups=mesh['y'=4,'x'=4,'zh'=4,'zl'=2,'c'=2] {'x','zl'}, dimensions={0} | all-to-all | bytes 3670016 | tf_op jit(solution)/shard_map/all_to_all | solution.py:108
  132.2 6.3 %collective-permute-start.10 = (bf16[4,2,4,224,128]{4,3,2,1,0:T(8,128)(2,1)S(1)}, bf16[4,2,4,224,128]{4,3,2,1,0:T(8,128)(2,1)}, u32[]{:S(2)}, u32[]{:S(2)}) collective-permute-start(bf16[4,2,4,224,128]{4,3,2,1,0:T(8,128)(2,1)S(1)} %bitcast.114), channel_id=1, source_target_pairs={{0,1},{1,0},{2,3},{3,2},{4,5},{5,4},{6,7},{7,6},{8,9},{9,8},{10,11... | collective-permute-start | bytes 5505032 | tf_op jit(solution)/shard_map/ppermute | solution.py:112
  139.8 0.5 fusion.21
  141.6 0.1 broadcast_bitcast_fusion
  141.7 0.3 collective-permute-done.10.other_ref
  142.0 12.2 %shard_map.77 = f32[224,128]{1,0:T(8,128)} custom-call(s32[1]{0:T(128)} %bitcast.1.core_ref, bf16[224,14336]{1,0:T(8,128)(2,1)} %basis_ref.3, bf16[4,2,4,224,128]{4,3,2,1,0:T(8,128)(2,1)} %bitcast.115, bf16[4,2,4,224,128]{4,3,2,1,0:T(8,128)(2,1)} %collective-permute-done.10.other_ref), custom_call_target="tpu_custom_call" | custom-call | tf_op jit(solution)/shard_map/pallas_call | solution.py:75
  154.3 1.0 select_bitcast_fusion
  155.3 0.6 collective-permute-start.11
  155.9 1.5 collective-permute-start.12
  157.4 0.7 collective-permute-start.13
  158.1 0.1 broadcast_in_dim.106
  158.2 0.1 broadcast_in_dim.104
  158.3 0.1 broadcast_in_dim.102
  158.3 0.1 broadcast_in_dim.97
  158.4 0.9 copy-done.4
  159.3 2.3 %fusion = (f32[1024,224]{0,1:T(8,128)}, f32[1024,224]{0,1:T(8,128)}) fusion(f32[1024,224]{0,1:T(8,128)S(1)} %copy-done.2, f32[28,8,8,128]{3,2,1,0:T(8,128)S(1)} %bitcast.116, f32[28,8,8,128]{3,2,1,0:T(8,128)S(1)} %bitcast.117, pred[1024]{0:T(1024)(128)(4,1)S(1)} %get-tuple-element.27, pred[1024]{0:T(1024)(128)(4,1)S(1)} %get-tuple-element.28, ...), kind=kLoop, calls=%fused_computation.5 | loop fusion | flops 917504 | bytes 7342080 | tf_op jit(solution)/shard_map/jit(_where)/select_n | solution.py:167
  161.6 0.5 collective-permute-done.13
  162.2 0.7 pad_maximum_fusion
  (35 shorter events, 0.2 us)
Async XLA Ops:
  1.5 10.1 %collective-permute-start.3 = (bf16[128,224]{0,1:T(8,128)(2,1)S(1)}, bf16[128,224]{0,1:T(8,128)(2,1)S(1)}, u32[]{:S(2)}, u32[]{:S(2)}) collective-permute-start(bf16[128,224]{0,1:T(8,128)(2,1)S(1)} %slice.30), channel_id=1, source_target_pairs={{0,192},{64,0},{128,64},{192,128},{1,193},{65,1},{129,65},{193,129... | collective-permute-start | bytes 172040 | tf_op jit(solution)/shard_map/ppermute | solution.py:98
  5.0 6.6 %collective-permute-start.4 = (bf16[128,224]{0,1:T(8,128)(2,1)S(1)}, bf16[128,224]{0,1:T(8,128)(2,1)S(1)}, u32[]{:S(2)}, u32[]{:S(2)}) collective-permute-start(bf16[128,224]{0,1:T(8,128)(2,1)S(1)} %slice.30), channel_id=1, source_target_pairs={{0,128},{64,192},{128,0},{192,64},{1,129},{65,193},{129,1},{193,65... | collective-permute-start | bytes 172040 | tf_op jit(solution)/shard_map/ppermute | solution.py:98
  5.4 6.2 %collective-permute-start.5 = (bf16[128,224]{0,1:T(8,128)(2,1)S(1)}, bf16[128,224]{0,1:T(8,128)(2,1)S(1)}, u32[]{:S(2)}, u32[]{:S(2)}) collective-permute-start(bf16[128,224]{0,1:T(8,128)(2,1)S(1)} %slice.30), channel_id=1, source_target_pairs={{0,64},{64,128},{128,192},{192,0},{1,65},{65,129},{129,193},{193,1... | collective-permute-start | bytes 172040 | tf_op jit(solution)/shard_map/ppermute | solution.py:98
  26.9 7.5 %copy-start.1 = (f32[4,2,4,224,128]{4,3,2,1,0:T(8,128)S(1)}, f32[4,2,4,224,128]{4,3,2,1,0:T(8,128)}, u32[]{:S(2)}) copy-start(f32[4,2,4,224,128]{4,3,2,1,0:T(8,128)} %get-tuple-element.5) | copy-start | bytes 11010052
  29.3 5.0 %collective-permute-start.6 = (f16[4,2,4,224,128]{4,3,2,1,0:T(8,128)(2,1)S(1)}, f16[4,2,4,224,128]{4,3,2,1,0:T(8,128)(2,1)S(1)}, u32[]{:S(2)}, u32[]{:S(2)}) collective-permute-start(f16[4,2,4,224,128]{4,3,2,1,0:T(8,128)(2,1)S(1)} %convert_element_type.68), channel_id=1, source_target_pairs={{0,1},{1,0},{2,3},{3,2},{4,5},{5,4},{6,7},{7,6},{8,9},{9,8},{10,11... | collective-permute-start | bytes 5505032 | tf_op jit(solution)/shard_map/ppermute | solution.py:112
  36.1 5.5 %copy-start.7 = (s32[4,2]{0,1:T(2,128)S(1)}, s32[4,2]{0,1:T(2,128)}, u32[]{:S(2)}) copy-start(s32[4,2]{0,1:T(2,128)} %param.9) | copy-start | bytes 100
  36.1 6.3 %copy-start.2 = (f32[1024,224]{0,1:T(8,128)S(1)}, f32[1024,224]{0,1:T(8,128)}, u32[]{:S(2)}) copy-start(f32[1024,224]{0,1:T(8,128)} %param.7) | copy-start | bytes 2752516
  36.1 29.1 %all-to-all-start = ((f16[8,896,128]{2,1,0:T(8,128)(2,1)}), f16[8,896,128]{2,1,0:T(8,128)(2,1)S(1)}, u32[]{:S(2)}, u32[]{:S(2)}) async-start(f16[8,896,128]{2,1,0:T(8,128)(2,1)} %bitcast.10), calls=%async_computation | async-start | bytes 3670016 | tf_op jit(solution)/shard_map/all_to_all | solution.py:108
  42.4 33.2 %copy-start.5 = (s32[1024]{0:T(1024)}, s32[1024]{0:T(1024)S(1)}, u32[]{:S(2)}) copy-start(s32[1024]{0:T(1024)S(1)} %pad_clamp_fusion) | copy-start | bytes 12292
  65.5 11.5 %copy-start.3 = (f32[1024,224]{0,1:T(8,128)S(1)}, f32[1024,224]{0,1:T(8,128)}, u32[]{:S(2)}) copy-start(f32[1024,224]{0,1:T(8,128)} %param.6) | copy-start | bytes 2752516
  66.2 15.1 %all-to-all-start.1 = ((f16[4,224,128]{2,1,0:T(8,128)(2,1)}), f16[4,224,128]{2,1,0:T(8,128)(2,1)S(1)}, u32[]{:S(2)}, u32[]{:S(2)}) async-start(f16[4,224,128]{2,1,0:T(8,128)(2,1)} %bitcast.11), calls=%async_computation.1 | async-start | bytes 458752 | tf_op jit(solution)/shard_map/all_to_all | solution.py:108
  73.5 12.0 %collective-permute-start.7 = (f32[128,224]{0,1:T(8,128)S(1)}, f32[128,224]{0,1:T(8,128)S(1)}, u32[]{:S(2)}, u32[]{:S(2)}) collective-permute-start(f32[128,224]{0,1:T(8,128)S(1)} %slice_bitcast_fusion.1), channel_id=1, source_target_pairs={{0,192},{64,0},{128,64},{192,128},{1,193},{65,1},{129,65},{193,129... | collective-permute-start | bytes 344072 | tf_op jit(solution)/shard_map/ppermute | solution.py:98
  75.6 14.8 %collective-permute-start.8 = (f32[128,224]{0,1:T(8,128)S(1)}, f32[128,224]{0,1:T(8,128)S(1)}, u32[]{:S(2)}, u32[]{:S(2)}) collective-permute-start(f32[128,224]{0,1:T(8,128)S(1)} %slice_bitcast_fusion.1), channel_id=1, source_target_pairs={{0,128},{64,192},{128,0},{192,64},{1,129},{65,193},{129,1},{193,65... | collective-permute-start | bytes 344072 | tf_op jit(solution)/shard_map/ppermute | solution.py:98
  81.4 5.5 %collective-permute-start.14 = (f32[128,224]{0,1:T(8,128)S(1)}, f32[128,224]{0,1:T(8,128)S(1)}, u32[]{:S(2)}, u32[]{:S(2)}) collective-permute-start(f32[128,224]{0,1:T(8,128)S(1)} %multiply_bitcast_fusion), channel_id=1, source_target_pairs={{0,192},{64,0},{128,64},{192,128},{1,193},{65,1},{129,65},{193,129... | collective-permute-start | bytes 344072 | tf_op jit(solution)/shard_map/ppermute | solution.py:98
  83.5 6.1 %collective-permute-start.15 = (f32[128,224]{0,1:T(8,128)S(1)}, f32[128,224]{0,1:T(8,128)S(1)}, u32[]{:S(2)}, u32[]{:S(2)}) collective-permute-start(f32[128,224]{0,1:T(8,128)S(1)} %multiply_bitcast_fusion), channel_id=1, source_target_pairs={{0,128},{64,192},{128,0},{192,64},{1,129},{65,193},{129,1},{193,65... | collective-permute-start | bytes 344072 | tf_op jit(solution)/shard_map/ppermute | solution.py:98
  84.9 5.3 %collective-permute-start.16 = (f32[128,224]{0,1:T(8,128)S(1)}, f32[128,224]{0,1:T(8,128)S(1)}, u32[]{:S(2)}, u32[]{:S(2)}) collective-permute-start(f32[128,224]{0,1:T(8,128)S(1)} %multiply_bitcast_fusion), channel_id=1, source_target_pairs={{0,64},{64,128},{128,192},{192,0},{1,65},{65,129},{129,193},{193,1... | collective-permute-start | bytes 344072 | tf_op jit(solution)/shard_map/ppermute | solution.py:98
  85.6 5.5 %collective-permute-start.9 = (f32[128,224]{0,1:T(8,128)S(1)}, f32[128,224]{0,1:T(8,128)S(1)}, u32[]{:S(2)}, u32[]{:S(2)}) collective-permute-start(f32[128,224]{0,1:T(8,128)S(1)} %slice_bitcast_fusion.1), channel_id=1, source_target_pairs={{0,64},{64,128},{128,192},{192,0},{1,65},{65,129},{129,193},{193,1... | collective-permute-start | bytes 344072 | tf_op jit(solution)/shard_map/ppermute | solution.py:98
  86.9 5.8 %collective-permute-start = (f32[128,224]{0,1:T(8,128)S(1)}, f32[128,224]{0,1:T(8,128)S(1)}, u32[]{:S(2)}, u32[]{:S(2)}) collective-permute-start(f32[128,224]{0,1:T(8,128)S(1)} %slice_bitcast_fusion.3), channel_id=1, source_target_pairs={{0,192},{64,0},{128,64},{192,128},{1,193},{65,1},{129,65},{193,129... | collective-permute-start | bytes 344072 | tf_op jit(solution)/shard_map/ppermute | solution.py:98
  89.6 6.0 %collective-permute-start.1 = (f32[128,224]{0,1:T(8,128)S(1)}, f32[128,224]{0,1:T(8,128)S(1)}, u32[]{:S(2)}, u32[]{:S(2)}) collective-permute-start(f32[128,224]{0,1:T(8,128)S(1)} %slice_bitcast_fusion.3), channel_id=1, source_target_pairs={{0,128},{64,192},{128,0},{192,64},{1,129},{65,193},{129,1},{193,65... | collective-permute-start | bytes 344072 | tf_op jit(solution)/shard_map/ppermute | solution.py:98
  90.1 7.5 %collective-permute-start.2 = (f32[128,224]{0,1:T(8,128)S(1)}, f32[128,224]{0,1:T(8,128)S(1)}, u32[]{:S(2)}, u32[]{:S(2)}) collective-permute-start(f32[128,224]{0,1:T(8,128)S(1)} %slice_bitcast_fusion.3), channel_id=1, source_target_pairs={{0,64},{64,128},{128,192},{192,0},{1,65},{65,129},{129,193},{193,1... | collective-permute-start | bytes 344072 | tf_op jit(solution)/shard_map/ppermute | solution.py:98
  109.3 30.5 %copy-start.6 = (s32[1,2]{0,1:T(2,128)S(1)}, s32[1,2]{0,1:T(2,128)}, u32[]{:S(2)}) copy-start(s32[1,2]{0,1:T(2,128)} %get-tuple-element.15) | copy-start | bytes 28
  132.2 9.9 %copy-start = (bf16[8,4,224,128]{3,2,1,0:T(8,128)(2,1)}, bf16[8,4,224,128]{3,2,1,0:T(8,128)(2,1)S(1)}, u32[]{:S(2)}) copy-start(bf16[8,4,224,128]{3,2,1,0:T(8,128)(2,1)S(1)} %all_to_all.21) | copy-start | bytes 5505028
  132.2 9.8 %collective-permute-start.10 = (bf16[4,2,4,224,128]{4,3,2,1,0:T(8,128)(2,1)S(1)}, bf16[4,2,4,224,128]{4,3,2,1,0:T(8,128)(2,1)}, u32[]{:S(2)}, u32[]{:S(2)}) collective-permute-start(bf16[4,2,4,224,128]{4,3,2,1,0:T(8,128)(2,1)S(1)} %bitcast.114), channel_id=1, source_target_pairs={{0,1},{1,0},{2,3},{3,2},{4,5},{5,4},{6,7},{7,6},{8,9},{9,8},{10,11... | collective-permute-start | bytes 5505032 | tf_op jit(solution)/shard_map/ppermute | solution.py:112
  155.3 6.4 %collective-permute-start.11 = (f16[128,224]{0,1:T(8,128)(2,1)S(1)}, f16[128,224]{0,1:T(8,128)(2,1)S(1)}, u32[]{:S(2)}, u32[]{:S(2)}) collective-permute-start(f16[128,224]{0,1:T(8,128)(2,1)S(1)} %get-tuple-element.18), channel_id=1, source_target_pairs={{0,192},{64,0},{128,64},{192,128},{1,193},{65,1},{129,65},{193,129... | collective-permute-start | bytes 172040 | tf_op jit(solution)/shard_map/ppermute | solution.py:98
  155.9 5.7 %collective-permute-start.12 = (f16[128,224]{0,1:T(8,128)(2,1)S(1)}, f16[128,224]{0,1:T(8,128)(2,1)S(1)}, u32[]{:S(2)}, u32[]{:S(2)}) collective-permute-start(f16[128,224]{0,1:T(8,128)(2,1)S(1)} %get-tuple-element.18), channel_id=1, source_target_pairs={{0,128},{64,192},{128,0},{192,64},{1,129},{65,193},{129,1},{193,65... | collective-permute-start | bytes 172040 | tf_op jit(solution)/shard_map/ppermute | solution.py:98
  157.4 4.7 %collective-permute-start.13 = (f16[128,224]{0,1:T(8,128)(2,1)S(1)}, f16[128,224]{0,1:T(8,128)(2,1)S(1)}, u32[]{:S(2)}, u32[]{:S(2)}) collective-permute-start(f16[128,224]{0,1:T(8,128)(2,1)S(1)} %get-tuple-element.18), channel_id=1, source_target_pairs={{0,64},{64,128},{128,192},{192,0},{1,65},{65,129},{129,193},{193,1... | collective-permute-start | bytes 172040 | tf_op jit(solution)/shard_map/ppermute | solution.py:98
  158.1 1.2 copy-start.4

commit v2 on v0

v2 whole, which is shorter than its diff:
```python
import functools

import jax
import jax.numpy as jnp
from jax import lax
from jax.experimental import pallas as pl
from jax.experimental.pallas import tpu as pltpu
from jax.sharding import PartitionSpec as P

BLK = 128
OWNERS = 4
XS, ZS, CORES = 4, 8, 2
HIDDEN = XS * ZS * CORES
NEAR, FAR = 4, 8
SCALE = 4.0
VMEM_LIMIT = 32 * 2**20
NEAR_LIMIT = 32 * 2**20

beta_first = 0.9
beta_second = 0.95
epsilon = 1e-08

f32, bf16, f16 = jnp.float32, jnp.bfloat16, jnp.float16

smem = pl.BlockSpec(memory_space=pltpu.SMEM)
vmem = pl.BlockSpec(memory_space=pltpu.VMEM)
anywhere = pl.BlockSpec(memory_space=pl.ANY)
params = pltpu.CompilerParams(vmem_limit_bytes=VMEM_LIMIT)

MATCH, COUNT, ID_0, ID_1 = range(4)


def live_slots(ids_ref, owner):
    return (ids_ref[0, owner] >= 0).astype(jnp.int32) + (ids_ref[1, owner] >= 0).astype(jnp.int32)


def matching(ids_ref):
    zero = live_slots(ids_ref, 0)
    return jnp.where(
        zero + live_slots(ids_ref, 1) == 2,
        1,
        jnp.where(zero + live_slots(ids_ref, 2) == 2, 2, 3),
    )


def pick(match, options):
    return jnp.where(match == 1, options[0], jnp.where(match == 2, options[1], options[2]))


def near_kernel(basis_ref, out_ref, sem):
    copy = pltpu.make_async_copy(basis_ref, out_ref, sem)
    copy.start()
    copy.wait()


def brought_near(basis):
    return pl.pallas_call(
        near_kernel,
        in_specs=[anywhere],
        out_specs=vmem,
        out_shape=jax.ShapeDtypeStruct(basis.shape, basis.dtype),
        scratch_shapes=[pltpu.SemaphoreType.DMA],
        compiler_params=pltpu.CompilerParams(vmem_limit_bytes=NEAR_LIMIT),
    )(basis)


def rotate_kernel(
    ids_ref, basis_ref, own_ref, one_ref, two_ref, three_ref, keep_ref, send_ref, roles_ref
):
    width = own_ref.shape[0]
    cols = 2 * CORES * width
    me = lax.axis_index("vocab")
    match, count = matching(ids_ref), live_slots(ids_ref, me)
    roles_ref[MATCH], roles_ref[COUNT] = match, count
    roles_ref[ID_0], roles_ref[ID_1] = ids_ref[0, me], ids_ref[1, me]
    lent = pick(match, [one_ref[...], two_ref[...], three_ref[...]])
    rows = jnp.where(count == 0, lent, own_ref[...]) * jnp.bfloat16(SCALE)
    mine = lax.rem(lax.axis_index("hidden"), CORES) == 0

    for i in range(XS * ZS // 2):
        at = pl.ds(i * cols, cols)
        part = lax.dot_general(
            basis_ref[:, at], rows, (((0,), (0,)), ((), ())), preferred_element_type=f32
        ).reshape(2, CORES, width, BLK)
        for j in range(2):
            even, odd = part[j, 0], part[j, 1]
            to_even, to_odd = (place(2 * i + j, core) for core in range(CORES))
            keep_at = [jnp.where(mine, a, b) for a, b in zip(to_even, to_odd)]
            send_at = [jnp.where(mine, b, a) for a, b in zip(to_even, to_odd)]
            keep_ref[keep_at[0], keep_at[1]] = jnp.where(mine, even, odd)
            send_ref[send_at[0], send_at[1]] = jnp.where(mine, odd, even).astype(bf16)


def rotate_partials(ids, basis, own, lent):
    shape = (NEAR, FAR, own.shape[0], BLK)
    return pl.pallas_call(
        rotate_kernel,
        in_specs=[smem] + [vmem] * 5,
        out_specs=[vmem, vmem, smem],
        out_shape=[
            jax.ShapeDtypeStruct(shape, f32),
            jax.ShapeDtypeStruct(shape, bf16),
            jax.ShapeDtypeStruct((4,), jnp.int32),
        ],
        compiler_params=params,
    )(ids, basis, own, *lent)


def adam_moments(rotated, old_first, old_second):
    first = beta_first * old_first + (1.0 - beta_first) * rotated
    second = beta_second * old_second + (1.0 - beta_second) * rotated * rotated
    return first, second


def back_kernel(basis_ref, own_ref, other_ref, out_ref):
    width = basis_ref.shape[0]
    cols = 2 * CORES * width
    mine = lax.rem(lax.axis_index("hidden"), CORES) == 0
    total = jnp.zeros((width, BLK), f32)
    for i in range(XS * ZS // 2):
        pieces = []
        for j in range(2):
            even, odd = (place(2 * i + j, core) for core in range(CORES))
            pieces.append(jnp.where(mine, own_ref[even], other_ref[even]))
            pieces.append(jnp.where(mine, other_ref[odd], own_ref[odd]))
        total += jnp.dot(
            basis_ref[:, i * cols : (i + 1) * cols],
            jnp.concatenate(pieces, axis=0),
            preferred_element_type=f32,
        )
    out_ref[...] = total


def rotate_back(basis, own, other):
    return pl.pallas_call(
        back_kernel,
        in_specs=[vmem] * 3,
        out_specs=vmem,
        out_shape=jax.ShapeDtypeStruct((basis.shape[0], BLK), f32),
        compiler_params=params,
    )(basis, own, other)


def place(chip, core):
    x, z = (chip // ZS + core) % XS, (chip % ZS + core) % ZS
    return ((x + 1) // 2 % 2) * 2 + z % 2, (x // 2) * (ZS // 2) + z // 2


def groups():
    near = [[None] * NEAR for _ in range(CORES * FAR)]
    far = [[None] * FAR for _ in range(CORES * NEAR)]
    for chip in range(XS * ZS):
        for core in range(CORES):
            a, b = place(chip, core)
            near[core * FAR + b][a] = far[core * NEAR + a][b] = chip * CORES + core
    return near, far


NEAR_GROUPS, FAR_GROUPS = groups()


def all_to_all(x, members):
    return lax.all_to_all(x, "hidden", 0, 0, axis_index_groups=members, tiled=True)


def swap_cores(x):
    return lax.ppermute(x, "hidden", [(i, i ^ 1) for i in range(HIDDEN)])


def swap_owners_by(k, x):
    return lax.ppermute(x, "vocab", [(i, i ^ k) for i in range(OWNERS)])


def swap_owners(x):
    return [swap_owners_by(k, x) for k in (1, 2, 3)]


def swap_with_partner(match, x):
    return lax.switch(
        match - 1, [functools.partial(swap_owners_by, k) for k in range(1, OWNERS)], x
    )


def together(*x):
    return lax.optimization_barrier(x)


def shards(gradient, moment_first, moment_second, basis, block_ids):
    gradient, moment_first, moment_second = gradient.T, moment_first.T, moment_second.T
    ids = block_ids.T
    width = gradient.shape[0]

    def rows_of(table, block):
        return lax.dynamic_slice_in_dim(table, jnp.maximum(block, 0) * BLK, BLK, 1)

    lent_rows = swap_owners(gradient[:, BLK:])
    keep, send, roles = rotate_partials(ids, brought_near(basis), gradient[:, :BLK], lent_rows)
    match, own_ids = roles[MATCH], roles[ID_0 : ID_1 + 1]
    helping, doubled = roles[COUNT] == 0, roles[COUNT] == 2
    held_first = rows_of(moment_first, own_ids[1])
    held_second = rows_of(moment_second, own_ids[1])
    held = jnp.concatenate([held_first, held_second], axis=1)
    part = (keep + swap_cores(send).astype(f32)).astype(f16)
    lent = swap_with_partner(match, held)
    old_first = jnp.where(helping, lent[:, :BLK], rows_of(moment_first, own_ids[0]))
    old_second = jnp.where(helping, lent[:, BLK:], rows_of(moment_second, own_ids[0]))

    part = all_to_all(part, NEAR_GROUPS)
    part, old_first, old_second = together(part, old_first, old_second)
    part = all_to_all(jnp.sum(part.astype(f32), axis=0).astype(f16), FAR_GROUPS)
    rotated = jnp.sum(part.astype(f32), axis=0) * (1.0 / SCALE)

    first, second = adam_moments(rotated, old_first, old_second)
    direction = (first / (jnp.sqrt(second) + epsilon)).astype(bf16)
    gathered = all_to_all(jnp.broadcast_to(direction[None], (FAR, width, BLK)), FAR_GROUPS)
    other_rotated = swap_with_partner(match, rotated)
    first_1, second_1 = adam_moments(other_rotated, held_first, held_second)
    gathered, first_1, second_1, basis = together(gathered, first_1, second_1, basis)
    basis = brought_near(basis)
    gathered = jnp.broadcast_to(gathered[None], (NEAR, FAR, width, BLK))
    gathered = all_to_all(gathered, NEAR_GROUPS)

    def written(table, slot_0, slot_1):
        for block, live, new in ((own_ids[0], ~helping, slot_0), (own_ids[1], doubled, slot_1)):
            new = jnp.where(live, new, rows_of(table, block))
            table = lax.dynamic_update_slice_in_dim(table, new, jnp.maximum(block, 0) * BLK, 1)
        return table

    new_first = written(moment_first, first, first_1)
    new_second = written(moment_second, second, second_1)
    gathered, new_first, new_second = together(gathered, new_first, new_second)

    update = rotate_back(basis, gathered, swap_cores(gathered))
    lent_update = swap_with_partner(match, update)
    update = jnp.concatenate([update, lent_update], axis=1)
    second_half = lax.broadcasted_iota(jnp.int32, update.shape, 1) >= BLK
    update = jnp.where(jnp.where(second_half, doubled, ~helping), update, 0.0)
    return (update.T, new_first.T, new_second.T)


def solution(mesh):
    placed = P("vocab", "hidden")
    return jax.shard_map(
        shards,
        mesh=mesh,
        in_specs=(placed, placed, placed, P("hidden", None), P()),
        out_specs=(placed,) * 3,
        check_vma=False,
    )
```

time: 285 us -> 116 us (0.41)
  waiting for transfers between devices: 243 us -> 49.4 us
  starting transfers between devices: 0.08 us -> 35 us
  matrix products: 17.7 us -> 0 us
  between operations: 14.1 us -> 4.01 us
  Pallas kernels: 0 us -> 6.25 us
  other arithmetic: 3.62 us -> 8.87 us
  local copies, waits for them, and re-layouts: 6.94 us -> 11.4 us
    reduce_scatter x1 -> x0, waiting for transfers between devices: 162 us -> none  [rotate(): lax.psum_scatter(lax.dot_general(basis, row_block, (((0,), (1,)), ((), ()...]
    all_gather x1 -> x0, waiting for transfers between devices: 80.8 us -> none  [rotate_back(): lax.all_gather(direction, 'hidden', axis=1, tiled=True)]
    all_to_all x0 -> x4, waiting for transfers between devices: none -> 34.8 us  [all_to_all(): lax.all_to_all(x, 'hidden', 0, 0, axis_index_groups=members, tiled=True)]
    all_to_all x0 -> x4, starting transfers between devices: none -> 25.2 us  [all_to_all(): lax.all_to_all(x, 'hidden', 0, 0, axis_index_groups=members, tiled=True)]
    dot_general x2 -> x0, matrix products: 17.7 us -> none  [the longest x1 10.3 us: rotate(): lax.dot_general(basis, row_block, (((0,), (1,)), ((), ())), preferred_ele...]
    ppermute x0 -> x8, waiting for transfers between devices: none -> 14.7 us  [the longest x6 11.2 us: swap_owners_by(): return lax.ppermute(x, 'vocab', [(i, i ^ k) for i in range(OWNERS)])]
    ppermute x0 -> x8, starting transfers between devices: none -> 9.75 us  [the longest x6 7.51 us: swap_owners_by(): return lax.ppermute(x, 'vocab', [(i, i ^ k) for i in range(OWNERS)])]
    pallas_call x0 -> x4, Pallas kernels: none -> 6.25 us  [the longest x1 3.14 us: rotate_partials(): pl.pallas_call(rotate_kernel, in_specs=[smem] + [vmem] * 5, out_specs=[vm...]
  transfers between devices with their start and end apart: 2 -> 12, of which waited for: 2 -> 9; matrix products, arithmetic and copies ran while one was open for 2% -> 5% of each run, Pallas kernels for 0% -> 1%
where the time goes in v2:
time: 116 us; the launch traced here: 115 us
  waiting for transfers between devices  49.4 us (43%)
  starting transfers between devices  35 us (30%)
  local copies, waits for them, and re-layouts  11.4 us (10%)
  other arithmetic  8.87 us (8%)
  Pallas kernels  6.25 us (5%)
  between operations  4.01 us (3%)
    all_to_all x4, waiting for transfers between devices, all_to_all(): lax.all_to_all(x, 'hidden', 0, 0, axis_index_groups=members, tiled=True)  34.8 us
    all_to_all x4, starting transfers between devices, all_to_all(): lax.all_to_all(x, 'hidden', 0, 0, axis_index_groups=members, tiled=True)  25.2 us
    ppermute x6, waiting for transfers between devices, swap_owners_by(): return lax.ppermute(x, 'vocab', [(i, i ^ k) for i in range(OWNERS)])  11.2 us
    ppermute x6, starting transfers between devices, swap_owners_by(): return lax.ppermute(x, 'vocab', [(i, i ^ k) for i in range(OWNERS)])  7.51 us
    unnamed x14, local copies, waits for them, and re-layouts  6.67 us
    ppermute x2, waiting for transfers between devices, swap_cores(): return lax.ppermute(x, 'hidden', [(i, i ^ 1) for i in range(HIDDEN)])  3.41 us
    pallas_call x1, Pallas kernels, rotate_partials(): pl.pallas_call(rotate_kernel, in_specs=[smem] + [vmem] * 5, out_specs=[vm...  3.14 us
    dynamic_update_slice x2, other arithmetic, written(): lax.dynamic_update_slice_in_dim(table, new, jnp.maximum(block, 0) * BLK, 1)  2.33 us
  transfers between devices with their start and end apart: 12, of which 9 were waited for; matrix products, arithmetic and copies ran while one was open for 5% of the time, Pallas kernels for 1%

profile of v2, /device:TPU:1, one launch (start us, length us, event | category | flops | bytes accessed | tf_op | source)
XLA Modules:
  0.0 115.0 jit_solution(14738030626244754958)
XLA Ops:
  0.6 0.9 fusion.4
  1.5 0.0 copy-start.2
  1.5 3.8 %collective-permute-start.10 = (bf16[224,128]{1,0:T(8,128)(2,1)S(1)}, bf16[224,128]{1,0:T(8,128)(2,1)S(1)}, u32[]{:S(2)}, u32[]{:S(2)}) collective-permute-start(bf16[224,128]{1,0:T(8,128)(2,1)S(1)} %get-tuple-element.64), channel_id=1, source_target_pairs={{0,128},{64,192},{128,0},{192,64},{1,129},{65,193},{129,1},{193,65... | collective-permute-start | bytes 172040 | tf_op jit(solution)/shard_map/ppermute | solution.py:171
  5.3 0.8 collective-permute-start.11
  6.1 0.0 collective-permute-start.9
  6.1 0.0 copy-start
  6.1 2.8 %copy-done = bf16[224,14336]{1,0:T(8,128)(2,1)S(1)} copy-done((bf16[224,14336]{1,0:T(8,128)(2,1)S(1)}, bf16[224,14336]{1,0:T(8,128)(2,1)}, u32[]{:S(2)}) %copy-start) | copy-done | bytes 6422552
  8.9 0.6 shard_map.76.basis_ref
  9.5 0.0 collective-permute-done.10.two_ref
  9.5 0.6 collective-permute-done.11.three_ref
  10.2 0.0 collective-permute-done.9.one_ref
  10.2 0.0 copy-done.2
  10.2 3.1 %shard_map.77 = (f32[4,8,224,128]{3,2,1,0:T(8,128)S(1)}, bf16[4,8,224,128]{3,2,1,0:T(8,128)(2,1)S(1)}, s32[4]{0:T(128)S(1)}) custom-call(s32[2,4]{1,0:T(2,128)S(1)} %bitcast.31, bf16[224,14336]{1,0:T(8,128)(2,1)S(1)} %shard_map.76.basis_ref, bf16[224,128]{1,0:T(8,128)(2,1)S(1)} %get-tuple-element.65.own_ref, ...), custom_call_target="tpu_custom_call" | custom-call | tf_op jit(solution)/shard_map/pallas_call | solution.py:96
  13.3 1.7 %collective-permute-start.12 = (bf16[4,8,224,128]{3,2,1,0:T(8,128)(2,1)S(1)}, bf16[4,8,224,128]{3,2,1,0:T(8,128)(2,1)S(1)}, u32[]{:S(2)}, u32[]{:S(2)}) collective-permute-start(bf16[4,8,224,128]{3,2,1,0:T(8,128)(2,1)S(1)} %get-tuple-element.45), channel_id=1, source_target_pairs={{0,1},{1,0},{2,3},{3,2},{4,5},{5,4},{6,7},{7,6},{8,9},{9,8},{10,11... | collective-permute-start | bytes 5505032 | tf_op jit(solution)/shard_map/ppermute | solution.py:167
  15.0 3.4 %collective-permute-done.12 = bf16[4,8,224,128]{3,2,1,0:T(8,128)(2,1)S(1)} collective-permute-done((bf16[4,8,224,128]{3,2,1,0:T(8,128)(2,1)S(1)}, bf16[4,8,224,128]{3,2,1,0:T(8,128)(2,1)S(1)}, u32[]{:S(2)}, u32[]{:S(2)}) %collective-permute-start.12) | collective-permute-done | bytes 1835040 | tf_op jit(solution)/shard_map/ppermute | solution.py:167
  18.4 1.8 %add_convert_fusion = f16[4,8,224,128]{3,2,1,0:T(8,128)(2,1)} fusion(f32[4,8,224,128]{3,2,1,0:T(8,128)S(1)} %get-tuple-element.44, bf16[4,8,224,128]{3,2,1,0:T(8,128)(2,1)S(1)} %collective-permute-done.12), kind=kLoop, calls=%fused_computation.1 | loop fusion | flops 2752512 | bytes 7340032 | tf_op jit(solution)/shard_map/convert_element_type | solution.py:203
  20.2 0.0 copy-start.3
  20.2 11.3 %all-to-all-start = ((f16[4,8,224,128]{3,2,1,0:T(8,128)(2,1)}), f16[4,8,224,128]{3,2,1,0:T(8,128)(2,1)S(1)}, u32[]{:S(2)}, u32[]{:S(2)}) async-start(f16[4,8,224,128]{3,2,1,0:T(8,128)(2,1)} %add_convert_fusion), calls=%async_computation | async-start | bytes 3670016 | tf_op jit(solution)/shard_map/all_to_all | solution.py:163
  31.6 0.6 fusion.5
  34.7 0.0 copy-done.3
  34.8 0.9 dynamic-slice_bitcast_fusion.1
  35.7 5.1 %conditional.3 = (f32[224,256]{1,0:T(8,128)}) conditional(s32[]{:T(128)} %bitcast.4, f32[224,256]{1,0:T(8,128)S(1)} %pad_maximum_fusion, f32[224,256]{1,0:T(8,128)S(1)} %pad_maximum_fusion, f32[224,256]{1,0:T(8,128)S(1)} %pad_maximum_fusion), branch_computations={%region_0.0_spmd, %region_1.0_spmd, %region_2.0_spmd} | conditional | bytes 917552 | solution.py:179
  35.7 1.0 collective-permute-start
  36.7 4.1 %collective-permute-done = f32[224,256]{1,0:T(8,128)} collective-permute-done((f32[224,256]{1,0:T(8,128)S(1)}, f32[224,256]{1,0:T(8,128)}, u32[]{:S(2)}, u32[]{:S(2)}) %collective-permute-start) | collective-permute-done | bytes 229408 | tf_op jit(solution)/shard_map/cond/branch_0_fun/ppermute | solution.py:171
  40.8 1.0 slice_select_fusion
  41.8 1.0 all-to-all-done
  42.8 0.3 convert_reduce_fusion
  43.1 0.0 copy-start.4
  43.1 0.8 convert_element_type.21
  44.0 4.4 %all-to-all-start.1 = ((f16[8,224,128]{2,1,0:T(8,128)(2,1)}), f16[8,224,128]{2,1,0:T(8,128)(2,1)S(1)}, u32[]{:S(2)}, u32[]{:S(2)}) async-start(f16[8,224,128]{2,1,0:T(8,128)(2,1)} %convert_element_type.21), calls=%async_computation.1 | async-start | bytes 917504 | tf_op jit(solution)/shard_map/all_to_all | solution.py:163
  48.3 0.1 copy.11
  48.4 0.0 copy-done.4
  48.4 0.9 copy.12
  49.4 14.3 %all-to-all-done.1 = f16[8,224,128]{2,1,0:T(8,128)(2,1)S(1)} async-done(((f16[8,224,128]{2,1,0:T(8,128)(2,1)}), f16[8,224,128]{2,1,0:T(8,128)(2,1)S(1)}, u32[]{:S(2)}, u32[]{:S(2)}) %all-to-all-start.1) | async-done | bytes 458784 | tf_op jit(solution)/shard_map/all_to_all | solution.py:163
  63.7 0.1 convert_reduce_fusion.1
  63.8 0.7 fusion.2
  64.5 0.8 broadcast_in_dim.26
  65.3 3.5 %all-to-all-start.2 = ((bf16[8,224,128]{2,1,0:T(8,128)(2,1)}), bf16[8,224,128]{2,1,0:T(8,128)(2,1)S(1)}, u32[]{:S(2)}, u32[]{:S(2)}) async-start(bf16[8,224,128]{2,1,0:T(8,128)(2,1)} %broadcast_in_dim.26), calls=%async_computation.2 | async-start | bytes 917504 | tf_op jit(solution)/shard_map/all_to_all | solution.py:163
  68.8 3.9 %conditional.4 = (f32[224,128]{1,0:T(8,128)}) conditional(s32[]{:T(128)} %bitcast.4, f32[224,128]{1,0:T(8,128)S(1)} %get-tuple-element.61, f32[224,128]{1,0:T(8,128)S(1)} %get-tuple-element.61, f32[224,128]{1,0:T(8,128)S(1)} %get-tuple-element.61), branch_computations={%region_5.6_spmd, %region_6.7_spmd, %region_7.8_spmd} | conditional | bytes 458800 | solution.py:179
  68.8 1.0 collective-permute-start.3
  69.8 2.9 %collective-permute-done.3 = f32[224,128]{1,0:T(8,128)} collective-permute-done((f32[224,128]{1,0:T(8,128)S(1)}, f32[224,128]{1,0:T(8,128)}, u32[]{:S(2)}, u32[]{:S(2)}) %collective-permute-start.3) | collective-permute-done | bytes 114720 | tf_op jit(solution)/shard_map/cond/branch_0_fun/ppermute | solution.py:171
  72.7 0.9 fusion.1
  73.6 10.4 %all-to-all-done.2 = bf16[8,224,128]{2,1,0:T(8,128)(2,1)S(1)} async-done(((bf16[8,224,128]{2,1,0:T(8,128)(2,1)}), bf16[8,224,128]{2,1,0:T(8,128)(2,1)S(1)}, u32[]{:S(2)}, u32[]{:S(2)}) %all-to-all-start.2) | async-done | bytes 458784 | tf_op jit(solution)/shard_map/all_to_all | solution.py:163
  84.0 1.5 %broadcast_in_dim.27 = bf16[4,8,224,128]{3,2,1,0:T(8,128)(2,1)} broadcast(bf16[8,224,128]{2,1,0:T(8,128)(2,1)S(1)} %all-to-all-done.2), dimensions={1,2,3} | broadcast | bytes 2293760 | tf_op jit(solution)/shard_map/broadcast_in_dim | solution.py:220
  85.5 6.1 %all-to-all-start.3 = ((bf16[4,8,224,128]{3,2,1,0:T(8,128)(2,1)}), bf16[4,8,224,128]{3,2,1,0:T(8,128)(2,1)S(1)}, u32[]{:S(2)}, u32[]{:S(2)}) async-start(bf16[4,8,224,128]{3,2,1,0:T(8,128)(2,1)} %broadcast_in_dim.27), calls=%async_computation.3 | async-start | bytes 3670016 | tf_op jit(solution)/shard_map/all_to_all | solution.py:163
  92.2 1.6 %select_dynamic-update-slice_fusion = (f32[224,1024]{1,0:T(8,128)S(1)}, f32[224,1024]{1,0:T(8,128)}) fusion(f32[224,1024]{1,0:T(8,128)S(1)} %get-tuple-element.56, s32[]{:T(128)S(6)} %select_n.59, f32[224,128]{1,0:T(8,128)S(1)} %get-tuple-element.52, pred[]{:T(512)} %bitcast.2, f32[224,1024]{1,0:T(8,128)} %get-tuple-element.58, ...), kind=kLoop, calls=%fused_computation.14 | loop fusion | flops 57344 | bytes 688644 | tf_op jit(solution)/shard_map/dynamic_update_slice | solution.py:226
  93.8 0.0 copy-start.5
  93.8 9.0 %all-to-all-done.3.own_ref = bf16[4,8,224,128]{3,2,1,0:T(8,128)(2,1)S(1)} async-done(((bf16[4,8,224,128]{3,2,1,0:T(8,128)(2,1)}), bf16[4,8,224,128]{3,2,1,0:T(8,128)(2,1)S(1)}, u32[]{:S(2)}, u32[]{:S(2)}) %all-to-all-start.3) | async-done | bytes 1835040 | tf_op jit(solution)/shard_map/all_to_all | solution.py:163
  102.8 0.6 collective-permute-start.13
  103.4 0.0 copy-start.1
  103.4 2.8 %copy-done.1 = bf16[224,14336]{1,0:T(8,128)(2,1)S(1)} copy-done((bf16[224,14336]{1,0:T(8,128)(2,1)S(1)}, bf16[224,14336]{1,0:T(8,128)(2,1)}, u32[]{:S(2)}) %copy-start.1) | copy-done | bytes 6422552
  106.2 0.6 shard_map.78.basis_ref
  106.8 0.0 copy-done.5
  106.9 0.0 collective-permute-done.13.other_ref
  106.9 1.9 %shard_map.79 = f32[224,128]{1,0:T(8,128)S(1)} custom-call(bf16[224,14336]{1,0:T(8,128)(2,1)S(1)} %shard_map.78.basis_ref, bf16[4,8,224,128]{3,2,1,0:T(8,128)(2,1)S(1)} %all-to-all-done.3.own_ref, bf16[4,8,224,128]{3,2,1,0:T(8,128)(2,1)S(1)} %collective-permute-done.13.other_ref), custom_call_target="tpu_custom_call" | custom-call | tf_op jit(solution)/shard_map/pallas_call | solution.py:135
  108.8 4.6 %conditional.5 = (f32[224,128]{1,0:T(8,128)}) conditional(s32[]{:T(128)} %bitcast.4, f32[224,128]{1,0:T(8,128)S(1)} %shard_map.79, f32[224,128]{1,0:T(8,128)S(1)} %shard_map.79, f32[224,128]{1,0:T(8,128)S(1)} %shard_map.79), branch_computations={%region_8.9_spmd, %region_9.10_spmd, %region_10.11_spmd} | conditional | bytes 458800 | solution.py:179
  108.8 1.0 collective-permute-start.6
  109.7 3.7 %collective-permute-done.6 = f32[224,128]{1,0:T(8,128)} collective-permute-done((f32[224,128]{1,0:T(8,128)S(1)}, f32[224,128]{1,0:T(8,128)}, u32[]{:S(2)}, u32[]{:S(2)}) %collective-permute-start.6) | collective-permute-done | bytes 114720 | tf_op jit(solution)/shard_map/cond/branch_0_fun/ppermute | solution.py:171
  113.4 1.6 %fusion = f32[256,224]{0,1:T(8,128)} fusion(f32[224,128]{1,0:T(8,128)} %get-tuple-element.74, f32[224,128]{1,0:T(8,128)S(1)} %shard_map.79, pred[256]{0:T(512)(128)(4,1)S(1)} %compare_select_fusion), kind=kLoop, calls=%fused_computation.5 | loop fusion | flops 114688 | bytes 459008 | tf_op jit(solution)/shard_map/transpose | solution.py:238
  (3 shorter events, 0.0 us)
Async XLA Ops:
  1.5 8.7 %copy-start.2 = (s32[4,2]{0,1:T(2,128)S(1)}, s32[4,2]{0,1:T(2,128)}, u32[]{:S(2)}) copy-start(s32[4,2]{0,1:T(2,128)} %param.18) | copy-start | bytes 100
  1.5 8.0 %collective-permute-start.10 = (bf16[224,128]{1,0:T(8,128)(2,1)S(1)}, bf16[224,128]{1,0:T(8,128)(2,1)S(1)}, u32[]{:S(2)}, u32[]{:S(2)}) collective-permute-start(bf16[224,128]{1,0:T(8,128)(2,1)S(1)} %get-tuple-element.64), channel_id=1, source_target_pairs={{0,128},{64,192},{128,0},{192,64},{1,129},{65,193},{129,1},{193,65... | collective-permute-start | bytes 172040 | tf_op jit(solution)/shard_map/ppermute | solution.py:171
  5.3 4.9 %collective-permute-start.11 = (bf16[224,128]{1,0:T(8,128)(2,1)S(1)}, bf16[224,128]{1,0:T(8,128)(2,1)S(1)}, u32[]{:S(2)}, u32[]{:S(2)}) collective-permute-start(bf16[224,128]{1,0:T(8,128)(2,1)S(1)} %get-tuple-element.64), channel_id=1, source_target_pairs={{0,192},{64,128},{128,64},{192,0},{1,193},{65,129},{129,65},{193,1... | collective-permute-start | bytes 172040 | tf_op jit(solution)/shard_map/ppermute | solution.py:171
  6.1 4.1 %collective-permute-start.9 = (bf16[224,128]{1,0:T(8,128)(2,1)S(1)}, bf16[224,128]{1,0:T(8,128)(2,1)S(1)}, u32[]{:S(2)}, u32[]{:S(2)}) collective-permute-start(bf16[224,128]{1,0:T(8,128)(2,1)S(1)} %get-tuple-element.64), channel_id=1, source_target_pairs={{0,64},{64,0},{128,192},{192,128},{1,65},{65,1},{129,193},{193,129... | collective-permute-start | bytes 172040 | tf_op jit(solution)/shard_map/ppermute | solution.py:171
  6.1 2.8 %copy-start = (bf16[224,14336]{1,0:T(8,128)(2,1)S(1)}, bf16[224,14336]{1,0:T(8,128)(2,1)}, u32[]{:S(2)}) copy-start(bf16[224,14336]{1,0:T(8,128)(2,1)} %basis_ref.2) | copy-start | bytes 19267588
  13.3 5.1 %collective-permute-start.12 = (bf16[4,8,224,128]{3,2,1,0:T(8,128)(2,1)S(1)}, bf16[4,8,224,128]{3,2,1,0:T(8,128)(2,1)S(1)}, u32[]{:S(2)}, u32[]{:S(2)}) collective-permute-start(bf16[4,8,224,128]{3,2,1,0:T(8,128)(2,1)S(1)} %get-tuple-element.45), channel_id=1, source_target_pairs={{0,1},{1,0},{2,3},{3,2},{4,5},{5,4},{6,7},{7,6},{8,9},{9,8},{10,11... | collective-permute-start | bytes 5505032 | tf_op jit(solution)/shard_map/ppermute | solution.py:167
  20.2 14.5 %copy-start.3 = (f32[1024,224]{0,1:T(8,128)S(1)}, f32[1024,224]{0,1:T(8,128)}, u32[]{:S(2)}) copy-start(f32[1024,224]{0,1:T(8,128)} %param.16) | copy-start | bytes 2752516
  20.2 22.6 %all-to-all-start = ((f16[4,8,224,128]{3,2,1,0:T(8,128)(2,1)}), f16[4,8,224,128]{3,2,1,0:T(8,128)(2,1)S(1)}, u32[]{:S(2)}, u32[]{:S(2)}) async-start(f16[4,8,224,128]{3,2,1,0:T(8,128)(2,1)} %add_convert_fusion), calls=%async_computation | async-start | bytes 3670016 | tf_op jit(solution)/shard_map/all_to_all | solution.py:163
  35.7 5.1 %collective-permute-start = (f32[224,256]{1,0:T(8,128)S(1)}, f32[224,256]{1,0:T(8,128)}, u32[]{:S(2)}, u32[]{:S(2)}) collective-permute-start(f32[224,256]{1,0:T(8,128)S(1)} %param), channel_id=1, source_target_pairs={{0,64},{64,0},{128,192},{192,128},{1,65},{65,1},{129,193},{193,129... | collective-permute-start | bytes 688136 | tf_op jit(solution)/shard_map/cond/branch_0_fun/ppermute | solution.py:171
  43.1 5.3 %copy-start.4 = (f32[1024,224]{0,1:T(8,128)S(1)}, f32[1024,224]{0,1:T(8,128)}, u32[]{:S(2)}) copy-start(f32[1024,224]{0,1:T(8,128)} %param.15) | copy-start | bytes 2752516
  44.0 19.8 %all-to-all-start.1 = ((f16[8,224,128]{2,1,0:T(8,128)(2,1)}), f16[8,224,128]{2,1,0:T(8,128)(2,1)S(1)}, u32[]{:S(2)}, u32[]{:S(2)}) async-start(f16[8,224,128]{2,1,0:T(8,128)(2,1)} %convert_element_type.21), calls=%async_computation.1 | async-start | bytes 917504 | tf_op jit(solution)/shard_map/all_to_all | solution.py:163
  65.3 18.7 %all-to-all-start.2 = ((bf16[8,224,128]{2,1,0:T(8,128)(2,1)}), bf16[8,224,128]{2,1,0:T(8,128)(2,1)S(1)}, u32[]{:S(2)}, u32[]{:S(2)}) async-start(bf16[8,224,128]{2,1,0:T(8,128)(2,1)} %broadcast_in_dim.26), calls=%async_computation.2 | async-start | bytes 917504 | tf_op jit(solution)/shard_map/all_to_all | solution.py:163
  68.8 3.8 %collective-permute-start.3 = (f32[224,128]{1,0:T(8,128)S(1)}, f32[224,128]{1,0:T(8,128)}, u32[]{:S(2)}, u32[]{:S(2)}) collective-permute-start(f32[224,128]{1,0:T(8,128)S(1)} %param.3), channel_id=1, source_target_pairs={{0,64},{64,0},{128,192},{192,128},{1,65},{65,1},{129,193},{193,129... | collective-permute-start | bytes 344072 | tf_op jit(solution)/shard_map/cond/branch_0_fun/ppermute | solution.py:171
  85.5 17.3 %all-to-all-start.3 = ((bf16[4,8,224,128]{3,2,1,0:T(8,128)(2,1)}), bf16[4,8,224,128]{3,2,1,0:T(8,128)(2,1)S(1)}, u32[]{:S(2)}, u32[]{:S(2)}) async-start(bf16[4,8,224,128]{3,2,1,0:T(8,128)(2,1)} %broadcast_in_dim.27), calls=%async_computation.3 | async-start | bytes 3670016 | tf_op jit(solution)/shard_map/all_to_all | solution.py:163
  93.8 13.0 %copy-start.5 = (f32[224,1024]{1,0:T(8,128)}, f32[224,1024]{1,0:T(8,128)S(1)}, u32[]{:S(2)}) copy-start(f32[224,1024]{1,0:T(8,128)S(1)} %get-tuple-element.55) | copy-start | bytes 2752516
  102.8 4.0 %collective-permute-start.13 = (bf16[4,8,224,128]{3,2,1,0:T(8,128)(2,1)S(1)}, bf16[4,8,224,128]{3,2,1,0:T(8,128)(2,1)S(1)}, u32[]{:S(2)}, u32[]{:S(2)}) collective-permute-start(bf16[4,8,224,128]{3,2,1,0:T(8,128)(2,1)S(1)} %all-to-all-done.3.own_ref), channel_id=1, source_target_pairs={{0,1},{1,0},{2,3},{3,2},{4,5},{5,4},{6,7},{7,6},{8,9},{9,8},{10,11... | collective-permute-start | bytes 5505032 | tf_op jit(solution)/shard_map/ppermute | solution.py:167
  103.4 2.8 %copy-start.1 = (bf16[224,14336]{1,0:T(8,128)(2,1)S(1)}, bf16[224,14336]{1,0:T(8,128)(2,1)}, u32[]{:S(2)}) copy-start(bf16[224,14336]{1,0:T(8,128)(2,1)} %basis_ref.2) | copy-start | bytes 19267588
  108.8 4.6 %collective-permute-start.6 = (f32[224,128]{1,0:T(8,128)S(1)}, f32[224,128]{1,0:T(8,128)}, u32[]{:S(2)}, u32[]{:S(2)}) collective-permute-start(f32[224,128]{1,0:T(8,128)S(1)} %param.6), channel_id=1, source_target_pairs={{0,64},{64,0},{128,192},{192,128},{1,65},{65,1},{129,193},{193,129... | collective-permute-start | bytes 344072 | tf_op jit(solution)/shard_map/cond/branch_0_fun/ppermute | solution.py:171

commit v3 on v2

--- a/solution.py
+++ b/solution.py
@@ -39,7 +39,7 @@
     return jnp.where(
         zero + live_slots(ids_ref, 1) == 2,
         1,
-        jnp.where(zero + live_slots(ids_ref, 2) == 2, 2, 3),
+        jnp.where(zero + live_slots(ids_ref, 3) == 2, 3, 2),
     )
 
 
@@ -65,8 +65,9 @@
 
 
 def rotate_kernel(
-    ids_ref, basis_ref, own_ref, one_ref, two_ref, three_ref, keep_ref, send_ref, roles_ref
+    ids_ref, basis_ref, own_ref, one_ref, two_ref, three_ref, roles_ref, *refs
 ):
+    keep_refs, send_refs, (keep_ref, send_ref) = refs[:NEAR], refs[NEAR : 2 * NEAR], refs[2 * NEAR :]
     width = own_ref.shape[0]
     cols = 2 * CORES * width
     me = lax.axis_index("vocab")
@@ -76,6 +77,7 @@
     lent = pick(match, [one_ref[...], two_ref[...], three_ref[...]])
     rows = jnp.where(count == 0, lent, own_ref[...]) * jnp.bfloat16(SCALE)
     mine = lax.rem(lax.axis_index("hidden"), CORES) == 0
+    members = [near_member(core) for core in range(CORES)]
 
     for i in range(XS * ZS // 2):
         at = pl.ds(i * cols, cols)
@@ -84,26 +86,31 @@
         ).reshape(2, CORES, width, BLK)
         for j in range(2):
             even, odd = part[j, 0], part[j, 1]
-            to_even, to_odd = (place(2 * i + j, core) for core in range(CORES))
+            to_even, to_odd = (
+                (place(2 * i + j, core)[0] ^ members[core], place(2 * i + j, core)[1])
+                for core in range(CORES)
+            )
             keep_at = [jnp.where(mine, a, b) for a, b in zip(to_even, to_odd)]
             send_at = [jnp.where(mine, b, a) for a, b in zip(to_even, to_odd)]
             keep_ref[keep_at[0], keep_at[1]] = jnp.where(mine, even, odd)
             send_ref[send_at[0], send_at[1]] = jnp.where(mine, odd, even).astype(bf16)
+    for turn in range(NEAR):
+        keep_refs[turn][...] = keep_ref[turn]
+        send_refs[turn][...] = send_ref[turn]
 
 
 def rotate_partials(ids, basis, own, lent):
-    shape = (NEAR, FAR, own.shape[0], BLK)
-    return pl.pallas_call(
+    shape = (FAR, own.shape[0], BLK)
+    out = pl.pallas_call(
         rotate_kernel,
         in_specs=[smem] + [vmem] * 5,
-        out_specs=[vmem, vmem, smem],
-        out_shape=[
-            jax.ShapeDtypeStruct(shape, f32),
-            jax.ShapeDtypeStruct(shape, bf16),
-            jax.ShapeDtypeStruct((4,), jnp.int32),
-        ],
+        out_specs=[smem] + [vmem] * (2 * NEAR),
+        out_shape=[jax.ShapeDtypeStruct((4,), jnp.int32)]
+        + [jax.ShapeDtypeStruct(shape, t) for t in (f32, bf16) for _ in range(NEAR)],
+        scratch_shapes=[pltpu.VMEM((NEAR,) + shape, t) for t in (f32, bf16)],
         compiler_params=params,
     )(ids, basis, own, *lent)
+    return out[0], out[1 : 1 + NEAR], out[1 + NEAR :]
 
 
 def adam_moments(rotated, old_first, old_second):
@@ -112,17 +119,20 @@
     return first, second
 
 
-def back_kernel(basis_ref, own_ref, other_ref, out_ref):
+def back_kernel(basis_ref, *refs):
+    own_refs, other_refs, out_ref, cols_ref = refs[:NEAR], refs[NEAR : 2 * NEAR], refs[-2], refs[-1]
     width = basis_ref.shape[0]
     cols = 2 * CORES * width
     mine = lax.rem(lax.axis_index("hidden"), CORES) == 0
+    for turn in range(NEAR):
+        own, other = own_refs[turn][...], other_refs[turn][...]
+        cols_ref[0, near_member(0) ^ turn] = jnp.where(mine, own, other)
+        cols_ref[1, near_member(1) ^ turn] = jnp.where(mine, other, own)
     total = jnp.zeros((width, BLK), f32)
     for i in range(XS * ZS // 2):
-        pieces = []
-        for j in range(2):
-            even, odd = (place(2 * i + j, core) for core in range(CORES))
-            pieces.append(jnp.where(mine, own_ref[even], other_ref[even]))
-            pieces.append(jnp.where(mine, other_ref[odd], own_ref[odd]))
+        pieces = [
+            cols_ref[(core,) + place(2 * i + j, core)] for j in range(2) for core in range(CORES)
+        ]
         total += jnp.dot(
             basis_ref[:, i * cols : (i + 1) * cols],
             jnp.concatenate(pieces, axis=0),
@@ -134,16 +144,23 @@
 def rotate_back(basis, own, other):
     return pl.pallas_call(
         back_kernel,
-        in_specs=[vmem] * 3,
+        in_specs=[vmem] * (1 + 2 * NEAR),
         out_specs=vmem,
         out_shape=jax.ShapeDtypeStruct((basis.shape[0], BLK), f32),
+        scratch_shapes=[pltpu.VMEM((CORES, NEAR, FAR, basis.shape[0], BLK), bf16)],
         compiler_params=params,
-    )(basis, own, other)
+    )(basis, *own, *other)
 
 
 def place(chip, core):
     x, z = (chip // ZS + core) % XS, (chip % ZS + core) % ZS
     return ((x + 1) // 2 % 2) * 2 + z % 2, (x // 2) * (ZS // 2) + z // 2
+
+
+def near_member(core):
+    at = lax.axis_index("hidden") // CORES
+    x, z = lax.rem(at // ZS + core, XS), lax.rem(lax.rem(at, ZS) + core, ZS)
+    return lax.rem((x + 1) // 2, 2) * 2 + lax.rem(z, 2)
 
 
 def groups():
@@ -163,6 +180,11 @@
     return lax.all_to_all(x, "hidden", 0, 0, axis_index_groups=members, tiled=True)
 
 
+def near_by(x, turn):
+    pairs = [(g[i], g[i ^ turn]) for g in NEAR_GROUPS for i in range(NEAR)]
+    return lax.ppermute(x, "hidden", pairs)
+
+
 def swap_cores(x):
     return lax.ppermute(x, "hidden", [(i, i ^ 1) for i in range(HIDDEN)])
 
@@ -191,23 +213,28 @@
     width = gradient.shape[0]
 
     def rows_of(table, block):
-        return lax.dynamic_slice_in_dim(table, jnp.maximum(block, 0) * BLK, BLK, 1)
+        at = (0, jnp.maximum(block, 0) * BLK)
+        return lax.dynamic_slice(table, at, (width, BLK), allow_negative_indices=False)
 
     lent_rows = swap_owners(gradient[:, BLK:])
-    keep, send, roles = rotate_partials(ids, brought_near(basis), gradient[:, :BLK], lent_rows)
+    roles, keep, send = rotate_partials(ids, brought_near(basis), gradient[:, :BLK], lent_rows)
     match, own_ids = roles[MATCH], roles[ID_0 : ID_1 + 1]
     helping, doubled = roles[COUNT] == 0, roles[COUNT] == 2
     held_first = rows_of(moment_first, own_ids[1])
     held_second = rows_of(moment_second, own_ids[1])
     held = jnp.concatenate([held_first, held_second], axis=1)
-    part = (keep + swap_cores(send).astype(f32)).astype(f16)
+    order = (3, 1, 2, 0)
+    got = {turn: swap_cores(send[turn]) for turn in order}
+    part = {turn: keep[turn] + got[turn].astype(f32) for turn in order}
+    total = part[0]
+    for turn in order[:-1]:
+        total = total + near_by(part[turn].astype(f16), turn).astype(f32)
+    part, held = together(total.astype(f16), held)
     lent = swap_with_partner(match, held)
     old_first = jnp.where(helping, lent[:, :BLK], rows_of(moment_first, own_ids[0]))
     old_second = jnp.where(helping, lent[:, BLK:], rows_of(moment_second, own_ids[0]))
 
-    part = all_to_all(part, NEAR_GROUPS)
-    part, old_first, old_second = together(part, old_first, old_second)
-    part = all_to_all(jnp.sum(part.astype(f32), axis=0).astype(f16), FAR_GROUPS)
+    part = all_to_all(part, FAR_GROUPS)
     rotated = jnp.sum(part.astype(f32), axis=0) * (1.0 / SCALE)
 
     first, second = adam_moments(rotated, old_first, old_second)
@@ -215,24 +242,27 @@
     gathered = all_to_all(jnp.broadcast_to(direction[None], (FAR, width, BLK)), FAR_GROUPS)
     other_rotated = swap_with_partner(match, rotated)
     first_1, second_1 = adam_moments(other_rotated, held_first, held_second)
-    gathered, first_1, second_1, basis = together(gathered, first_1, second_1, basis)
+    gathered, first, second, first_1, second_1, basis = together(
+        gathered, first, second, first_1, second_1, basis
+    )
     basis = brought_near(basis)
-    gathered = jnp.broadcast_to(gathered[None], (NEAR, FAR, width, BLK))
-    gathered = all_to_all(gathered, NEAR_GROUPS)
+    own = [gathered] + [near_by(gathered, turn) for turn in range(1, NEAR)]
 
     def written(table, slot_0, slot_1):
         for block, live, new in ((own_ids[0], ~helping, slot_0), (own_ids[1], doubled, slot_1)):
             new = jnp.where(live, new, rows_of(table, block))
-            table = lax.dynamic_update_slice_in_dim(table, new, jnp.maximum(block, 0) * BLK, 1)
+            at = (0, jnp.maximum(block, 0) * BLK)
+            table = lax.dynamic_update_slice(table, new, at, allow_negative_indices=False)
         return table
 
     new_first = written(moment_first, first, first_1)
     new_second = written(moment_second, second, second_1)
-    gathered, new_first, new_second = together(gathered, new_first, new_second)
-
-    update = rotate_back(basis, gathered, swap_cores(gathered))
-    lent_update = swap_with_partner(match, update)
-    update = jnp.concatenate([update, lent_update], axis=1)
+    own[-1], new_first, new_second, basis = together(own[-1], new_first, new_second, basis)
+    other = [swap_cores(x) for x in own]
+
+    update = rotate_back(basis, own, other)
+    lent_update = swap_with_partner(match, update.astype(f16))
+    update = jnp.concatenate([update, lent_update.astype(f32)], axis=1)
     second_half = lax.broadcasted_iota(jnp.int32, update.shape, 1) >= BLK
     update = jnp.where(jnp.where(second_half, doubled, ~helping), update, 0.0)
     return (update.T, new_first.T, new_second.T)

time: 116 us -> 104 us (0.90)
  waiting for transfers between devices: 49.4 us -> 37.7 us
  local copies, waits for them, and re-layouts: 11.4 us -> 9 us
  Pallas kernels: 6.25 us -> 7.97 us
    all_to_all x4 -> x2, waiting for transfers between devices: 34.8 us -> 14.1 us  [all_to_all(): lax.all_to_all(x, 'hidden', 0, 0, axis_index_groups=members, tiled=True)]
    all_to_all x4 -> x2, starting transfers between devices: 25.2 us -> 9.25 us  [all_to_all(): lax.all_to_all(x, 'hidden', 0, 0, axis_index_groups=members, tiled=True)]
    ppermute x0 -> x6, starting transfers between devices: none -> 14.3 us  [near_by(): return lax.ppermute(x, 'hidden', pairs)]
    ppermute x0 -> x6, waiting for transfers between devices: none -> 10.8 us  [near_by(): return lax.ppermute(x, 'hidden', pairs)]
    ppermute x2 -> x8, starting transfers between devices: 2.24 us -> 4.97 us  [swap_cores(): return lax.ppermute(x, 'hidden', [(i, i ^ 1) for i in range(HIDDEN)])]
    pallas_call x2, Pallas kernels: 5.05 us -> 6.76 us  [the longest x1 3.73 us: rotate_partials(): pl.pallas_call(rotate_kernel, in_specs=[smem] + [vmem] * 5, out_specs=[sm...]
    broadcast_in_dim x1 -> x0, local copies, waits for them, and re-layouts: 1.52 us -> none  [shards(): gathered = jnp.broadcast_to(gathered[None], (NEAR, FAR, width, BLK))]
    ppermute x2 -> x8, waiting for transfers between devices: 3.41 us -> 2.27 us  [swap_cores(): return lax.ppermute(x, 'hidden', [(i, i ^ 1) for i in range(HIDDEN)])]
  transfers between devices with their start and end apart: 12 -> 22, of which waited for: 9 -> 13; matrix products, arithmetic and copies ran while one was open for 5% -> 6% of each run, Pallas kernels for 1% -> 1%
where the time goes in v3:
time: 104 us; the launch traced here: 103 us
  waiting for transfers between devices  37.7 us (36%)
  starting transfers between devices  36.1 us (35%)
  local copies, waits for them, and re-layouts  9 us (9%)
  other arithmetic  8.01 us (8%)
  Pallas kernels  7.97 us (8%)
  between operations  4.08 us (4%)
    ppermute x6, starting transfers between devices, near_by(): return lax.ppermute(x, 'hidden', pairs)  14.3 us
    all_to_all x2, waiting for transfers between devices, all_to_all(): lax.all_to_all(x, 'hidden', 0, 0, axis_index_groups=members, tiled=True)  14.1 us
    ppermute x6, waiting for transfers between devices, near_by(): return lax.ppermute(x, 'hidden', pairs)  10.8 us
    ppermute x6, waiting for transfers between devices, swap_owners_by(): return lax.ppermute(x, 'vocab', [(i, i ^ k) for i in range(OWNERS)])  10.5 us
    all_to_all x2, starting transfers between devices, all_to_all(): lax.all_to_all(x, 'hidden', 0, 0, axis_index_groups=members, tiled=True)  9.25 us
    ppermute x6, starting transfers between devices, swap_owners_by(): return lax.ppermute(x, 'vocab', [(i, i ^ k) for i in range(OWNERS)])  7.58 us
    unnamed x16, local copies, waits for them, and re-layouts  6.67 us
    ppermute x8, starting transfers between devices, swap_cores(): return lax.ppermute(x, 'hidden', [(i, i ^ 1) for i in range(HIDDEN)])  4.97 us
  transfers between devices with their start and end apart: 22, of which 13 were waited for; matrix products, arithmetic and copies ran while one was open for 6% of the time, Pallas kernels for 1%

profile of v3, /device:TPU:1, one launch (start us, length us, event | category | flops | bytes accessed | tf_op | source)
XLA Modules:
  0.0 102.8 jit_solution(11575739243098830722)
XLA Ops:
  0.6 0.9 fusion.10
  1.5 3.8 %collective-permute-start.10 = (bf16[224,128]{1,0:T(8,128)(2,1)S(1)}, bf16[224,128]{1,0:T(8,128)(2,1)S(1)}, u32[]{:S(2)}, u32[]{:S(2)}) collective-permute-start(bf16[224,128]{1,0:T(8,128)(2,1)S(1)} %get-tuple-element.84), channel_id=1, source_target_pairs={{0,128},{64,192},{128,0},{192,64},{1,129},{65,193},{129,1},{193,65... | collective-permute-start | bytes 172040 | tf_op jit(solution)/shard_map/ppermute | solution.py:193
  5.3 0.8 collective-permute-start.11
  6.1 0.0 collective-permute-start.9
  6.1 2.8 %copy-done = bf16[224,14336]{1,0:T(8,128)(2,1)S(1)} copy-done((bf16[224,14336]{1,0:T(8,128)(2,1)S(1)}, bf16[224,14336]{1,0:T(8,128)(2,1)}, u32[]{:S(2)}) %copy-start) | copy-done | bytes 6422552
  8.9 0.6 shard_map.76.basis_ref
  9.5 0.0 copy-start.4
  9.6 0.0 copy-start.3
  9.6 0.0 collective-permute-done.10.two_ref
  9.6 0.6 collective-permute-done.11.three_ref
  10.2 0.0 collective-permute-done.9.one_ref
  10.2 3.7 %shard_map.77 = (s32[4]{0:T(128)S(1)}, f32[8,224,128]{2,1,0:T(8,128)S(1)}, f32[8,224,128]{2,1,0:T(8,128)S(1)}, f32[8,224,128]{2,1,0:T(8,128)S(1)}, f32[8,224,128...) custom-call(s32[2,4]{1,0:T(2,128)S(1)} %bitcast.33, ...), custom_call_target="tpu_custom_call" | custom-call | tf_op jit(solution)/shard_map/pallas_call | solution.py:104
  13.9 1.7 %collective-permute-start.13 = (bf16[8,224,128]{2,1,0:T(8,128)(2,1)S(1)}, bf16[8,224,128]{2,1,0:T(8,128)(2,1)S(1)}, u32[]{:S(2)}, u32[]{:S(2)}) collective-permute-start(bf16[8,224,128]{2,1,0:T(8,128)(2,1)S(1)} %get-tuple-element.61), channel_id=1, source_target_pairs={{0,1},{1,0},{2,3},{3,2},{4,5},{5,4},{6,7},{7,6},{8,9},{9,8},{10,11... | collective-permute-start | bytes 1376264 | tf_op jit(solution)/shard_map/ppermute | solution.py:189
  15.6 0.1 collective-permute-start.15
  15.7 0.4 collective-permute-start.17
  16.2 0.1 collective-permute-start.12
  16.3 0.8 collective-permute-done.13
  17.1 0.1 add_convert_fusion.3
  17.2 7.7 %collective-permute-start.14 = (f16[8,224,128]{2,1,0:T(8,128)(2,1)S(1)}, f16[8,224,128]{2,1,0:T(8,128)(2,1)S(1)}, u32[]{:S(2)}, u32[]{:S(2)}) collective-permute-start(f16[8,224,128]{2,1,0:T(8,128)(2,1)S(1)} %add_convert_fusion.3), channel_id=1, source_target_pairs={{0,18},{2,16},{16,2},{18,0},{4,22},{6,20},{20,6},{22,4},{8,26},{10... | collective-permute-start | bytes 1376264 | tf_op jit(solution)/shard_map/ppermute | solution.py:185
  24.9 0.1 add_convert_fusion.2
  25.1 0.1 collective-permute-start.16
  25.2 0.1 add_convert_fusion.1
  25.3 0.8 collective-permute-start.18
  26.1 0.6 fusion.11
  27.4 3.5 %collective-permute-done.14 = f16[8,224,128]{2,1,0:T(8,128)(2,1)S(1)} collective-permute-done((f16[8,224,128]{2,1,0:T(8,128)(2,1)S(1)}, f16[8,224,128]{2,1,0:T(8,128)(2,1)S(1)}, u32[]{:S(2)}, u32[]{:S(2)}) %collective-permute-start.14) | collective-permute-done | bytes 458784 | tf_op jit(solution)/shard_map/ppermute | solution.py:185
  30.9 4.4 %collective-permute-done.16 = f16[8,224,128]{2,1,0:T(8,128)(2,1)S(1)} collective-permute-done((f16[8,224,128]{2,1,0:T(8,128)(2,1)S(1)}, f16[8,224,128]{2,1,0:T(8,128)(2,1)S(1)}, u32[]{:S(2)}, u32[]{:S(2)}) %collective-permute-start.16) | collective-permute-done | bytes 458784 | tf_op jit(solution)/shard_map/ppermute | solution.py:185
  35.3 0.4 collective-permute-done.18
  35.7 1.1 %add_convert_fusion = f16[8,224,128]{2,1,0:T(8,128)(2,1)} fusion(f16[8,224,128]{2,1,0:T(8,128)(2,1)S(1)} %collective-permute-done.18, f16[8,224,128]{2,1,0:T(8,128)(2,1)S(1)} %collective-permute-done.16, f16[8,224,128]{2,1,0:T(8,128)(2,1)S(1)} %collective-permute-done.14, f32[8,224,128]{2,1,0:T(8,128)S(1)} %get-tuple-element.58, ...), kind=kLoop, calls=%fused_computation.1 | loop fusion | flops 2064384 | bytes 3211264 | tf_op jit(solution)/shard_map/convert_element_type | solution.py:232
  36.8 5.3 %all-to-all-start = ((f16[8,224,128]{2,1,0:T(8,128)(2,1)}), f16[8,224,128]{2,1,0:T(8,128)(2,1)S(1)}, u32[]{:S(2)}, u32[]{:S(2)}) async-start(f16[8,224,128]{2,1,0:T(8,128)(2,1)} %add_convert_fusion), calls=%async_computation | async-start | bytes 917504 | tf_op jit(solution)/shard_map/all_to_all | solution.py:180
  44.0 5.9 %conditional.6 = (f32[224,256]{1,0:T(8,128)}) conditional(s32[]{:T(128)} %bitcast.4, f32[224,256]{1,0:T(8,128)S(1)} %pad_maximum_fusion, f32[224,256]{1,0:T(8,128)S(1)} %pad_maximum_fusion, f32[224,256]{1,0:T(8,128)S(1)} %pad_maximum_fusion), branch_computations={%region_0.0_spmd, %region_1.0_spmd, %region_2.0_spmd} | conditional | bytes 917552 | solution.py:201
  44.1 1.0 collective-permute-start
  45.1 4.8 %collective-permute-done = f32[224,256]{1,0:T(8,128)} collective-permute-done((f32[224,256]{1,0:T(8,128)S(1)}, f32[224,256]{1,0:T(8,128)}, u32[]{:S(2)}, u32[]{:S(2)}) %collective-permute-start) | collective-permute-done | bytes 229408 | tf_op jit(solution)/shard_map/cond/branch_0_fun/ppermute | solution.py:193
  49.9 7.0 %all-to-all-done = f16[8,224,128]{2,1,0:T(8,128)(2,1)S(1)} async-done(((f16[8,224,128]{2,1,0:T(8,128)(2,1)}), f16[8,224,128]{2,1,0:T(8,128)(2,1)S(1)}, u32[]{:S(2)}, u32[]{:S(2)}) %all-to-all-start) | async-done | bytes 458784 | tf_op jit(solution)/shard_map/all_to_all | solution.py:180
  56.9 0.1 convert_reduce_fusion
  57.0 1.1 %divide_convert_fusion = (bf16[224,128]{1,0:T(8,128)(2,1)S(1)}, f32[224,128]{1,0:T(8,128)S(1)}, f32[224,128]{1,0:T(8,128)S(1)}, f32[224,128]{1,0:T(8,128)S(1)}) fusion(f32[224,128]{1,0:T(8,128)S(1)} %convert_reduce_fusion, f32[1024,224]{0,1:T(8,128)S(1)} %copy-done.4, s32[]{:T(128)} %bitcast.8, f32[224,256]{1,0:T(8,128)} %get-tuple-element.92, pred[]{:T(512)} %bitcast.3, ...), kind=kLoop, calls=%fused_computation.23 | loop fusion | flops 372736 | bytes 974853 | tf_op jit(solution)/shard_map/convert_element_type | solution.py:241
  58.0 0.8 broadcast_in_dim.20
  58.9 3.9 %all-to-all-start.1 = ((bf16[8,224,128]{2,1,0:T(8,128)(2,1)}), bf16[8,224,128]{2,1,0:T(8,128)(2,1)S(1)}, u32[]{:S(2)}, u32[]{:S(2)}) async-start(bf16[8,224,128]{2,1,0:T(8,128)(2,1)} %broadcast_in_dim.20), calls=%async_computation.1 | async-start | bytes 917504 | tf_op jit(solution)/shard_map/all_to_all | solution.py:180
  62.8 0.9 copy.15
  63.7 0.1 copy.14
  64.4 3.9 %conditional.7 = (f32[224,128]{1,0:T(8,128)}) conditional(s32[]{:T(128)} %bitcast.4, f32[224,128]{1,0:T(8,128)S(1)} %get-tuple-element.83, f32[224,128]{1,0:T(8,128)S(1)} %get-tuple-element.83, f32[224,128]{1,0:T(8,128)S(1)} %get-tuple-element.83), branch_computations={%region_4.5_spmd, %region_5.6_spmd, %region_6.7_spmd} | conditional | bytes 458800 | solution.py:201
  64.5 1.0 collective-permute-start.3
  65.5 2.8 %collective-permute-done.3 = f32[224,128]{1,0:T(8,128)} collective-permute-done((f32[224,128]{1,0:T(8,128)S(1)}, f32[224,128]{1,0:T(8,128)}, u32[]{:S(2)}, u32[]{:S(2)}) %collective-permute-start.3) | collective-permute-done | bytes 114720 | tf_op jit(solution)/shard_map/cond/branch_0_fun/ppermute | solution.py:193
  68.3 1.6 %fusion.1 = (f32[224,128]{1,0:T(8,128)S(1)}, f32[224,128]{1,0:T(8,128)}) fusion(f32[224,128]{1,0:T(8,128)} %get-tuple-element.93, f32[1024,224]{0,1:T(8,128)S(1)} %copy-done.3, s32[]{:T(128)} %bitcast.5, f32[1024,224]{0,1:T(8,128)S(1)} %copy-done.4), kind=kLoop, calls=%fused_computation.9 | loop fusion | flops 200704 | bytes 573444 | tf_op jit(solution)/shard_map/add | solution.py:118
  69.9 7.1 %all-to-all-done.1.refs_0_ = bf16[8,224,128]{2,1,0:T(8,128)(2,1)S(1)} async-done(((bf16[8,224,128]{2,1,0:T(8,128)(2,1)}), bf16[8,224,128]{2,1,0:T(8,128)(2,1)S(1)}, u32[]{:S(2)}, u32[]{:S(2)}) %all-to-all-start.1) | async-done | bytes 458784 | tf_op jit(solution)/shard_map/all_to_all | solution.py:180
  77.0 3.1 %collective-permute-start.19 = (bf16[8,224,128]{2,1,0:T(8,128)(2,1)S(1)}, bf16[8,224,128]{2,1,0:T(8,128)(2,1)S(1)}, u32[]{:S(2)}, u32[]{:S(2)}) collective-permute-start(bf16[8,224,128]{2,1,0:T(8,128)(2,1)S(1)} %all-to-all-done.1.refs_0_), channel_id=1, source_target_pairs={{0,18},{2,16},{16,2},{18,0},{4,22},{6,20},{20,6},{22,4},{8,26},{10... | collective-permute-start | bytes 1376264 | tf_op jit(solution)/shard_map/ppermute | solution.py:185
  80.1 0.6 collective-permute-start.20
  80.6 2.0 %collective-permute-start.21 = (bf16[8,224,128]{2,1,0:T(8,128)(2,1)S(1)}, bf16[8,224,128]{2,1,0:T(8,128)(2,1)S(1)}, u32[]{:S(2)}, u32[]{:S(2)}) collective-permute-start(bf16[8,224,128]{2,1,0:T(8,128)(2,1)S(1)} %all-to-all-done.1.refs_0_), channel_id=1, source_target_pairs={{0,16},{2,18},{16,0},{18,2},{4,20},{6,22},{20,4},{22,6},{8,24},{10... | collective-permute-start | bytes 1376264 | tf_op jit(solution)/shard_map/ppermute | solution.py:185
  82.6 0.1 collective-permute-start.22
  82.7 2.8 %copy-done.1 = bf16[224,14336]{1,0:T(8,128)(2,1)S(1)} copy-done((bf16[224,14336]{1,0:T(8,128)(2,1)S(1)}, bf16[224,14336]{1,0:T(8,128)(2,1)}, u32[]{:S(2)}) %copy-start.1) | copy-done | bytes 6422552
  85.5 0.6 shard_map.78.basis_ref
  86.2 0.7 fusion.7
  86.9 1.6 %select_dynamic-update-slice_fusion = (f32[224,1024]{1,0:T(8,128)S(1)}, f32[224,1024]{1,0:T(8,128)}) fusion(f32[224,1024]{1,0:T(8,128)S(1)} %fusion.6, s32[]{:T(128)} %bitcast.5, f32[224,128]{1,0:T(8,128)S(1)} %get-tuple-element.72, pred[]{:T(512)} %bitcast.2, f32[224,1024]{1,0:T(8,128)} %fusion.7, f32[224,128]{1,0:T(8,128)S(1)} %copy-done.6), kind=kLoop, calls=%fused_computation.20 | loop fusion | flops 57344 | bytes 689152 | tf_op jit(solution)/shard_map/dynamic_update_slice | solution.py:255
  88.5 0.4 collective-permute-start.25
  88.9 2.5 %collective-permute-done.20.refs_1_ = bf16[8,224,128]{2,1,0:T(8,128)(2,1)S(1)} collective-permute-done((bf16[8,224,128]{2,1,0:T(8,128)(2,1)S(1)}, bf16[8,224,128]{2,1,0:T(8,128)(2,1)S(1)}, u32[]{:S(2)}, u32[]{:S(2)}) %collective-permute-start.20) | collective-permute-done | bytes 458784 | tf_op jit(solution)/shard_map/ppermute | solution.py:185
  91.4 1.3 %collective-permute-start.23 = (bf16[8,224,128]{2,1,0:T(8,128)(2,1)S(1)}, bf16[8,224,128]{2,1,0:T(8,128)(2,1)S(1)}, u32[]{:S(2)}, u32[]{:S(2)}) collective-permute-start(bf16[8,224,128]{2,1,0:T(8,128)(2,1)S(1)} %collective-permute-done.20.refs_1_), channel_id=1, source_target_pairs={{0,1},{1,0},{2,3},{3,2},{4,5},{5,4},{6,7},{7,6},{8,9},{9,8},{10,11... | collective-permute-start | bytes 1376264 | tf_op jit(solution)/shard_map/ppermute | solution.py:189
  92.7 0.8 collective-permute-start.24
  93.5 0.6 collective-permute-done.23.refs_5_
  94.1 0.8 collective-permute-done.24.refs_6_
  95.0 3.0 %shard_map.79 = f32[224,128]{1,0:T(8,128)S(1)} custom-call(bf16[224,14336]{1,0:T(8,128)(2,1)S(1)} %shard_map.78.basis_ref, bf16[8,224,128]{2,1,0:T(8,128)(2,1)S(1)} %all-to-all-done.1.refs_0_, bf16[8,224,128]{2,1,0:T(8,128)(2,1)S(1)} %collective-permute-done.20.refs_1_, bf16[8,224,128]{2,1,0:T(8,128)(2,1)S(1)} %collective-permute-done.21.refs_2_, ...), custom_call_target="tpu_custom_call" | custom-call | tf_op jit(solution)/shard_map/pallas_call | solution.py:145
  98.0 3.2 %conditional.8 = (f16[224,128]{1,0:T(8,128)(2,1)}) conditional(s32[]{:T(128)} %bitcast.4, f16[224,128]{1,0:T(8,128)(2,1)S(1)} %convert_element_type.75, f16[224,128]{1,0:T(8,128)(2,1)S(1)} %convert_element_type.75, f16[224,128]{1,0:T(8,128)(2,1)S(1)} %convert_element_type.75), branch_computations={%region_7.8_spmd, %region_8.9_spmd, %region_9.10_spmd} | conditional | bytes 229424
  98.0 1.0 collective-permute-start.6
  99.0 2.2 %collective-permute-done.6 = f16[224,128]{1,0:T(8,128)(2,1)} collective-permute-done((f16[224,128]{1,0:T(8,128)(2,1)S(1)}, f16[224,128]{1,0:T(8,128)(2,1)}, u32[]{:S(2)}, u32[]{:S(2)}) %collective-permute-start.6) | collective-permute-done | bytes 57376 | tf_op jit(solution)/shard_map/cond/branch_0_fun/ppermute | solution.py:193
  101.3 0.8 convert_element_type.76
  102.1 0.7 fusion
  (23 shorter events, 0.1 us)
Async XLA Ops:
  1.5 8.7 %copy-start.2 = (s32[4,2]{0,1:T(2,128)S(1)}, s32[4,2]{0,1:T(2,128)}, u32[]{:S(2)}) copy-start(s32[4,2]{0,1:T(2,128)} %param.18) | copy-start | bytes 100
  1.5 8.1 %collective-permute-start.10 = (bf16[224,128]{1,0:T(8,128)(2,1)S(1)}, bf16[224,128]{1,0:T(8,128)(2,1)S(1)}, u32[]{:S(2)}, u32[]{:S(2)}) collective-permute-start(bf16[224,128]{1,0:T(8,128)(2,1)S(1)} %get-tuple-element.84), channel_id=1, source_target_pairs={{0,128},{64,192},{128,0},{192,64},{1,129},{65,193},{129,1},{193,65... | collective-permute-start | bytes 172040 | tf_op jit(solution)/shard_map/ppermute | solution.py:193
  5.3 4.9 %collective-permute-start.11 = (bf16[224,128]{1,0:T(8,128)(2,1)S(1)}, bf16[224,128]{1,0:T(8,128)(2,1)S(1)}, u32[]{:S(2)}, u32[]{:S(2)}) collective-permute-start(bf16[224,128]{1,0:T(8,128)(2,1)S(1)} %get-tuple-element.84), channel_id=1, source_target_pairs={{0,192},{64,128},{128,64},{192,0},{1,193},{65,129},{129,65},{193,1... | collective-permute-start | bytes 172040 | tf_op jit(solution)/shard_map/ppermute | solution.py:193
  6.1 4.1 %collective-permute-start.9 = (bf16[224,128]{1,0:T(8,128)(2,1)S(1)}, bf16[224,128]{1,0:T(8,128)(2,1)S(1)}, u32[]{:S(2)}, u32[]{:S(2)}) collective-permute-start(bf16[224,128]{1,0:T(8,128)(2,1)S(1)} %get-tuple-element.84), channel_id=1, source_target_pairs={{0,64},{64,0},{128,192},{192,128},{1,65},{65,1},{129,193},{193,129... | collective-permute-start | bytes 172040 | tf_op jit(solution)/shard_map/ppermute | solution.py:193
  6.1 2.8 %copy-start = (bf16[224,14336]{1,0:T(8,128)(2,1)S(1)}, bf16[224,14336]{1,0:T(8,128)(2,1)}, u32[]{:S(2)}) copy-start(bf16[224,14336]{1,0:T(8,128)(2,1)} %basis_ref.2) | copy-start | bytes 19267588
  9.5 17.8 %copy-start.4 = (f32[1024,224]{0,1:T(8,128)S(1)}, f32[1024,224]{0,1:T(8,128)}, u32[]{:S(2)}) copy-start(f32[1024,224]{0,1:T(8,128)} %param.16) | copy-start | bytes 2752516
  9.6 17.8 %copy-start.3 = (f32[1024,224]{0,1:T(8,128)S(1)}, f32[1024,224]{0,1:T(8,128)}, u32[]{:S(2)}) copy-start(f32[1024,224]{0,1:T(8,128)} %param.15) | copy-start | bytes 2752516
  13.9 3.2 %collective-permute-start.13 = (bf16[8,224,128]{2,1,0:T(8,128)(2,1)S(1)}, bf16[8,224,128]{2,1,0:T(8,128)(2,1)S(1)}, u32[]{:S(2)}, u32[]{:S(2)}) collective-permute-start(bf16[8,224,128]{2,1,0:T(8,128)(2,1)S(1)} %get-tuple-element.61), channel_id=1, source_target_pairs={{0,1},{1,0},{2,3},{3,2},{4,5},{5,4},{6,7},{7,6},{8,9},{9,8},{10,11... | collective-permute-start | bytes 1376264 | tf_op jit(solution)/shard_map/ppermute | solution.py:189
  15.6 9.3 %collective-permute-start.15 = (bf16[8,224,128]{2,1,0:T(8,128)(2,1)S(1)}, bf16[8,224,128]{2,1,0:T(8,128)(2,1)S(1)}, u32[]{:S(2)}, u32[]{:S(2)}) collective-permute-start(bf16[8,224,128]{2,1,0:T(8,128)(2,1)S(1)} %get-tuple-element.63), channel_id=1, source_target_pairs={{0,1},{1,0},{2,3},{3,2},{4,5},{5,4},{6,7},{7,6},{8,9},{9,8},{10,11... | collective-permute-start | bytes 1376264 | tf_op jit(solution)/shard_map/ppermute | solution.py:189
  15.7 9.4 %collective-permute-start.17 = (bf16[8,224,128]{2,1,0:T(8,128)(2,1)S(1)}, bf16[8,224,128]{2,1,0:T(8,128)(2,1)S(1)}, u32[]{:S(2)}, u32[]{:S(2)}) collective-permute-start(bf16[8,224,128]{2,1,0:T(8,128)(2,1)S(1)} %get-tuple-element.65), channel_id=1, source_target_pairs={{0,1},{1,0},{2,3},{3,2},{4,5},{5,4},{6,7},{7,6},{8,9},{9,8},{10,11... | collective-permute-start | bytes 1376264 | tf_op jit(solution)/shard_map/ppermute | solution.py:189
  16.2 11.3 %collective-permute-start.12 = (bf16[8,224,128]{2,1,0:T(8,128)(2,1)S(1)}, bf16[8,224,128]{2,1,0:T(8,128)(2,1)S(1)}, u32[]{:S(2)}, u32[]{:S(2)}) collective-permute-start(bf16[8,224,128]{2,1,0:T(8,128)(2,1)S(1)} %get-tuple-element.59), channel_id=1, source_target_pairs={{0,1},{1,0},{2,3},{3,2},{4,5},{5,4},{6,7},{7,6},{8,9},{9,8},{10,11... | collective-permute-start | bytes 1376264 | tf_op jit(solution)/shard_map/ppermute | solution.py:189
  17.2 13.7 %collective-permute-start.14 = (f16[8,224,128]{2,1,0:T(8,128)(2,1)S(1)}, f16[8,224,128]{2,1,0:T(8,128)(2,1)S(1)}, u32[]{:S(2)}, u32[]{:S(2)}) collective-permute-start(f16[8,224,128]{2,1,0:T(8,128)(2,1)S(1)} %add_convert_fusion.3), channel_id=1, source_target_pairs={{0,18},{2,16},{16,2},{18,0},{4,22},{6,20},{20,6},{22,4},{8,26},{10... | collective-permute-start | bytes 1376264 | tf_op jit(solution)/shard_map/ppermute | solution.py:185
  25.1 10.3 %collective-permute-start.16 = (f16[8,224,128]{2,1,0:T(8,128)(2,1)S(1)}, f16[8,224,128]{2,1,0:T(8,128)(2,1)S(1)}, u32[]{:S(2)}, u32[]{:S(2)}) collective-permute-start(f16[8,224,128]{2,1,0:T(8,128)(2,1)S(1)} %add_convert_fusion.2), channel_id=1, source_target_pairs={{0,2},{2,0},{16,18},{18,16},{4,6},{6,4},{20,22},{22,20},{8,10},{10... | collective-permute-start | bytes 1376264 | tf_op jit(solution)/shard_map/ppermute | solution.py:185
  25.3 10.4 %collective-permute-start.18 = (f16[8,224,128]{2,1,0:T(8,128)(2,1)S(1)}, f16[8,224,128]{2,1,0:T(8,128)(2,1)S(1)}, u32[]{:S(2)}, u32[]{:S(2)}) collective-permute-start(f16[8,224,128]{2,1,0:T(8,128)(2,1)S(1)} %add_convert_fusion.1), channel_id=1, source_target_pairs={{0,16},{2,18},{16,0},{18,2},{4,20},{6,22},{20,4},{22,6},{8,24},{10... | collective-permute-start | bytes 1376264 | tf_op jit(solution)/shard_map/ppermute | solution.py:185
  36.8 20.1 %all-to-all-start = ((f16[8,224,128]{2,1,0:T(8,128)(2,1)}), f16[8,224,128]{2,1,0:T(8,128)(2,1)S(1)}, u32[]{:S(2)}, u32[]{:S(2)}) async-start(f16[8,224,128]{2,1,0:T(8,128)(2,1)} %add_convert_fusion), calls=%async_computation | async-start | bytes 917504 | tf_op jit(solution)/shard_map/all_to_all | solution.py:180
  44.1 5.8 %collective-permute-start = (f32[224,256]{1,0:T(8,128)S(1)}, f32[224,256]{1,0:T(8,128)}, u32[]{:S(2)}, u32[]{:S(2)}) collective-permute-start(f32[224,256]{1,0:T(8,128)S(1)} %param), channel_id=1, source_target_pairs={{0,64},{64,0},{128,192},{192,128},{1,65},{65,1},{129,193},{193,129... | collective-permute-start | bytes 688136 | tf_op jit(solution)/shard_map/cond/branch_0_fun/ppermute | solution.py:193
  58.9 18.1 %all-to-all-start.1 = ((bf16[8,224,128]{2,1,0:T(8,128)(2,1)}), bf16[8,224,128]{2,1,0:T(8,128)(2,1)S(1)}, u32[]{:S(2)}, u32[]{:S(2)}) async-start(bf16[8,224,128]{2,1,0:T(8,128)(2,1)} %broadcast_in_dim.20), calls=%async_computation.1 | async-start | bytes 917504 | tf_op jit(solution)/shard_map/all_to_all | solution.py:180
  64.5 3.8 %collective-permute-start.3 = (f32[224,128]{1,0:T(8,128)S(1)}, f32[224,128]{1,0:T(8,128)}, u32[]{:S(2)}, u32[]{:S(2)}) collective-permute-start(f32[224,128]{1,0:T(8,128)S(1)} %param.3), channel_id=1, source_target_pairs={{0,64},{64,0},{128,192},{192,128},{1,65},{65,1},{129,193},{193,129... | collective-permute-start | bytes 344072 | tf_op jit(solution)/shard_map/cond/branch_0_fun/ppermute | solution.py:193
  77.0 11.5 %collective-permute-start.19 = (bf16[8,224,128]{2,1,0:T(8,128)(2,1)S(1)}, bf16[8,224,128]{2,1,0:T(8,128)(2,1)S(1)}, u32[]{:S(2)}, u32[]{:S(2)}) collective-permute-start(bf16[8,224,128]{2,1,0:T(8,128)(2,1)S(1)} %all-to-all-done.1.refs_0_), channel_id=1, source_target_pairs={{0,18},{2,16},{16,2},{18,0},{4,22},{6,20},{20,6},{22,4},{8,26},{10... | collective-permute-start | bytes 1376264 | tf_op jit(solution)/shard_map/ppermute | solution.py:185
  80.1 11.3 %collective-permute-start.20 = (bf16[8,224,128]{2,1,0:T(8,128)(2,1)S(1)}, bf16[8,224,128]{2,1,0:T(8,128)(2,1)S(1)}, u32[]{:S(2)}, u32[]{:S(2)}) collective-permute-start(bf16[8,224,128]{2,1,0:T(8,128)(2,1)S(1)} %all-to-all-done.1.refs_0_), channel_id=1, source_target_pairs={{0,2},{2,0},{16,18},{18,16},{4,6},{6,4},{20,22},{22,20},{8,10},{10... | collective-permute-start | bytes 1376264 | tf_op jit(solution)/shard_map/ppermute | solution.py:185
  80.6 12.1 %collective-permute-start.21 = (bf16[8,224,128]{2,1,0:T(8,128)(2,1)S(1)}, bf16[8,224,128]{2,1,0:T(8,128)(2,1)S(1)}, u32[]{:S(2)}, u32[]{:S(2)}) collective-permute-start(bf16[8,224,128]{2,1,0:T(8,128)(2,1)S(1)} %all-to-all-done.1.refs_0_), channel_id=1, source_target_pairs={{0,16},{2,18},{16,0},{18,2},{4,20},{6,22},{20,4},{22,6},{8,24},{10... | collective-permute-start | bytes 1376264 | tf_op jit(solution)/shard_map/ppermute | solution.py:185
  82.6 10.9 %collective-permute-start.22 = (bf16[8,224,128]{2,1,0:T(8,128)(2,1)S(1)}, bf16[8,224,128]{2,1,0:T(8,128)(2,1)S(1)}, u32[]{:S(2)}, u32[]{:S(2)}) collective-permute-start(bf16[8,224,128]{2,1,0:T(8,128)(2,1)S(1)} %all-to-all-done.1.refs_0_), channel_id=1, source_target_pairs={{0,1},{1,0},{2,3},{3,2},{4,5},{5,4},{6,7},{7,6},{8,9},{9,8},{10,11... | collective-permute-start | bytes 1376264 | tf_op jit(solution)/shard_map/ppermute | solution.py:189
  82.7 2.8 %copy-start.1 = (bf16[224,14336]{1,0:T(8,128)(2,1)S(1)}, bf16[224,14336]{1,0:T(8,128)(2,1)}, u32[]{:S(2)}) copy-start(bf16[224,14336]{1,0:T(8,128)(2,1)} %basis_ref.2) | copy-start | bytes 19267588
  85.5 1.3 %copy-start.6 = (f32[224,128]{1,0:T(8,128)S(1)}, f32[224,128]{1,0:T(8,128)}, u32[]{:S(2)}) copy-start(f32[224,128]{1,0:T(8,128)} %get-tuple-element.70) | copy-start | bytes 344068
  88.5 14.3 %copy-start.5 = (f32[224,1024]{1,0:T(8,128)}, f32[224,1024]{1,0:T(8,128)S(1)}, u32[]{:S(2)}) copy-start(f32[224,1024]{1,0:T(8,128)S(1)} %get-tuple-element.77) | copy-start | bytes 2752516
  88.5 5.1 %collective-permute-start.25 = (bf16[8,224,128]{2,1,0:T(8,128)(2,1)S(1)}, bf16[8,224,128]{2,1,0:T(8,128)(2,1)S(1)}, u32[]{:S(2)}, u32[]{:S(2)}) collective-permute-start(bf16[8,224,128]{2,1,0:T(8,128)(2,1)S(1)} %collective-permute-done.19.refs_3_), channel_id=1, source_target_pairs={{0,1},{1,0},{2,3},{3,2},{4,5},{5,4},{6,7},{7,6},{8,9},{9,8},{10,11... | collective-permute-start | bytes 1376264 | tf_op jit(solution)/shard_map/ppermute | solution.py:189
  91.4 2.7 %collective-permute-start.23 = (bf16[8,224,128]{2,1,0:T(8,128)(2,1)S(1)}, bf16[8,224,128]{2,1,0:T(8,128)(2,1)S(1)}, u32[]{:S(2)}, u32[]{:S(2)}) collective-permute-start(bf16[8,224,128]{2,1,0:T(8,128)(2,1)S(1)} %collective-permute-done.20.refs_1_), channel_id=1, source_target_pairs={{0,1},{1,0},{2,3},{3,2},{4,5},{5,4},{6,7},{7,6},{8,9},{9,8},{10,11... | collective-permute-start | bytes 1376264 | tf_op jit(solution)/shard_map/ppermute | solution.py:189
  92.7 2.3 %collective-permute-start.24 = (bf16[8,224,128]{2,1,0:T(8,128)(2,1)S(1)}, bf16[8,224,128]{2,1,0:T(8,128)(2,1)S(1)}, u32[]{:S(2)}, u32[]{:S(2)}) collective-permute-start(bf16[8,224,128]{2,1,0:T(8,128)(2,1)S(1)} %collective-permute-done.21.refs_2_), channel_id=1, source_target_pairs={{0,1},{1,0},{2,3},{3,2},{4,5},{5,4},{6,7},{7,6},{8,9},{9,8},{10,11... | collective-permute-start | bytes 1376264 | tf_op jit(solution)/shard_map/ppermute | solution.py:189
  98.0 3.2 %collective-permute-start.6 = (f16[224,128]{1,0:T(8,128)(2,1)S(1)}, f16[224,128]{1,0:T(8,128)(2,1)}, u32[]{:S(2)}, u32[]{:S(2)}) collective-permute-start(f16[224,128]{1,0:T(8,128)(2,1)S(1)} %param.6), channel_id=1, source_target_pairs={{0,64},{64,0},{128,192},{192,128},{1,65},{65,1},{129,193},{193,129... | collective-permute-start | bytes 172040 | tf_op jit(solution)/shard_map/cond/branch_0_fun/ppermute | solution.py:193

commit v4 on v3

--- a/solution.py
+++ b/solution.py
@@ -12,9 +12,9 @@
 XS, ZS, CORES = 4, 8, 2
 HIDDEN = XS * ZS * CORES
 NEAR, FAR = 4, 8
-SCALE = 4.0
-VMEM_LIMIT = 32 * 2**20
-NEAR_LIMIT = 32 * 2**20
+NEAR_SCALE, FAR_SCALE = 128.0, 32.0
+VMEM_LIMIT = 24 * 2**20
+NEAR_LIMIT = 8 * 2**20
 
 beta_first = 0.9
 beta_second = 0.95
@@ -75,7 +75,7 @@
     roles_ref[MATCH], roles_ref[COUNT] = match, count
     roles_ref[ID_0], roles_ref[ID_1] = ids_ref[0, me], ids_ref[1, me]
     lent = pick(match, [one_ref[...], two_ref[...], three_ref[...]])
-    rows = jnp.where(count == 0, lent, own_ref[...]) * jnp.bfloat16(SCALE)
+    rows = jnp.where(count == 0, lent, own_ref[:, :BLK]) * jnp.bfloat16(NEAR_SCALE)
     mine = lax.rem(lax.axis_index("hidden"), CORES) == 0
     members = [near_member(core) for core in range(CORES)]
 
@@ -217,7 +217,7 @@
         return lax.dynamic_slice(table, at, (width, BLK), allow_negative_indices=False)
 
     lent_rows = swap_owners(gradient[:, BLK:])
-    roles, keep, send = rotate_partials(ids, brought_near(basis), gradient[:, :BLK], lent_rows)
+    roles, keep, send = rotate_partials(ids, brought_near(basis), gradient, lent_rows)
     match, own_ids = roles[MATCH], roles[ID_0 : ID_1 + 1]
     helping, doubled = roles[COUNT] == 0, roles[COUNT] == 2
     held_first = rows_of(moment_first, own_ids[1])
@@ -229,13 +229,13 @@
     total = part[0]
     for turn in order[:-1]:
         total = total + near_by(part[turn].astype(f16), turn).astype(f32)
-    part, held = together(total.astype(f16), held)
+    part, held = together((total * (FAR_SCALE / NEAR_SCALE)).astype(f16), held)
     lent = swap_with_partner(match, held)
     old_first = jnp.where(helping, lent[:, :BLK], rows_of(moment_first, own_ids[0]))
     old_second = jnp.where(helping, lent[:, BLK:], rows_of(moment_second, own_ids[0]))
 
     part = all_to_all(part, FAR_GROUPS)
-    rotated = jnp.sum(part.astype(f32), axis=0) * (1.0 / SCALE)
+    rotated = jnp.sum(part.astype(f32), axis=0) * (1.0 / FAR_SCALE)
 
     first, second = adam_moments(rotated, old_first, old_second)
     direction = (first / (jnp.sqrt(second) + epsilon)).astype(bf16)

time: 104 us -> 104 us (level)
    unnamed x16 -> x18, local copies, waits for them, and re-layouts: 6.67 us -> 6.68 us
where the time goes in v4:
time: 104 us; the launch traced here: 103 us
  waiting for transfers between devices  37.7 us (36%)
  starting transfers between devices  36 us (35%)
  local copies, waits for them, and re-layouts  9.03 us (9%)
  other arithmetic  8.04 us (8%)
  Pallas kernels  7.93 us (8%)
  between operations  4.09 us (4%)
    ppermute x6, starting transfers between devices, near_by(): return lax.ppermute(x, 'hidden', pairs)  14.3 us
    all_to_all x2, waiting for transfers between devices, all_to_all(): lax.all_to_all(x, 'hidden', 0, 0, axis_index_groups=members, tiled=True)  14.1 us
    ppermute x6, waiting for transfers between devices, near_by(): return lax.ppermute(x, 'hidden', pairs)  10.8 us
    ppermute x6, waiting for transfers between devices, swap_owners_by(): return lax.ppermute(x, 'vocab', [(i, i ^ k) for i in range(OWNERS)])  10.5 us
    all_to_all x2, starting transfers between devices, all_to_all(): lax.all_to_all(x, 'hidden', 0, 0, axis_index_groups=members, tiled=True)  9.21 us
    ppermute x6, starting transfers between devices, swap_owners_by(): return lax.ppermute(x, 'vocab', [(i, i ^ k) for i in range(OWNERS)])  7.52 us
    unnamed x18, local copies, waits for them, and re-layouts  6.68 us
    ppermute x8, starting transfers between devices, swap_cores(): return lax.ppermute(x, 'hidden', [(i, i ^ 1) for i in range(HIDDEN)])  4.97 us
  transfers between devices with their start and end apart: 22, of which 13 were waited for; matrix products, arithmetic and copies ran while one was open for 6% of the time, Pallas kernels for 1%

profile of v4, /device:TPU:1, one launch (start us, length us, event | category | flops | bytes accessed | tf_op | source)
XLA Modules:
  0.0 102.8 jit_solution(2265762686002813230)
XLA Ops:
  0.6 0.9 slice.54
  1.5 3.7 %collective-permute-start.10 = (bf16[224,128]{1,0:T(8,128)(2,1)S(1)}, bf16[224,128]{1,0:T(8,128)(2,1)S(1)}, u32[]{:S(2)}, u32[]{:S(2)}) collective-permute-start(bf16[224,128]{1,0:T(8,128)(2,1)S(1)} %slice.54), channel_id=1, source_target_pairs={{0,128},{64,192},{128,0},{192,64},{1,129},{65,193},{129,1},{193,65... | collective-permute-start | bytes 172040 | tf_op jit(solution)/shard_map/ppermute | solution.py:193
  5.3 0.8 collective-permute-start.11
  6.1 2.8 %copy-done = bf16[224,14336]{1,0:T(8,128)(2,1)S(1)} copy-done((bf16[224,14336]{1,0:T(8,128)(2,1)S(1)}, bf16[224,14336]{1,0:T(8,128)(2,1)}, u32[]{:S(2)}) %copy-start) | copy-done | bytes 6422552
  8.9 0.6 shard_map.76.basis_ref
  9.5 0.0 copy-start.5
  9.5 0.0 copy-start.4
  9.5 0.6 collective-permute-done.11.three_ref
  10.1 3.7 %shard_map.77 = (s32[4]{0:T(128)S(1)}, f32[8,224,128]{2,1,0:T(8,128)S(1)}, f32[8,224,128]{2,1,0:T(8,128)S(1)}, f32[8,224,128]{2,1,0:T(8,128)S(1)}, f32[8,224,128...) custom-call(s32[2,4]{1,0:T(2,128)S(1)} %bitcast.35, ...), custom_call_target="tpu_custom_call" | custom-call | tf_op jit(solution)/shard_map/pallas_call | solution.py:104
  13.9 1.7 %collective-permute-start.13 = (bf16[8,224,128]{2,1,0:T(8,128)(2,1)S(1)}, bf16[8,224,128]{2,1,0:T(8,128)(2,1)S(1)}, u32[]{:S(2)}, u32[]{:S(2)}) collective-permute-start(bf16[8,224,128]{2,1,0:T(8,128)(2,1)S(1)} %get-tuple-element.61), channel_id=1, source_target_pairs={{0,1},{1,0},{2,3},{3,2},{4,5},{5,4},{6,7},{7,6},{8,9},{9,8},{10,11... | collective-permute-start | bytes 1376264 | tf_op jit(solution)/shard_map/ppermute | solution.py:189
  15.6 0.1 collective-permute-start.15
  15.7 0.4 collective-permute-start.17
  16.1 0.1 collective-permute-start.12
  16.2 0.8 collective-permute-done.13
  17.0 0.1 add_convert_fusion.2
  17.1 7.7 %collective-permute-start.14 = (f16[8,224,128]{2,1,0:T(8,128)(2,1)S(1)}, f16[8,224,128]{2,1,0:T(8,128)(2,1)S(1)}, u32[]{:S(2)}, u32[]{:S(2)}) collective-permute-start(f16[8,224,128]{2,1,0:T(8,128)(2,1)S(1)} %add_convert_fusion.2), channel_id=1, source_target_pairs={{0,18},{2,16},{16,2},{18,0},{4,22},{6,20},{20,6},{22,4},{8,26},{10... | collective-permute-start | bytes 1376264 | tf_op jit(solution)/shard_map/ppermute | solution.py:185
  24.9 0.0 collective-permute-done.15
  24.9 0.1 add_convert_fusion.1
  25.0 0.1 collective-permute-start.16
  25.1 0.0 collective-permute-done.17
  25.1 0.1 add_convert_fusion
  25.2 0.8 collective-permute-start.18
  26.0 0.6 fusion.10
  27.4 0.0 collective-permute-done.12
  27.4 3.4 %collective-permute-done.14 = f16[8,224,128]{2,1,0:T(8,128)(2,1)S(1)} collective-permute-done((f16[8,224,128]{2,1,0:T(8,128)(2,1)S(1)}, f16[8,224,128]{2,1,0:T(8,128)(2,1)S(1)}, u32[]{:S(2)}, u32[]{:S(2)}) %collective-permute-start.14) | collective-permute-done | bytes 458784 | tf_op jit(solution)/shard_map/ppermute | solution.py:185
  30.8 4.4 %collective-permute-done.16 = f16[8,224,128]{2,1,0:T(8,128)(2,1)S(1)} collective-permute-done((f16[8,224,128]{2,1,0:T(8,128)(2,1)S(1)}, f16[8,224,128]{2,1,0:T(8,128)(2,1)S(1)}, u32[]{:S(2)}, u32[]{:S(2)}) %collective-permute-start.16) | collective-permute-done | bytes 458784 | tf_op jit(solution)/shard_map/ppermute | solution.py:185
  35.2 0.4 collective-permute-done.18
  35.6 1.1 %multiply_convert_fusion = f16[8,224,128]{2,1,0:T(8,128)(2,1)} fusion(f16[8,224,128]{2,1,0:T(8,128)(2,1)S(1)} %collective-permute-done.18, f16[8,224,128]{2,1,0:T(8,128)(2,1)S(1)} %collective-permute-done.16, f16[8,224,128]{2,1,0:T(8,128)(2,1)S(1)} %collective-permute-done.14, f32[8,224,128]{2,1,0:T(8,128)S(1)} %get-tuple-element.58, ...), kind=kLoop, calls=%fused_computation.1 | loop fusion | flops 2293760 | bytes 3211264 | tf_op jit(solution)/shard_map/convert_element_type | solution.py:232
  36.8 5.3 %all-to-all-start = ((f16[8,224,128]{2,1,0:T(8,128)(2,1)}), f16[8,224,128]{2,1,0:T(8,128)(2,1)S(1)}, u32[]{:S(2)}, u32[]{:S(2)}) async-start(f16[8,224,128]{2,1,0:T(8,128)(2,1)} %multiply_convert_fusion), calls=%async_computation | async-start | bytes 917504 | tf_op jit(solution)/shard_map/all_to_all | solution.py:180
  44.0 5.9 %conditional.6 = (f32[224,256]{1,0:T(8,128)}) conditional(s32[]{:T(128)} %bitcast.4, f32[224,256]{1,0:T(8,128)S(1)} %pad_maximum_fusion, f32[224,256]{1,0:T(8,128)S(1)} %pad_maximum_fusion, f32[224,256]{1,0:T(8,128)S(1)} %pad_maximum_fusion), branch_computations={%region_0.0_spmd, %region_1.0_spmd, %region_2.0_spmd} | conditional | bytes 917552 | solution.py:201
  44.0 1.0 collective-permute-start
  45.0 4.8 %collective-permute-done = f32[224,256]{1,0:T(8,128)} collective-permute-done((f32[224,256]{1,0:T(8,128)S(1)}, f32[224,256]{1,0:T(8,128)}, u32[]{:S(2)}, u32[]{:S(2)}) %collective-permute-start) | collective-permute-done | bytes 229408 | tf_op jit(solution)/shard_map/cond/branch_0_fun/ppermute | solution.py:193
  49.9 7.0 %all-to-all-done = f16[8,224,128]{2,1,0:T(8,128)(2,1)S(1)} async-done(((f16[8,224,128]{2,1,0:T(8,128)(2,1)}), f16[8,224,128]{2,1,0:T(8,128)(2,1)S(1)}, u32[]{:S(2)}, u32[]{:S(2)}) %all-to-all-start) | async-done | bytes 458784 | tf_op jit(solution)/shard_map/all_to_all | solution.py:180
  56.9 0.1 convert_reduce_fusion
  57.0 1.1 %divide_convert_fusion = (bf16[224,128]{1,0:T(8,128)(2,1)S(1)}, f32[224,128]{1,0:T(8,128)S(1)}, f32[224,128]{1,0:T(8,128)S(1)}, f32[224,128]{1,0:T(8,128)S(1)}) fusion(f32[224,128]{1,0:T(8,128)S(1)} %convert_reduce_fusion, f32[1024,224]{0,1:T(8,128)S(1)} %copy-done.5, s32[]{:T(128)} %bitcast.8, f32[224,256]{1,0:T(8,128)} %get-tuple-element.90, pred[]{:T(512)} %bitcast.3, ...), kind=kLoop, calls=%fused_computation.23 | loop fusion | flops 372736 | bytes 974853 | tf_op jit(solution)/shard_map/convert_element_type | solution.py:241
  58.0 0.8 broadcast_in_dim.20
  58.9 3.9 %all-to-all-start.1 = ((bf16[8,224,128]{2,1,0:T(8,128)(2,1)}), bf16[8,224,128]{2,1,0:T(8,128)(2,1)S(1)}, u32[]{:S(2)}, u32[]{:S(2)}) async-start(bf16[8,224,128]{2,1,0:T(8,128)(2,1)} %broadcast_in_dim.20), calls=%async_computation.1 | async-start | bytes 917504 | tf_op jit(solution)/shard_map/all_to_all | solution.py:180
  62.7 0.9 copy.15
  63.7 0.1 copy.14
  64.4 3.9 %conditional.7 = (f32[224,128]{1,0:T(8,128)}) conditional(s32[]{:T(128)} %bitcast.4, f32[224,128]{1,0:T(8,128)S(1)} %get-tuple-element.83, f32[224,128]{1,0:T(8,128)S(1)} %get-tuple-element.83, f32[224,128]{1,0:T(8,128)S(1)} %get-tuple-element.83), branch_computations={%region_4.5_spmd, %region_5.6_spmd, %region_6.7_spmd} | conditional | bytes 458800 | solution.py:201
  64.4 1.0 collective-permute-start.3
  65.4 2.8 %collective-permute-done.3 = f32[224,128]{1,0:T(8,128)} collective-permute-done((f32[224,128]{1,0:T(8,128)S(1)}, f32[224,128]{1,0:T(8,128)}, u32[]{:S(2)}, u32[]{:S(2)}) %collective-permute-start.3) | collective-permute-done | bytes 114720 | tf_op jit(solution)/shard_map/cond/branch_0_fun/ppermute | solution.py:193
  68.3 1.6 %fusion.1 = (f32[224,128]{1,0:T(8,128)S(1)}, f32[224,128]{1,0:T(8,128)}) fusion(f32[224,128]{1,0:T(8,128)} %get-tuple-element.91, f32[1024,224]{0,1:T(8,128)S(1)} %copy-done.4, s32[]{:T(128)} %bitcast.5, f32[1024,224]{0,1:T(8,128)S(1)} %copy-done.5), kind=kLoop, calls=%fused_computation.9 | loop fusion | flops 200704 | bytes 573444 | tf_op jit(solution)/shard_map/add | solution.py:118
  69.8 7.1 %all-to-all-done.1.refs_0_ = bf16[8,224,128]{2,1,0:T(8,128)(2,1)S(1)} async-done(((bf16[8,224,128]{2,1,0:T(8,128)(2,1)}), bf16[8,224,128]{2,1,0:T(8,128)(2,1)S(1)}, u32[]{:S(2)}, u32[]{:S(2)}) %all-to-all-start.1) | async-done | bytes 458784 | tf_op jit(solution)/shard_map/all_to_all | solution.py:180
  76.9 3.1 %collective-permute-start.19 = (bf16[8,224,128]{2,1,0:T(8,128)(2,1)S(1)}, bf16[8,224,128]{2,1,0:T(8,128)(2,1)S(1)}, u32[]{:S(2)}, u32[]{:S(2)}) collective-permute-start(bf16[8,224,128]{2,1,0:T(8,128)(2,1)S(1)} %all-to-all-done.1.refs_0_), channel_id=1, source_target_pairs={{0,18},{2,16},{16,2},{18,0},{4,22},{6,20},{20,6},{22,4},{8,26},{10... | collective-permute-start | bytes 1376264 | tf_op jit(solution)/shard_map/ppermute | solution.py:185
  80.0 0.6 collective-permute-start.20
  80.6 2.0 %collective-permute-start.21 = (bf16[8,224,128]{2,1,0:T(8,128)(2,1)S(1)}, bf16[8,224,128]{2,1,0:T(8,128)(2,1)S(1)}, u32[]{:S(2)}, u32[]{:S(2)}) collective-permute-start(bf16[8,224,128]{2,1,0:T(8,128)(2,1)S(1)} %all-to-all-done.1.refs_0_), channel_id=1, source_target_pairs={{0,16},{2,18},{16,0},{18,2},{4,20},{6,22},{20,4},{22,6},{8,24},{10... | collective-permute-start | bytes 1376264 | tf_op jit(solution)/shard_map/ppermute | solution.py:185
  82.6 0.1 collective-permute-start.22
  82.7 2.8 %copy-done.1 = bf16[224,14336]{1,0:T(8,128)(2,1)S(1)} copy-done((bf16[224,14336]{1,0:T(8,128)(2,1)S(1)}, bf16[224,14336]{1,0:T(8,128)(2,1)}, u32[]{:S(2)}) %copy-start.1) | copy-done | bytes 6422552
  85.5 0.6 shard_map.78.basis_ref
  86.1 0.7 fusion.7
  86.8 1.6 %select_dynamic-update-slice_fusion = (f32[224,1024]{1,0:T(8,128)S(1)}, f32[224,1024]{1,0:T(8,128)}) fusion(f32[224,1024]{1,0:T(8,128)S(1)} %fusion.6, s32[]{:T(128)} %bitcast.5, f32[224,128]{1,0:T(8,128)S(1)} %get-tuple-element.72, pred[]{:T(512)} %bitcast.2, f32[224,1024]{1,0:T(8,128)} %fusion.7, f32[224,128]{1,0:T(8,128)S(1)} %copy-done.7), kind=kLoop, calls=%fused_computation.20 | loop fusion | flops 57344 | bytes 689152 | tf_op jit(solution)/shard_map/dynamic_update_slice | solution.py:255
  88.4 0.4 collective-permute-start.25
  88.8 2.5 %collective-permute-done.20.refs_1_ = bf16[8,224,128]{2,1,0:T(8,128)(2,1)S(1)} collective-permute-done((bf16[8,224,128]{2,1,0:T(8,128)(2,1)S(1)}, bf16[8,224,128]{2,1,0:T(8,128)(2,1)S(1)}, u32[]{:S(2)}, u32[]{:S(2)}) %collective-permute-start.20) | collective-permute-done | bytes 458784 | tf_op jit(solution)/shard_map/ppermute | solution.py:185
  91.4 1.3 %collective-permute-start.23 = (bf16[8,224,128]{2,1,0:T(8,128)(2,1)S(1)}, bf16[8,224,128]{2,1,0:T(8,128)(2,1)S(1)}, u32[]{:S(2)}, u32[]{:S(2)}) collective-permute-start(bf16[8,224,128]{2,1,0:T(8,128)(2,1)S(1)} %collective-permute-done.20.refs_1_), channel_id=1, source_target_pairs={{0,1},{1,0},{2,3},{3,2},{4,5},{5,4},{6,7},{7,6},{8,9},{9,8},{10,11... | collective-permute-start | bytes 1376264 | tf_op jit(solution)/shard_map/ppermute | solution.py:189
  92.6 0.8 collective-permute-start.24
  93.5 0.6 collective-permute-done.23.refs_5_
  94.1 0.9 collective-permute-done.24.refs_6_
  94.9 3.0 %shard_map.79 = f32[224,128]{1,0:T(8,128)S(1)} custom-call(bf16[224,14336]{1,0:T(8,128)(2,1)S(1)} %shard_map.78.basis_ref, bf16[8,224,128]{2,1,0:T(8,128)(2,1)S(1)} %all-to-all-done.1.refs_0_, bf16[8,224,128]{2,1,0:T(8,128)(2,1)S(1)} %collective-permute-done.20.refs_1_, bf16[8,224,128]{2,1,0:T(8,128)(2,1)S(1)} %collective-permute-done.21.refs_2_, ...), custom_call_target="tpu_custom_call" | custom-call | tf_op jit(solution)/shard_map/pallas_call | solution.py:145
  98.0 3.2 %conditional.8 = (f16[224,128]{1,0:T(8,128)(2,1)}) conditional(s32[]{:T(128)} %bitcast.4, f16[224,128]{1,0:T(8,128)(2,1)S(1)} %convert_element_type.75, f16[224,128]{1,0:T(8,128)(2,1)S(1)} %convert_element_type.75, f16[224,128]{1,0:T(8,128)(2,1)S(1)} %convert_element_type.75), branch_computations={%region_7.8_spmd, %region_8.9_spmd, %region_9.10_spmd} | conditional | bytes 229424
  98.0 1.0 collective-permute-start.6
  99.0 2.2 %collective-permute-done.6 = f16[224,128]{1,0:T(8,128)(2,1)} collective-permute-done((f16[224,128]{1,0:T(8,128)(2,1)S(1)}, f16[224,128]{1,0:T(8,128)(2,1)}, u32[]{:S(2)}, u32[]{:S(2)}) %collective-permute-start.6) | collective-permute-done | bytes 57376 | tf_op jit(solution)/shard_map/cond/branch_0_fun/ppermute | solution.py:193
  101.2 0.8 convert_element_type.76
  102.1 0.7 fusion
  (25 shorter events, 0.1 us)
Async XLA Ops:
  0.6 9.5 %copy-start.3 = (s32[4,2]{0,1:T(2,128)S(1)}, s32[4,2]{0,1:T(2,128)}, u32[]{:S(2)}) copy-start(s32[4,2]{0,1:T(2,128)} %param.18) | copy-start | bytes 100
  0.6 9.5 %copy-start.2 = (bf16[256,224]{0,1:T(8,128)(2,1)S(1)}, bf16[256,224]{0,1:T(8,128)(2,1)}, u32[]{:S(2)}) copy-start(bf16[256,224]{0,1:T(8,128)(2,1)} %param.14) | copy-start | bytes 344068
  1.5 8.0 %collective-permute-start.10 = (bf16[224,128]{1,0:T(8,128)(2,1)S(1)}, bf16[224,128]{1,0:T(8,128)(2,1)S(1)}, u32[]{:S(2)}, u32[]{:S(2)}) collective-permute-start(bf16[224,128]{1,0:T(8,128)(2,1)S(1)} %slice.54), channel_id=1, source_target_pairs={{0,128},{64,192},{128,0},{192,64},{1,129},{65,193},{129,1},{193,65... | collective-permute-start | bytes 172040 | tf_op jit(solution)/shard_map/ppermute | solution.py:193
  5.3 4.9 %collective-permute-start.11 = (bf16[224,128]{1,0:T(8,128)(2,1)S(1)}, bf16[224,128]{1,0:T(8,128)(2,1)S(1)}, u32[]{:S(2)}, u32[]{:S(2)}) collective-permute-start(bf16[224,128]{1,0:T(8,128)(2,1)S(1)} %slice.54), channel_id=1, source_target_pairs={{0,192},{64,128},{128,64},{192,0},{1,193},{65,129},{129,65},{193,1... | collective-permute-start | bytes 172040 | tf_op jit(solution)/shard_map/ppermute | solution.py:193
  6.1 4.1 %collective-permute-start.9 = (bf16[224,128]{1,0:T(8,128)(2,1)S(1)}, bf16[224,128]{1,0:T(8,128)(2,1)S(1)}, u32[]{:S(2)}, u32[]{:S(2)}) collective-permute-start(bf16[224,128]{1,0:T(8,128)(2,1)S(1)} %slice.54), channel_id=1, source_target_pairs={{0,64},{64,0},{128,192},{192,128},{1,65},{65,1},{129,193},{193,129... | collective-permute-start | bytes 172040 | tf_op jit(solution)/shard_map/ppermute | solution.py:193
  6.1 2.8 %copy-start = (bf16[224,14336]{1,0:T(8,128)(2,1)S(1)}, bf16[224,14336]{1,0:T(8,128)(2,1)}, u32[]{:S(2)}) copy-start(bf16[224,14336]{1,0:T(8,128)(2,1)} %basis_ref.2) | copy-start | bytes 19267588
  9.5 17.8 %copy-start.5 = (f32[1024,224]{0,1:T(8,128)S(1)}, f32[1024,224]{0,1:T(8,128)}, u32[]{:S(2)}) copy-start(f32[1024,224]{0,1:T(8,128)} %param.16) | copy-start | bytes 2752516
  9.5 17.8 %copy-start.4 = (f32[1024,224]{0,1:T(8,128)S(1)}, f32[1024,224]{0,1:T(8,128)}, u32[]{:S(2)}) copy-start(f32[1024,224]{0,1:T(8,128)} %param.15) | copy-start | bytes 2752516
  13.9 3.2 %collective-permute-start.13 = (bf16[8,224,128]{2,1,0:T(8,128)(2,1)S(1)}, bf16[8,224,128]{2,1,0:T(8,128)(2,1)S(1)}, u32[]{:S(2)}, u32[]{:S(2)}) collective-permute-start(bf16[8,224,128]{2,1,0:T(8,128)(2,1)S(1)} %get-tuple-element.61), channel_id=1, source_target_pairs={{0,1},{1,0},{2,3},{3,2},{4,5},{5,4},{6,7},{7,6},{8,9},{9,8},{10,11... | collective-permute-start | bytes 1376264 | tf_op jit(solution)/shard_map/ppermute | solution.py:189
  15.6 9.3 %collective-permute-start.15 = (bf16[8,224,128]{2,1,0:T(8,128)(2,1)S(1)}, bf16[8,224,128]{2,1,0:T(8,128)(2,1)S(1)}, u32[]{:S(2)}, u32[]{:S(2)}) collective-permute-start(bf16[8,224,128]{2,1,0:T(8,128)(2,1)S(1)} %get-tuple-element.63), channel_id=1, source_target_pairs={{0,1},{1,0},{2,3},{3,2},{4,5},{5,4},{6,7},{7,6},{8,9},{9,8},{10,11... | collective-permute-start | bytes 1376264 | tf_op jit(solution)/shard_map/ppermute | solution.py:189
  15.7 9.4 %collective-permute-start.17 = (bf16[8,224,128]{2,1,0:T(8,128)(2,1)S(1)}, bf16[8,224,128]{2,1,0:T(8,128)(2,1)S(1)}, u32[]{:S(2)}, u32[]{:S(2)}) collective-permute-start(bf16[8,224,128]{2,1,0:T(8,128)(2,1)S(1)} %get-tuple-element.65), channel_id=1, source_target_pairs={{0,1},{1,0},{2,3},{3,2},{4,5},{5,4},{6,7},{7,6},{8,9},{9,8},{10,11... | collective-permute-start | bytes 1376264 | tf_op jit(solution)/shard_map/ppermute | solution.py:189
  16.1 11.3 %collective-permute-start.12 = (bf16[8,224,128]{2,1,0:T(8,128)(2,1)S(1)}, bf16[8,224,128]{2,1,0:T(8,128)(2,1)S(1)}, u32[]{:S(2)}, u32[]{:S(2)}) collective-permute-start(bf16[8,224,128]{2,1,0:T(8,128)(2,1)S(1)} %get-tuple-element.59), channel_id=1, source_target_pairs={{0,1},{1,0},{2,3},{3,2},{4,5},{5,4},{6,7},{7,6},{8,9},{9,8},{10,11... | collective-permute-start | bytes 1376264 | tf_op jit(solution)/shard_map/ppermute | solution.py:189
  17.1 13.7 %collective-permute-start.14 = (f16[8,224,128]{2,1,0:T(8,128)(2,1)S(1)}, f16[8,224,128]{2,1,0:T(8,128)(2,1)S(1)}, u32[]{:S(2)}, u32[]{:S(2)}) collective-permute-start(f16[8,224,128]{2,1,0:T(8,128)(2,1)S(1)} %add_convert_fusion.2), channel_id=1, source_target_pairs={{0,18},{2,16},{16,2},{18,0},{4,22},{6,20},{20,6},{22,4},{8,26},{10... | collective-permute-start | bytes 1376264 | tf_op jit(solution)/shard_map/ppermute | solution.py:185
  25.0 10.3 %collective-permute-start.16 = (f16[8,224,128]{2,1,0:T(8,128)(2,1)S(1)}, f16[8,224,128]{2,1,0:T(8,128)(2,1)S(1)}, u32[]{:S(2)}, u32[]{:S(2)}) collective-permute-start(f16[8,224,128]{2,1,0:T(8,128)(2,1)S(1)} %add_convert_fusion.1), channel_id=1, source_target_pairs={{0,2},{2,0},{16,18},{18,16},{4,6},{6,4},{20,22},{22,20},{8,10},{10... | collective-permute-start | bytes 1376264 | tf_op jit(solution)/shard_map/ppermute | solution.py:185
  25.2 10.4 %collective-permute-start.18 = (f16[8,224,128]{2,1,0:T(8,128)(2,1)S(1)}, f16[8,224,128]{2,1,0:T(8,128)(2,1)S(1)}, u32[]{:S(2)}, u32[]{:S(2)}) collective-permute-start(f16[8,224,128]{2,1,0:T(8,128)(2,1)S(1)} %add_convert_fusion), channel_id=1, source_target_pairs={{0,16},{2,18},{16,0},{18,2},{4,20},{6,22},{20,4},{22,6},{8,24},{10... | collective-permute-start | bytes 1376264 | tf_op jit(solution)/shard_map/ppermute | solution.py:185
  36.8 20.1 %all-to-all-start = ((f16[8,224,128]{2,1,0:T(8,128)(2,1)}), f16[8,224,128]{2,1,0:T(8,128)(2,1)S(1)}, u32[]{:S(2)}, u32[]{:S(2)}) async-start(f16[8,224,128]{2,1,0:T(8,128)(2,1)} %multiply_convert_fusion), calls=%async_computation | async-start | bytes 917504 | tf_op jit(solution)/shard_map/all_to_all | solution.py:180
  44.0 5.8 %collective-permute-start = (f32[224,256]{1,0:T(8,128)S(1)}, f32[224,256]{1,0:T(8,128)}, u32[]{:S(2)}, u32[]{:S(2)}) collective-permute-start(f32[224,256]{1,0:T(8,128)S(1)} %param), channel_id=1, source_target_pairs={{0,64},{64,0},{128,192},{192,128},{1,65},{65,1},{129,193},{193,129... | collective-permute-start | bytes 688136 | tf_op jit(solution)/shard_map/cond/branch_0_fun/ppermute | solution.py:193
  58.9 18.1 %all-to-all-start.1 = ((bf16[8,224,128]{2,1,0:T(8,128)(2,1)}), bf16[8,224,128]{2,1,0:T(8,128)(2,1)S(1)}, u32[]{:S(2)}, u32[]{:S(2)}) async-start(bf16[8,224,128]{2,1,0:T(8,128)(2,1)} %broadcast_in_dim.20), calls=%async_computation.1 | async-start | bytes 917504 | tf_op jit(solution)/shard_map/all_to_all | solution.py:180
  64.4 3.8 %collective-permute-start.3 = (f32[224,128]{1,0:T(8,128)S(1)}, f32[224,128]{1,0:T(8,128)}, u32[]{:S(2)}, u32[]{:S(2)}) collective-permute-start(f32[224,128]{1,0:T(8,128)S(1)} %param.3), channel_id=1, source_target_pairs={{0,64},{64,0},{128,192},{192,128},{1,65},{65,1},{129,193},{193,129... | collective-permute-start | bytes 344072 | tf_op jit(solution)/shard_map/cond/branch_0_fun/ppermute | solution.py:193
  76.9 11.5 %collective-permute-start.19 = (bf16[8,224,128]{2,1,0:T(8,128)(2,1)S(1)}, bf16[8,224,128]{2,1,0:T(8,128)(2,1)S(1)}, u32[]{:S(2)}, u32[]{:S(2)}) collective-permute-start(bf16[8,224,128]{2,1,0:T(8,128)(2,1)S(1)} %all-to-all-done.1.refs_0_), channel_id=1, source_target_pairs={{0,18},{2,16},{16,2},{18,0},{4,22},{6,20},{20,6},{22,4},{8,26},{10... | collective-permute-start | bytes 1376264 | tf_op jit(solution)/shard_map/ppermute | solution.py:185
  80.0 11.3 %collective-permute-start.20 = (bf16[8,224,128]{2,1,0:T(8,128)(2,1)S(1)}, bf16[8,224,128]{2,1,0:T(8,128)(2,1)S(1)}, u32[]{:S(2)}, u32[]{:S(2)}) collective-permute-start(bf16[8,224,128]{2,1,0:T(8,128)(2,1)S(1)} %all-to-all-done.1.refs_0_), channel_id=1, source_target_pairs={{0,2},{2,0},{16,18},{18,16},{4,6},{6,4},{20,22},{22,20},{8,10},{10... | collective-permute-start | bytes 1376264 | tf_op jit(solution)/shard_map/ppermute | solution.py:185
  80.6 12.1 %collective-permute-start.21 = (bf16[8,224,128]{2,1,0:T(8,128)(2,1)S(1)}, bf16[8,224,128]{2,1,0:T(8,128)(2,1)S(1)}, u32[]{:S(2)}, u32[]{:S(2)}) collective-permute-start(bf16[8,224,128]{2,1,0:T(8,128)(2,1)S(1)} %all-to-all-done.1.refs_0_), channel_id=1, source_target_pairs={{0,16},{2,18},{16,0},{18,2},{4,20},{6,22},{20,4},{22,6},{8,24},{10... | collective-permute-start | bytes 1376264 | tf_op jit(solution)/shard_map/ppermute | solution.py:185
  82.6 10.9 %collective-permute-start.22 = (bf16[8,224,128]{2,1,0:T(8,128)(2,1)S(1)}, bf16[8,224,128]{2,1,0:T(8,128)(2,1)S(1)}, u32[]{:S(2)}, u32[]{:S(2)}) collective-permute-start(bf16[8,224,128]{2,1,0:T(8,128)(2,1)S(1)} %all-to-all-done.1.refs_0_), channel_id=1, source_target_pairs={{0,1},{1,0},{2,3},{3,2},{4,5},{5,4},{6,7},{7,6},{8,9},{9,8},{10,11... | collective-permute-start | bytes 1376264 | tf_op jit(solution)/shard_map/ppermute | solution.py:189
  82.7 2.8 %copy-start.1 = (bf16[224,14336]{1,0:T(8,128)(2,1)S(1)}, bf16[224,14336]{1,0:T(8,128)(2,1)}, u32[]{:S(2)}) copy-start(bf16[224,14336]{1,0:T(8,128)(2,1)} %basis_ref.2) | copy-start | bytes 19267588
  85.5 1.3 %copy-start.7 = (f32[224,128]{1,0:T(8,128)S(1)}, f32[224,128]{1,0:T(8,128)}, u32[]{:S(2)}) copy-start(f32[224,128]{1,0:T(8,128)} %get-tuple-element.70) | copy-start | bytes 344068
  88.4 14.3 %copy-start.6 = (f32[224,1024]{1,0:T(8,128)}, f32[224,1024]{1,0:T(8,128)S(1)}, u32[]{:S(2)}) copy-start(f32[224,1024]{1,0:T(8,128)S(1)} %get-tuple-element.77) | copy-start | bytes 2752516
  88.4 5.1 %collective-permute-start.25 = (bf16[8,224,128]{2,1,0:T(8,128)(2,1)S(1)}, bf16[8,224,128]{2,1,0:T(8,128)(2,1)S(1)}, u32[]{:S(2)}, u32[]{:S(2)}) collective-permute-start(bf16[8,224,128]{2,1,0:T(8,128)(2,1)S(1)} %collective-permute-done.19.refs_3_), channel_id=1, source_target_pairs={{0,1},{1,0},{2,3},{3,2},{4,5},{5,4},{6,7},{7,6},{8,9},{9,8},{10,11... | collective-permute-start | bytes 1376264 | tf_op jit(solution)/shard_map/ppermute | solution.py:189
  91.4 2.7 %collective-permute-start.23 = (bf16[8,224,128]{2,1,0:T(8,128)(2,1)S(1)}, bf16[8,224,128]{2,1,0:T(8,128)(2,1)S(1)}, u32[]{:S(2)}, u32[]{:S(2)}) collective-permute-start(bf16[8,224,128]{2,1,0:T(8,128)(2,1)S(1)} %collective-permute-done.20.refs_1_), channel_id=1, source_target_pairs={{0,1},{1,0},{2,3},{3,2},{4,5},{5,4},{6,7},{7,6},{8,9},{9,8},{10,11... | collective-permute-start | bytes 1376264 | tf_op jit(solution)/shard_map/ppermute | solution.py:189
  92.6 2.3 %collective-permute-start.24 = (bf16[8,224,128]{2,1,0:T(8,128)(2,1)S(1)}, bf16[8,224,128]{2,1,0:T(8,128)(2,1)S(1)}, u32[]{:S(2)}, u32[]{:S(2)}) collective-permute-start(bf16[8,224,128]{2,1,0:T(8,128)(2,1)S(1)} %collective-permute-done.21.refs_2_), channel_id=1, source_target_pairs={{0,1},{1,0},{2,3},{3,2},{4,5},{5,4},{6,7},{7,6},{8,9},{9,8},{10,11... | collective-permute-start | bytes 1376264 | tf_op jit(solution)/shard_map/ppermute | solution.py:189
  98.0 3.2 %collective-permute-start.6 = (f16[224,128]{1,0:T(8,128)(2,1)S(1)}, f16[224,128]{1,0:T(8,128)(2,1)}, u32[]{:S(2)}, u32[]{:S(2)}) collective-permute-start(f16[224,128]{1,0:T(8,128)(2,1)S(1)} %param.6), channel_id=1, source_target_pairs={{0,64},{64,0},{128,192},{192,128},{1,65},{65,1},{129,193},{193,129... | collective-permute-start | bytes 172040 | tf_op jit(solution)/shard_map/cond/branch_0_fun/ppermute | solution.py:193

commit v5 on v4

--- a/solution.py
+++ b/solution.py
@@ -262,9 +262,14 @@
 
     update = rotate_back(basis, own, other)
     lent_update = swap_with_partner(match, update.astype(f16))
-    update = jnp.concatenate([update, lent_update.astype(f32)], axis=1)
+    update = jnp.pad(update, ((0, 0), (0, BLK)))
+    lent_update = jnp.pad(lent_update, ((0, 0), (BLK, 0)))
     second_half = lax.broadcasted_iota(jnp.int32, update.shape, 1) >= BLK
-    update = jnp.where(jnp.where(second_half, doubled, ~helping), update, 0.0)
+    update = jnp.where(
+        second_half,
+        jnp.where(doubled, lent_update.astype(f32), 0.0),
+        jnp.where(helping, 0.0, update),
+    )
     return (update.T, new_first.T, new_second.T)
 
 

time: 104 us -> 104 us (level)
  no operation moved by 1% of the time
where the time goes in v5:
time: 104 us; the launch traced here: 103 us
  waiting for transfers between devices  37.6 us (36%)
  starting transfers between devices  36 us (35%)
  local copies, waits for them, and re-layouts  9.03 us (9%)
  other arithmetic  8.02 us (8%)
  Pallas kernels  7.94 us (8%)
  between operations  4.09 us (4%)
    ppermute x6, starting transfers between devices, near_by(): return lax.ppermute(x, 'hidden', pairs)  14.3 us
    all_to_all x2, waiting for transfers between devices, all_to_all(): lax.all_to_all(x, 'hidden', 0, 0, axis_index_groups=members, tiled=True)  14.1 us
    ppermute x6, waiting for transfers between devices, near_by(): return lax.ppermute(x, 'hidden', pairs)  10.8 us
    ppermute x6, waiting for transfers between devices, swap_owners_by(): return lax.ppermute(x, 'vocab', [(i, i ^ k) for i in range(OWNERS)])  10.5 us
    all_to_all x2, starting transfers between devices, all_to_all(): lax.all_to_all(x, 'hidden', 0, 0, axis_index_groups=members, tiled=True)  9.21 us
    ppermute x6, starting transfers between devices, swap_owners_by(): return lax.ppermute(x, 'vocab', [(i, i ^ k) for i in range(OWNERS)])  7.54 us
    unnamed x18, local copies, waits for them, and re-layouts  6.68 us
    ppermute x8, starting transfers between devices, swap_cores(): return lax.ppermute(x, 'hidden', [(i, i ^ 1) for i in range(HIDDEN)])  4.97 us
  transfers between devices with their start and end apart: 22, of which 13 were waited for; matrix products, arithmetic and copies ran while one was open for 6% of the time, Pallas kernels for 1%

profile of v5, /device:TPU:1, one launch (start us, length us, event | category | flops | bytes accessed | tf_op | source)
XLA Modules:
  0.0 102.8 jit_solution(8954430495003943796)
XLA Ops:
  0.6 0.9 slice.54
  1.5 3.7 %collective-permute-start.10 = (bf16[224,128]{1,0:T(8,128)(2,1)S(1)}, bf16[224,128]{1,0:T(8,128)(2,1)S(1)}, u32[]{:S(2)}, u32[]{:S(2)}) collective-permute-start(bf16[224,128]{1,0:T(8,128)(2,1)S(1)} %slice.54), channel_id=1, source_target_pairs={{0,128},{64,192},{128,0},{192,64},{1,129},{65,193},{129,1},{193,65... | collective-permute-start | bytes 172040 | tf_op jit(solution)/shard_map/ppermute | solution.py:193
  5.3 0.8 collective-permute-start.11
  6.1 0.0 collective-permute-start.9
  6.1 2.8 %copy-done = bf16[224,14336]{1,0:T(8,128)(2,1)S(1)} copy-done((bf16[224,14336]{1,0:T(8,128)(2,1)S(1)}, bf16[224,14336]{1,0:T(8,128)(2,1)}, u32[]{:S(2)}) %copy-start) | copy-done | bytes 6422552
  8.9 0.6 shard_map.76.basis_ref
  9.5 0.0 copy-start.5
  9.5 0.0 copy-start.4
  9.5 0.0 collective-permute-done.10.two_ref
  9.5 0.6 collective-permute-done.11.three_ref
  10.1 0.0 collective-permute-done.9.one_ref
  10.1 3.7 %shard_map.77 = (s32[4]{0:T(128)S(1)}, f32[8,224,128]{2,1,0:T(8,128)S(1)}, f32[8,224,128]{2,1,0:T(8,128)S(1)}, f32[8,224,128]{2,1,0:T(8,128)S(1)}, f32[8,224,128...) custom-call(s32[2,4]{1,0:T(2,128)S(1)} %bitcast.35, ...), custom_call_target="tpu_custom_call" | custom-call | tf_op jit(solution)/shard_map/pallas_call | solution.py:104
  13.9 1.7 %collective-permute-start.13 = (bf16[8,224,128]{2,1,0:T(8,128)(2,1)S(1)}, bf16[8,224,128]{2,1,0:T(8,128)(2,1)S(1)}, u32[]{:S(2)}, u32[]{:S(2)}) collective-permute-start(bf16[8,224,128]{2,1,0:T(8,128)(2,1)S(1)} %get-tuple-element.55), channel_id=1, source_target_pairs={{0,1},{1,0},{2,3},{3,2},{4,5},{5,4},{6,7},{7,6},{8,9},{9,8},{10,11... | collective-permute-start | bytes 1376264 | tf_op jit(solution)/shard_map/ppermute | solution.py:189
  15.6 0.1 collective-permute-start.15
  15.7 0.4 collective-permute-start.17
  16.1 0.1 collective-permute-start.12
  16.2 0.8 collective-permute-done.13
  17.0 0.1 add_convert_fusion.2
  17.1 7.7 %collective-permute-start.14 = (f16[8,224,128]{2,1,0:T(8,128)(2,1)S(1)}, f16[8,224,128]{2,1,0:T(8,128)(2,1)S(1)}, u32[]{:S(2)}, u32[]{:S(2)}) collective-permute-start(f16[8,224,128]{2,1,0:T(8,128)(2,1)S(1)} %add_convert_fusion.2), channel_id=1, source_target_pairs={{0,18},{2,16},{16,2},{18,0},{4,22},{6,20},{20,6},{22,4},{8,26},{10... | collective-permute-start | bytes 1376264 | tf_op jit(solution)/shard_map/ppermute | solution.py:185
  24.9 0.1 add_convert_fusion.1
  25.0 0.1 collective-permute-start.16
  25.1 0.1 add_convert_fusion
  25.2 0.8 collective-permute-start.18
  26.0 0.6 fusion.9
  27.4 3.4 %collective-permute-done.14 = f16[8,224,128]{2,1,0:T(8,128)(2,1)S(1)} collective-permute-done((f16[8,224,128]{2,1,0:T(8,128)(2,1)S(1)}, f16[8,224,128]{2,1,0:T(8,128)(2,1)S(1)}, u32[]{:S(2)}, u32[]{:S(2)}) %collective-permute-start.14) | collective-permute-done | bytes 458784 | tf_op jit(solution)/shard_map/ppermute | solution.py:185
  30.8 4.4 %collective-permute-done.16 = f16[8,224,128]{2,1,0:T(8,128)(2,1)S(1)} collective-permute-done((f16[8,224,128]{2,1,0:T(8,128)(2,1)S(1)}, f16[8,224,128]{2,1,0:T(8,128)(2,1)S(1)}, u32[]{:S(2)}, u32[]{:S(2)}) %collective-permute-start.16) | collective-permute-done | bytes 458784 | tf_op jit(solution)/shard_map/ppermute | solution.py:185
  35.2 0.4 collective-permute-done.18
  35.6 1.1 %multiply_convert_fusion = f16[8,224,128]{2,1,0:T(8,128)(2,1)} fusion(f16[8,224,128]{2,1,0:T(8,128)(2,1)S(1)} %collective-permute-done.18, f16[8,224,128]{2,1,0:T(8,128)(2,1)S(1)} %collective-permute-done.16, f16[8,224,128]{2,1,0:T(8,128)(2,1)S(1)} %collective-permute-done.14, f32[8,224,128]{2,1,0:T(8,128)S(1)} %get-tuple-element.52, ...), kind=kLoop, calls=%fused_computation.1 | loop fusion | flops 2293760 | bytes 3211264 | tf_op jit(solution)/shard_map/convert_element_type | solution.py:232
  36.8 5.3 %all-to-all-start = ((f16[8,224,128]{2,1,0:T(8,128)(2,1)}), f16[8,224,128]{2,1,0:T(8,128)(2,1)S(1)}, u32[]{:S(2)}, u32[]{:S(2)}) async-start(f16[8,224,128]{2,1,0:T(8,128)(2,1)} %multiply_convert_fusion), calls=%async_computation | async-start | bytes 917504 | tf_op jit(solution)/shard_map/all_to_all | solution.py:180
  44.0 5.9 %conditional.3 = (f32[224,256]{1,0:T(8,128)}) conditional(s32[]{:T(128)} %bitcast.3, f32[224,256]{1,0:T(8,128)S(1)} %pad_maximum_fusion, f32[224,256]{1,0:T(8,128)S(1)} %pad_maximum_fusion, f32[224,256]{1,0:T(8,128)S(1)} %pad_maximum_fusion), branch_computations={%region_0.0_spmd, %region_1.0_spmd, %region_2.0_spmd} | conditional | bytes 917552 | solution.py:201
  44.0 1.0 collective-permute-start
  45.0 4.8 %collective-permute-done = f32[224,256]{1,0:T(8,128)} collective-permute-done((f32[224,256]{1,0:T(8,128)S(1)}, f32[224,256]{1,0:T(8,128)}, u32[]{:S(2)}, u32[]{:S(2)}) %collective-permute-start) | collective-permute-done | bytes 229408 | tf_op jit(solution)/shard_map/cond/branch_0_fun/ppermute | solution.py:193
  49.9 7.0 %all-to-all-done = f16[8,224,128]{2,1,0:T(8,128)(2,1)S(1)} async-done(((f16[8,224,128]{2,1,0:T(8,128)(2,1)}), f16[8,224,128]{2,1,0:T(8,128)(2,1)S(1)}, u32[]{:S(2)}, u32[]{:S(2)}) %all-to-all-start) | async-done | bytes 458784 | tf_op jit(solution)/shard_map/all_to_all | solution.py:180
  56.9 0.1 convert_reduce_fusion
  57.0 1.1 %divide_convert_fusion = (bf16[224,128]{1,0:T(8,128)(2,1)S(1)}, f32[224,128]{1,0:T(8,128)S(1)}, f32[224,128]{1,0:T(8,128)S(1)}, f32[224,128]{1,0:T(8,128)S(1)}) fusion(f32[224,128]{1,0:T(8,128)S(1)} %convert_reduce_fusion, f32[1024,224]{0,1:T(8,128)S(1)} %copy-done.5, s32[]{:T(128)} %bitcast.8, f32[224,256]{1,0:T(8,128)} %get-tuple-element.84, pred[]{:T(512)} %bitcast.4, ...), kind=kLoop, calls=%fused_computation.22 | loop fusion | flops 372736 | bytes 974853 | tf_op jit(solution)/shard_map/convert_element_type | solution.py:241
  58.0 0.8 broadcast_in_dim.12
  58.8 3.9 %all-to-all-start.1 = ((bf16[8,224,128]{2,1,0:T(8,128)(2,1)}), bf16[8,224,128]{2,1,0:T(8,128)(2,1)S(1)}, u32[]{:S(2)}, u32[]{:S(2)}) async-start(bf16[8,224,128]{2,1,0:T(8,128)(2,1)} %broadcast_in_dim.12), calls=%async_computation.1 | async-start | bytes 917504 | tf_op jit(solution)/shard_map/all_to_all | solution.py:180
  62.7 0.9 copy.15
  63.7 0.1 copy.14
  64.4 3.9 %conditional.4 = (f32[224,128]{1,0:T(8,128)}) conditional(s32[]{:T(128)} %bitcast.3, f32[224,128]{1,0:T(8,128)S(1)} %get-tuple-element.77, f32[224,128]{1,0:T(8,128)S(1)} %get-tuple-element.77, f32[224,128]{1,0:T(8,128)S(1)} %get-tuple-element.77), branch_computations={%region_4.5_spmd, %region_5.6_spmd, %region_6.7_spmd} | conditional | bytes 458800 | solution.py:201
  64.4 1.0 collective-permute-start.3
  65.4 2.8 %collective-permute-done.3 = f32[224,128]{1,0:T(8,128)} collective-permute-done((f32[224,128]{1,0:T(8,128)S(1)}, f32[224,128]{1,0:T(8,128)}, u32[]{:S(2)}, u32[]{:S(2)}) %collective-permute-start.3) | collective-permute-done | bytes 114720 | tf_op jit(solution)/shard_map/cond/branch_0_fun/ppermute | solution.py:193
  68.3 1.6 %fusion = (f32[224,128]{1,0:T(8,128)S(1)}, f32[224,128]{1,0:T(8,128)}) fusion(f32[224,128]{1,0:T(8,128)} %get-tuple-element.85, f32[1024,224]{0,1:T(8,128)S(1)} %copy-done.4, s32[]{:T(128)} %bitcast.5, f32[1024,224]{0,1:T(8,128)S(1)} %copy-done.5), kind=kLoop, calls=%fused_computation.8 | loop fusion | flops 200704 | bytes 573444 | tf_op jit(solution)/shard_map/add | solution.py:118
  69.8 7.1 %all-to-all-done.1.refs_0_ = bf16[8,224,128]{2,1,0:T(8,128)(2,1)S(1)} async-done(((bf16[8,224,128]{2,1,0:T(8,128)(2,1)}), bf16[8,224,128]{2,1,0:T(8,128)(2,1)S(1)}, u32[]{:S(2)}, u32[]{:S(2)}) %all-to-all-start.1) | async-done | bytes 458784 | tf_op jit(solution)/shard_map/all_to_all | solution.py:180
  76.9 3.1 %collective-permute-start.19 = (bf16[8,224,128]{2,1,0:T(8,128)(2,1)S(1)}, bf16[8,224,128]{2,1,0:T(8,128)(2,1)S(1)}, u32[]{:S(2)}, u32[]{:S(2)}) collective-permute-start(bf16[8,224,128]{2,1,0:T(8,128)(2,1)S(1)} %all-to-all-done.1.refs_0_), channel_id=1, source_target_pairs={{0,18},{2,16},{16,2},{18,0},{4,22},{6,20},{20,6},{22,4},{8,26},{10... | collective-permute-start | bytes 1376264 | tf_op jit(solution)/shard_map/ppermute | solution.py:185
  80.0 0.6 collective-permute-start.20
  80.6 2.0 %collective-permute-start.21 = (bf16[8,224,128]{2,1,0:T(8,128)(2,1)S(1)}, bf16[8,224,128]{2,1,0:T(8,128)(2,1)S(1)}, u32[]{:S(2)}, u32[]{:S(2)}) collective-permute-start(bf16[8,224,128]{2,1,0:T(8,128)(2,1)S(1)} %all-to-all-done.1.refs_0_), channel_id=1, source_target_pairs={{0,16},{2,18},{16,0},{18,2},{4,20},{6,22},{20,4},{22,6},{8,24},{10... | collective-permute-start | bytes 1376264 | tf_op jit(solution)/shard_map/ppermute | solution.py:185
  82.6 0.1 collective-permute-start.22
  82.7 2.8 %copy-done.1 = bf16[224,14336]{1,0:T(8,128)(2,1)S(1)} copy-done((bf16[224,14336]{1,0:T(8,128)(2,1)S(1)}, bf16[224,14336]{1,0:T(8,128)(2,1)}, u32[]{:S(2)}) %copy-start.1) | copy-done | bytes 6422552
  85.5 0.6 shard_map.78.basis_ref
  86.1 0.7 fusion.6
  86.8 1.6 %select_dynamic-update-slice_fusion = (f32[224,1024]{1,0:T(8,128)S(1)}, f32[224,1024]{1,0:T(8,128)}) fusion(f32[224,1024]{1,0:T(8,128)S(1)} %fusion.5, s32[]{:T(128)} %bitcast.5, f32[224,128]{1,0:T(8,128)S(1)} %get-tuple-element.66, pred[]{:T(512)} %bitcast.2, f32[224,1024]{1,0:T(8,128)} %fusion.6, f32[224,128]{1,0:T(8,128)S(1)} %copy-done.7), kind=kLoop, calls=%fused_computation.19 | loop fusion | flops 57344 | bytes 689152 | tf_op jit(solution)/shard_map/dynamic_update_slice | solution.py:255
  88.4 0.0 collective-permute-done.19.refs_3_
  88.4 0.4 collective-permute-start.25
  88.8 2.5 %collective-permute-done.20.refs_1_ = bf16[8,224,128]{2,1,0:T(8,128)(2,1)S(1)} collective-permute-done((bf16[8,224,128]{2,1,0:T(8,128)(2,1)S(1)}, bf16[8,224,128]{2,1,0:T(8,128)(2,1)S(1)}, u32[]{:S(2)}, u32[]{:S(2)}) %collective-permute-start.20) | collective-permute-done | bytes 458784 | tf_op jit(solution)/shard_map/ppermute | solution.py:185
  91.4 1.3 %collective-permute-start.23 = (bf16[8,224,128]{2,1,0:T(8,128)(2,1)S(1)}, bf16[8,224,128]{2,1,0:T(8,128)(2,1)S(1)}, u32[]{:S(2)}, u32[]{:S(2)}) collective-permute-start(bf16[8,224,128]{2,1,0:T(8,128)(2,1)S(1)} %collective-permute-done.20.refs_1_), channel_id=1, source_target_pairs={{0,1},{1,0},{2,3},{3,2},{4,5},{5,4},{6,7},{7,6},{8,9},{9,8},{10,11... | collective-permute-start | bytes 1376264 | tf_op jit(solution)/shard_map/ppermute | solution.py:189
  92.6 0.8 collective-permute-start.24
  93.5 0.6 collective-permute-done.23.refs_5_
  94.1 0.9 collective-permute-done.24.refs_6_
  94.9 3.0 %shard_map.79 = f32[224,128]{1,0:T(8,128)S(1)} custom-call(bf16[224,14336]{1,0:T(8,128)(2,1)S(1)} %shard_map.78.basis_ref, bf16[8,224,128]{2,1,0:T(8,128)(2,1)S(1)} %all-to-all-done.1.refs_0_, bf16[8,224,128]{2,1,0:T(8,128)(2,1)S(1)} %collective-permute-done.20.refs_1_, bf16[8,224,128]{2,1,0:T(8,128)(2,1)S(1)} %collective-permute-done.21.refs_2_, ...), custom_call_target="tpu_custom_call" | custom-call | tf_op jit(solution)/shard_map/pallas_call | solution.py:145
  98.0 3.2 %conditional.5 = (f16[224,128]{1,0:T(8,128)(2,1)}) conditional(s32[]{:T(128)} %bitcast.3, f16[224,128]{1,0:T(8,128)(2,1)S(1)} %convert_element_type.71, f16[224,128]{1,0:T(8,128)(2,1)S(1)} %convert_element_type.71, f16[224,128]{1,0:T(8,128)(2,1)S(1)} %convert_element_type.71), branch_computations={%region_7.8_spmd, %region_8.9_spmd, %region_9.10_spmd} | conditional | bytes 229424 | solution.py:201
  98.0 1.0 collective-permute-start.6
  99.0 2.2 %collective-permute-done.6 = f16[224,128]{1,0:T(8,128)(2,1)} collective-permute-done((f16[224,128]{1,0:T(8,128)(2,1)S(1)}, f16[224,128]{1,0:T(8,128)(2,1)}, u32[]{:S(2)}, u32[]{:S(2)}) %collective-permute-start.6) | collective-permute-done | bytes 57376 | tf_op jit(solution)/shard_map/cond/branch_0_fun/ppermute | solution.py:193
  101.2 1.5 %select_bitcast_fusion = f32[256,224]{0,1:T(8,128)} fusion(f32[224,128]{1,0:T(8,128)S(1)} %shard_map.79, f16[224,128]{1,0:T(8,128)(2,1)} %get-tuple-element.86, pred[]{:T(512)} %bitcast.4, pred[]{:T(512)} %bitcast.2, pred[256]{0:T(512)(128)(4,1)S(1)} %iota_compare_fusion), kind=kLoop, calls=%fused_computation.6 | loop fusion | flops 229376 | bytes 401666 | tf_op jit(solution)/shard_map/transpose | solution.py:273
  (24 shorter events, 0.1 us)
Async XLA Ops:
  0.6 9.5 %copy-start.3 = (s32[4,2]{0,1:T(2,128)S(1)}, s32[4,2]{0,1:T(2,128)}, u32[]{:S(2)}) copy-start(s32[4,2]{0,1:T(2,128)} %param.18) | copy-start | bytes 100
  0.6 9.5 %copy-start.2 = (bf16[256,224]{0,1:T(8,128)(2,1)S(1)}, bf16[256,224]{0,1:T(8,128)(2,1)}, u32[]{:S(2)}) copy-start(bf16[256,224]{0,1:T(8,128)(2,1)} %param.14) | copy-start | bytes 344068
  1.5 8.0 %collective-permute-start.10 = (bf16[224,128]{1,0:T(8,128)(2,1)S(1)}, bf16[224,128]{1,0:T(8,128)(2,1)S(1)}, u32[]{:S(2)}, u32[]{:S(2)}) collective-permute-start(bf16[224,128]{1,0:T(8,128)(2,1)S(1)} %slice.54), channel_id=1, source_target_pairs={{0,128},{64,192},{128,0},{192,64},{1,129},{65,193},{129,1},{193,65... | collective-permute-start | bytes 172040 | tf_op jit(solution)/shard_map/ppermute | solution.py:193
  5.3 4.9 %collective-permute-start.11 = (bf16[224,128]{1,0:T(8,128)(2,1)S(1)}, bf16[224,128]{1,0:T(8,128)(2,1)S(1)}, u32[]{:S(2)}, u32[]{:S(2)}) collective-permute-start(bf16[224,128]{1,0:T(8,128)(2,1)S(1)} %slice.54), channel_id=1, source_target_pairs={{0,192},{64,128},{128,64},{192,0},{1,193},{65,129},{129,65},{193,1... | collective-permute-start | bytes 172040 | tf_op jit(solution)/shard_map/ppermute | solution.py:193
  6.1 4.1 %collective-permute-start.9 = (bf16[224,128]{1,0:T(8,128)(2,1)S(1)}, bf16[224,128]{1,0:T(8,128)(2,1)S(1)}, u32[]{:S(2)}, u32[]{:S(2)}) collective-permute-start(bf16[224,128]{1,0:T(8,128)(2,1)S(1)} %slice.54), channel_id=1, source_target_pairs={{0,64},{64,0},{128,192},{192,128},{1,65},{65,1},{129,193},{193,129... | collective-permute-start | bytes 172040 | tf_op jit(solution)/shard_map/ppermute | solution.py:193
  6.1 2.8 %copy-start = (bf16[224,14336]{1,0:T(8,128)(2,1)S(1)}, bf16[224,14336]{1,0:T(8,128)(2,1)}, u32[]{:S(2)}) copy-start(bf16[224,14336]{1,0:T(8,128)(2,1)} %basis_ref.2) | copy-start | bytes 19267588
  9.5 17.8 %copy-start.5 = (f32[1024,224]{0,1:T(8,128)S(1)}, f32[1024,224]{0,1:T(8,128)}, u32[]{:S(2)}) copy-start(f32[1024,224]{0,1:T(8,128)} %param.16) | copy-start | bytes 2752516
  9.5 17.8 %copy-start.4 = (f32[1024,224]{0,1:T(8,128)S(1)}, f32[1024,224]{0,1:T(8,128)}, u32[]{:S(2)}) copy-start(f32[1024,224]{0,1:T(8,128)} %param.15) | copy-start | bytes 2752516
  13.9 3.2 %collective-permute-start.13 = (bf16[8,224,128]{2,1,0:T(8,128)(2,1)S(1)}, bf16[8,224,128]{2,1,0:T(8,128)(2,1)S(1)}, u32[]{:S(2)}, u32[]{:S(2)}) collective-permute-start(bf16[8,224,128]{2,1,0:T(8,128)(2,1)S(1)} %get-tuple-element.55), channel_id=1, source_target_pairs={{0,1},{1,0},{2,3},{3,2},{4,5},{5,4},{6,7},{7,6},{8,9},{9,8},{10,11... | collective-permute-start | bytes 1376264 | tf_op jit(solution)/shard_map/ppermute | solution.py:189
  15.6 9.3 %collective-permute-start.15 = (bf16[8,224,128]{2,1,0:T(8,128)(2,1)S(1)}, bf16[8,224,128]{2,1,0:T(8,128)(2,1)S(1)}, u32[]{:S(2)}, u32[]{:S(2)}) collective-permute-start(bf16[8,224,128]{2,1,0:T(8,128)(2,1)S(1)} %get-tuple-element.57), channel_id=1, source_target_pairs={{0,1},{1,0},{2,3},{3,2},{4,5},{5,4},{6,7},{7,6},{8,9},{9,8},{10,11... | collective-permute-start | bytes 1376264 | tf_op jit(solution)/shard_map/ppermute | solution.py:189
  15.7 9.4 %collective-permute-start.17 = (bf16[8,224,128]{2,1,0:T(8,128)(2,1)S(1)}, bf16[8,224,128]{2,1,0:T(8,128)(2,1)S(1)}, u32[]{:S(2)}, u32[]{:S(2)}) collective-permute-start(bf16[8,224,128]{2,1,0:T(8,128)(2,1)S(1)} %get-tuple-element.59), channel_id=1, source_target_pairs={{0,1},{1,0},{2,3},{3,2},{4,5},{5,4},{6,7},{7,6},{8,9},{9,8},{10,11... | collective-permute-start | bytes 1376264 | tf_op jit(solution)/shard_map/ppermute | solution.py:189
  16.1 11.3 %collective-permute-start.12 = (bf16[8,224,128]{2,1,0:T(8,128)(2,1)S(1)}, bf16[8,224,128]{2,1,0:T(8,128)(2,1)S(1)}, u32[]{:S(2)}, u32[]{:S(2)}) collective-permute-start(bf16[8,224,128]{2,1,0:T(8,128)(2,1)S(1)} %get-tuple-element.53), channel_id=1, source_target_pairs={{0,1},{1,0},{2,3},{3,2},{4,5},{5,4},{6,7},{7,6},{8,9},{9,8},{10,11... | collective-permute-start | bytes 1376264 | tf_op jit(solution)/shard_map/ppermute | solution.py:189
  17.1 13.7 %collective-permute-start.14 = (f16[8,224,128]{2,1,0:T(8,128)(2,1)S(1)}, f16[8,224,128]{2,1,0:T(8,128)(2,1)S(1)}, u32[]{:S(2)}, u32[]{:S(2)}) collective-permute-start(f16[8,224,128]{2,1,0:T(8,128)(2,1)S(1)} %add_convert_fusion.2), channel_id=1, source_target_pairs={{0,18},{2,16},{16,2},{18,0},{4,22},{6,20},{20,6},{22,4},{8,26},{10... | collective-permute-start | bytes 1376264 | tf_op jit(solution)/shard_map/ppermute | solution.py:185
  25.0 10.3 %collective-permute-start.16 = (f16[8,224,128]{2,1,0:T(8,128)(2,1)S(1)}, f16[8,224,128]{2,1,0:T(8,128)(2,1)S(1)}, u32[]{:S(2)}, u32[]{:S(2)}) collective-permute-start(f16[8,224,128]{2,1,0:T(8,128)(2,1)S(1)} %add_convert_fusion.1), channel_id=1, source_target_pairs={{0,2},{2,0},{16,18},{18,16},{4,6},{6,4},{20,22},{22,20},{8,10},{10... | collective-permute-start | bytes 1376264 | tf_op jit(solution)/shard_map/ppermute | solution.py:185
  25.2 10.4 %collective-permute-start.18 = (f16[8,224,128]{2,1,0:T(8,128)(2,1)S(1)}, f16[8,224,128]{2,1,0:T(8,128)(2,1)S(1)}, u32[]{:S(2)}, u32[]{:S(2)}) collective-permute-start(f16[8,224,128]{2,1,0:T(8,128)(2,1)S(1)} %add_convert_fusion), channel_id=1, source_target_pairs={{0,16},{2,18},{16,0},{18,2},{4,20},{6,22},{20,4},{22,6},{8,24},{10... | collective-permute-start | bytes 1376264 | tf_op jit(solution)/shard_map/ppermute | solution.py:185
  36.8 20.1 %all-to-all-start = ((f16[8,224,128]{2,1,0:T(8,128)(2,1)}), f16[8,224,128]{2,1,0:T(8,128)(2,1)S(1)}, u32[]{:S(2)}, u32[]{:S(2)}) async-start(f16[8,224,128]{2,1,0:T(8,128)(2,1)} %multiply_convert_fusion), calls=%async_computation | async-start | bytes 917504 | tf_op jit(solution)/shard_map/all_to_all | solution.py:180
  44.0 5.8 %collective-permute-start = (f32[224,256]{1,0:T(8,128)S(1)}, f32[224,256]{1,0:T(8,128)}, u32[]{:S(2)}, u32[]{:S(2)}) collective-permute-start(f32[224,256]{1,0:T(8,128)S(1)} %param), channel_id=1, source_target_pairs={{0,64},{64,0},{128,192},{192,128},{1,65},{65,1},{129,193},{193,129... | collective-permute-start | bytes 688136 | tf_op jit(solution)/shard_map/cond/branch_0_fun/ppermute | solution.py:193
  58.8 18.1 %all-to-all-start.1 = ((bf16[8,224,128]{2,1,0:T(8,128)(2,1)}), bf16[8,224,128]{2,1,0:T(8,128)(2,1)S(1)}, u32[]{:S(2)}, u32[]{:S(2)}) async-start(bf16[8,224,128]{2,1,0:T(8,128)(2,1)} %broadcast_in_dim.12), calls=%async_computation.1 | async-start | bytes 917504 | tf_op jit(solution)/shard_map/all_to_all | solution.py:180
  64.4 3.8 %collective-permute-start.3 = (f32[224,128]{1,0:T(8,128)S(1)}, f32[224,128]{1,0:T(8,128)}, u32[]{:S(2)}, u32[]{:S(2)}) collective-permute-start(f32[224,128]{1,0:T(8,128)S(1)} %param.3), channel_id=1, source_target_pairs={{0,64},{64,0},{128,192},{192,128},{1,65},{65,1},{129,193},{193,129... | collective-permute-start | bytes 344072 | tf_op jit(solution)/shard_map/cond/branch_0_fun/ppermute | solution.py:193
  76.9 11.5 %collective-permute-start.19 = (bf16[8,224,128]{2,1,0:T(8,128)(2,1)S(1)}, bf16[8,224,128]{2,1,0:T(8,128)(2,1)S(1)}, u32[]{:S(2)}, u32[]{:S(2)}) collective-permute-start(bf16[8,224,128]{2,1,0:T(8,128)(2,1)S(1)} %all-to-all-done.1.refs_0_), channel_id=1, source_target_pairs={{0,18},{2,16},{16,2},{18,0},{4,22},{6,20},{20,6},{22,4},{8,26},{10... | collective-permute-start | bytes 1376264 | tf_op jit(solution)/shard_map/ppermute | solution.py:185
  80.0 11.3 %collective-permute-start.20 = (bf16[8,224,128]{2,1,0:T(8,128)(2,1)S(1)}, bf16[8,224,128]{2,1,0:T(8,128)(2,1)S(1)}, u32[]{:S(2)}, u32[]{:S(2)}) collective-permute-start(bf16[8,224,128]{2,1,0:T(8,128)(2,1)S(1)} %all-to-all-done.1.refs_0_), channel_id=1, source_target_pairs={{0,2},{2,0},{16,18},{18,16},{4,6},{6,4},{20,22},{22,20},{8,10},{10... | collective-permute-start | bytes 1376264 | tf_op jit(solution)/shard_map/ppermute | solution.py:185
  80.6 12.1 %collective-permute-start.21 = (bf16[8,224,128]{2,1,0:T(8,128)(2,1)S(1)}, bf16[8,224,128]{2,1,0:T(8,128)(2,1)S(1)}, u32[]{:S(2)}, u32[]{:S(2)}) collective-permute-start(bf16[8,224,128]{2,1,0:T(8,128)(2,1)S(1)} %all-to-all-done.1.refs_0_), channel_id=1, source_target_pairs={{0,16},{2,18},{16,0},{18,2},{4,20},{6,22},{20,4},{22,6},{8,24},{10... | collective-permute-start | bytes 1376264 | tf_op jit(solution)/shard_map/ppermute | solution.py:185
  82.6 10.9 %collective-permute-start.22 = (bf16[8,224,128]{2,1,0:T(8,128)(2,1)S(1)}, bf16[8,224,128]{2,1,0:T(8,128)(2,1)S(1)}, u32[]{:S(2)}, u32[]{:S(2)}) collective-permute-start(bf16[8,224,128]{2,1,0:T(8,128)(2,1)S(1)} %all-to-all-done.1.refs_0_), channel_id=1, source_target_pairs={{0,1},{1,0},{2,3},{3,2},{4,5},{5,4},{6,7},{7,6},{8,9},{9,8},{10,11... | collective-permute-start | bytes 1376264 | tf_op jit(solution)/shard_map/ppermute | solution.py:189
  82.7 2.8 %copy-start.1 = (bf16[224,14336]{1,0:T(8,128)(2,1)S(1)}, bf16[224,14336]{1,0:T(8,128)(2,1)}, u32[]{:S(2)}) copy-start(bf16[224,14336]{1,0:T(8,128)(2,1)} %basis_ref.2) | copy-start | bytes 19267588
  85.5 1.3 %copy-start.7 = (f32[224,128]{1,0:T(8,128)S(1)}, f32[224,128]{1,0:T(8,128)}, u32[]{:S(2)}) copy-start(f32[224,128]{1,0:T(8,128)} %get-tuple-element.64) | copy-start | bytes 344068
  88.4 14.3 %copy-start.6 = (f32[224,1024]{1,0:T(8,128)}, f32[224,1024]{1,0:T(8,128)S(1)}, u32[]{:S(2)}) copy-start(f32[224,1024]{1,0:T(8,128)S(1)} %get-tuple-element.71) | copy-start | bytes 2752516
  88.4 5.1 %collective-permute-start.25 = (bf16[8,224,128]{2,1,0:T(8,128)(2,1)S(1)}, bf16[8,224,128]{2,1,0:T(8,128)(2,1)S(1)}, u32[]{:S(2)}, u32[]{:S(2)}) collective-permute-start(bf16[8,224,128]{2,1,0:T(8,128)(2,1)S(1)} %collective-permute-done.19.refs_3_), channel_id=1, source_target_pairs={{0,1},{1,0},{2,3},{3,2},{4,5},{5,4},{6,7},{7,6},{8,9},{9,8},{10,11... | collective-permute-start | bytes 1376264 | tf_op jit(solution)/shard_map/ppermute | solution.py:189
  91.4 2.7 %collective-permute-start.23 = (bf16[8,224,128]{2,1,0:T(8,128)(2,1)S(1)}, bf16[8,224,128]{2,1,0:T(8,128)(2,1)S(1)}, u32[]{:S(2)}, u32[]{:S(2)}) collective-permute-start(bf16[8,224,128]{2,1,0:T(8,128)(2,1)S(1)} %collective-permute-done.20.refs_1_), channel_id=1, source_target_pairs={{0,1},{1,0},{2,3},{3,2},{4,5},{5,4},{6,7},{7,6},{8,9},{9,8},{10,11... | collective-permute-start | bytes 1376264 | tf_op jit(solution)/shard_map/ppermute | solution.py:189
  92.6 2.3 %collective-permute-start.24 = (bf16[8,224,128]{2,1,0:T(8,128)(2,1)S(1)}, bf16[8,224,128]{2,1,0:T(8,128)(2,1)S(1)}, u32[]{:S(2)}, u32[]{:S(2)}) collective-permute-start(bf16[8,224,128]{2,1,0:T(8,128)(2,1)S(1)} %collective-permute-done.21.refs_2_), channel_id=1, source_target_pairs={{0,1},{1,0},{2,3},{3,2},{4,5},{5,4},{6,7},{7,6},{8,9},{9,8},{10,11... | collective-permute-start | bytes 1376264 | tf_op jit(solution)/shard_map/ppermute | solution.py:189
  98.0 3.2 %collective-permute-start.6 = (f16[224,128]{1,0:T(8,128)(2,1)S(1)}, f16[224,128]{1,0:T(8,128)(2,1)}, u32[]{:S(2)}, u32[]{:S(2)}) collective-permute-start(f16[224,128]{1,0:T(8,128)(2,1)S(1)} %param.6), channel_id=1, source_target_pairs={{0,64},{64,0},{128,192},{192,128},{1,65},{65,1},{129,193},{193,129... | collective-permute-start | bytes 172040 | tf_op jit(solution)/shard_map/cond/branch_0_fun/ppermute | solution.py:193
